TPU v7x, 128 devices: a whole 4x4x4 slice. The times are simulated.
128 devices in a mesh: dp: 2 (over z_lo), ctx: 16 (over z_hi, y, core), tensor: 4 (over x).
Axes of the slice: x: 4, y: 4, z: 4 (z_hi: 2, z_lo: 2; z = z_hi * 2 + z_lo), core: 2. Of those that a mesh axis runs over, the one named last changes fastest.
Arguments:
- normed_input: bfloat16 [2, 8192, 9216], P('dp', ('ctx', 'tensor')), may hold values from -16 to 16
- queries: bfloat16 [2, 8192, 3072], P('dp', 'ctx', 'tensor'), may hold values from -10 to 10
- key_heads: bfloat16 [2, 8192, 512], P('dp', 'ctx', 'tensor'), may hold values from -10 to 10
- value_heads: bfloat16 [2, 8192, 512], P('dp', 'ctx', 'tensor'), may hold values from -6 to 6
- attn_out: bfloat16 [2, 8192, 3072], P('dp', 'ctx', 'tensor'), may hold values from -6 to 6
- out_grad: bfloat16 [2, 8192, 3072], P('dp', 'ctx', 'tensor'), may hold values from -6 to 6
- key_weight: bfloat16 [9216, 512], P(None, 'tensor'), may hold values from -0.5 to 0.5
- value_weight: bfloat16 [9216, 512], P(None, 'tensor'), may hold values from -0.5 to 0.5
- block_order: int32 [32], replicated, may hold values from 0 to 31, each once
Outputs:
- query_grad: bfloat16 [2, 8192, 3072], P('dp', 'ctx', 'tensor')
- input_grad: bfloat16 [2, 8192, 9216], P('dp', ('ctx', 'tensor'))
- keyproj_grad: bfloat16 [9216, 512], P(('dp', 'ctx'), 'tensor')
- valueproj_grad: bfloat16 [9216, 512], P(('dp', 'ctx'), 'tensor')
Inputs may be any that keep to these rules, and one draw needn't show every extreme that they name: Each block number appears once; stored block c of every sequence holds the places block_order[c] * 256 to block_order[c] * 256 + 255 in order.
All inputs are finite; a program needn't handle non-finite values.
Results may differ from a plain program's by a relative error of at most 0.014.
Values may be sent and summed in bfloat16 or wider, within the bound.
No kernel may reach another device: no remote copies, remote signals or barrier semaphores. Data moves between devices by JAX's collectives and lax.ppermute only.
A program may use at most 128 MiB of HBM per device.

v0:
```python
import jax
import jax.numpy as jnp
from jax import lax
from jax.sharding import PartitionSpec as P

HD = 128
HQ = 6
KV_DEV = 1


NEG_BIG = -1e30


def passed_along(shard, axis, by):
    peers = lax.axis_size(axis)
    return lax.ppermute(shard, axis, [(i, (i + by) % peers) for i in range(peers)])


def per_device(
    normed_input,
    queries,
    key_heads,
    value_heads,
    attn_out,
    out_grad,
    key_weight,
    value_weight,
    block_order,
):
    ctx_count = lax.axis_size("ctx")
    ctx_here = lax.axis_index("ctx")
    local_rows = queries.shape[1]
    block_rows = local_rows // 2
    head_cols = KV_DEV * HD
    score_scale = HD ** (-0.5)

    def row_places(first_block):
        picked = lax.dynamic_slice_in_dim(block_order, first_block, 2)
        offsets = jnp.arange(block_rows, dtype=jnp.int32)
        return (picked[:, None] * block_rows + offsets[None, :]).reshape(-1)

    query_places = row_places(2 * ctx_here)
    query_last = jnp.max(query_places)
    query_block = queries[0].reshape(local_rows, KV_DEV, HQ, HD)
    grad_block = out_grad[0].reshape(local_rows, KV_DEV, HQ, HD)
    out_dot = jnp.sum(
        grad_block.astype(jnp.float32)
        * attn_out[0].reshape(local_rows, KV_DEV, HQ, HD).astype(jnp.float32),
        axis=-1,
    )
    out_dot = jnp.transpose(out_dot, (1, 2, 0))

    def tile_scores(key_tile, key_places):
        key_view = key_tile.reshape(local_rows, KV_DEV, HD)
        raw_scores = (
            jnp.einsum("rghd,ngd->ghrn", query_block, key_view, preferred_element_type=jnp.float32)
            * score_scale
        )
        allowed = key_places[None, :] <= query_places[:, None]
        return (raw_scores, allowed)

    def stats_tile(running, key_tile, first_block):
        key_places = row_places(first_block)

        def stats_compute(current):
            top_run, total_run = current
            raw_scores, allowed = tile_scores(key_tile, key_places)
            tile_top = jnp.max(jnp.where(allowed, raw_scores, NEG_BIG), axis=-1)
            new_top = jnp.maximum(top_run, tile_top)
            shifted = jnp.where(allowed, jnp.exp(raw_scores - new_top[..., None]), 0.0)
            return (new_top, total_run * jnp.exp(top_run - new_top) + jnp.sum(shifted, axis=-1))

        return lax.cond(
            jnp.min(key_places) <= query_last, stats_compute, lambda unchanged: unchanged, running
        )

    def backward_tile(query_sum, key_tile, value_tile, first_block, log_total):
        key_places = row_places(first_block)

        def backward_compute(sum_in):
            raw_scores, allowed = tile_scores(key_tile, key_places)
            key_view = key_tile.reshape(local_rows, KV_DEV, HD)
            value_view = value_tile.reshape(local_rows, KV_DEV, HD)
            attn_probs = jnp.where(allowed, jnp.exp(raw_scores - log_total[..., None]), 0.0)
            grad_probs = jnp.einsum(
                "rghd,ngd->ghrn", grad_block, value_view, preferred_element_type=jnp.float32
            )
            grad_scores = (attn_probs * (grad_probs - out_dot[..., None])).astype(jnp.bfloat16)
            probs_half = attn_probs.astype(jnp.bfloat16)
            sum_out = (
                sum_in
                + jnp.einsum(
                    "ghrn,ngd->rghd", grad_scores, key_view, preferred_element_type=jnp.float32
                )
                * score_scale
            )
            key_part = (
                jnp.einsum(
                    "ghrn,rghd->ngd", grad_scores, query_block, preferred_element_type=jnp.float32
                )
                * score_scale
            )
            value_part = jnp.einsum(
                "ghrn,rghd->ngd", probs_half, grad_block, preferred_element_type=jnp.float32
            )
            return (
                sum_out,
                jnp.stack(
                    [
                        key_part.reshape(local_rows, head_cols),
                        value_part.reshape(local_rows, head_cols),
                    ]
                ),
            )

        def skipped(sum_in):
            return (sum_in, jnp.zeros((2, local_rows, head_cols), jnp.float32))

        return lax.cond(jnp.min(key_places) <= query_last, backward_compute, skipped, query_sum)

    top_init = jnp.full((KV_DEV, HQ, local_rows), NEG_BIG, jnp.float32)
    total_init = jnp.zeros((KV_DEV, HQ, local_rows), jnp.float32)
    query_init = jnp.zeros((local_rows, KV_DEV, HQ, HD), jnp.float32)
    pair_home = jnp.stack([key_heads[0], value_heads[0]])
    tile_stack = lax.all_gather(key_heads[0], "ctx", axis=0, tiled=True).reshape(
        -1, local_rows, head_cols
    )

    def over_tiles(current, tile_pack):
        tile_rows, tile_index = tile_pack
        return (stats_tile(current, tile_rows, tile_index * local_rows // block_rows), None)

    result, unused = lax.scan(
        over_tiles,
        (top_init, total_init),
        (tile_stack, jnp.arange(tile_stack.shape[0], dtype=jnp.int32)),
    )
    top_all, total_all = result
    log_total = top_all + jnp.log(total_all)

    def pass_turn(turn_index, current):
        query_sum, pair_tile, pair_grads = current
        anchor = (ctx_here - turn_index) % ctx_count
        query_sum, grads_add = backward_tile(
            query_sum, pair_tile[0], pair_tile[1], 2 * anchor, log_total
        )
        pair_tile = passed_along(pair_tile, "ctx", 1)
        pair_grads = passed_along(pair_grads + grads_add, "ctx", 1)
        return (query_sum, pair_tile, pair_grads)

    grads_init = jnp.zeros((2, local_rows, head_cols), jnp.float32)
    query_sum, pair_tile, pair_grads = lax.fori_loop(
        0, ctx_count - 1, pass_turn, (query_init, pair_home, grads_init)
    )
    anchor = (ctx_here - (ctx_count - 1)) % ctx_count
    query_sum, grads_add = backward_tile(
        query_sum, pair_tile[0], pair_tile[1], 2 * anchor, log_total
    )
    pair_grads = passed_along(pair_grads + grads_add, "ctx", 1)
    grads_half = jnp.concatenate([pair_grads[0], pair_grads[1]], axis=1).astype(jnp.bfloat16)
    query_grad = query_sum.reshape(1, local_rows, KV_DEV * HQ * HD).astype(jnp.bfloat16)
    part_rows = grads_half
    contract = (((1,), (1,)), ((), ()))
    key_term = lax.dot_general(
        part_rows[:, :head_cols], key_weight, contract, preferred_element_type=jnp.float32
    )
    value_term = lax.dot_general(
        part_rows[:, head_cols:], value_weight, contract, preferred_element_type=jnp.float32
    )
    input_grad = lax.psum_scatter(
        (key_term + value_term).astype(jnp.bfloat16), "tensor", scatter_dimension=0, tiled=True
    )
    part_rows = grads_half
    weight_total = lax.dot_general(
        lax.all_gather(normed_input, "tensor", axis=1, tiled=True)[0],
        part_rows,
        (((0,), (0,)), ((), ())),
        preferred_element_type=jnp.float32,
    )
    shared = lax.psum_scatter(weight_total, ("dp", "ctx"), scatter_dimension=0, tiled=True).astype(
        jnp.bfloat16
    )
    return (query_grad, input_grad[None], shared[:, :head_cols], shared[:, head_cols:])


def solution(mesh):
    in_specs = (
        P("dp", ("ctx", "tensor"), None),
        P("dp", "ctx", "tensor"),
        P("dp", "ctx", "tensor"),
        P("dp", "ctx", "tensor"),
        P("dp", "ctx", "tensor"),
        P("dp", "ctx", "tensor"),
        P(None, "tensor"),
        P(None, "tensor"),
        P(),
    )
    out_specs = (
        P("dp", "ctx", "tensor"),
        P("dp", ("ctx", "tensor"), None),
        P(("dp", "ctx"), "tensor"),
        P(("dp", "ctx"), "tensor"),
    )
    return jax.shard_map(
        per_device, mesh=mesh, in_specs=in_specs, out_specs=out_specs, check_vma=False
    )
```

profile of v0, /device:TPU:5, one launch (start us, length us, event | category | flops | bytes accessed | tf_op | source)
XLA Modules:
  0.0 851.1 jit_solution(12904006077860579154)
XLA Ops:
  16.0 2.3 copy.36
  18.3 2.3 copy.39
  20.6 2.3 copy.37
  25.3 36.5 %all-gather.6.cloned.1.call-done = bf16[1,8192,128]{2,1,0:T(8,128)(2,1)} async-done(((bf16[1,512,128]{2,1,0:T(8,128)(2,1)}), bf16[1,8192,128]{2,1,0:T(8,128)(2,1)}) %all-gather.6.cloned.1.call-update) | async-done | bytes 2097168 | tf_op jit(solution)/shard_map/all_gather | solution.py:125
  61.8 107.0 %while.41 = (s32[]{:T(128)}, f32[1,6,512]{2,1,0:T(8,128)S(1)}, f32[1,6,512]{2,1,0:T(8,128)S(1)}, s32[16]{0:T(128)S(1)}, s32[32]{0:T(128)S(1)}, /*index=5*/s32[]{...) while((s32[]{:T(128)}, f32[1,6,512]{2,1,0:T(8,128)S(1)}, ...), condition=%wide.region_8.9_spmd.clone, body=%wide.region_2.8_spmd.clone.sunk | while | flops 413933088 | bytes 14468107 | solution.py:133
  65.1 3.8 conditional.8
  72.3 3.8 conditional.8
  79.5 3.8 conditional.8
  90.0 3.8 conditional.8
  97.2 3.8 conditional.8
  104.3 3.8 conditional.8
  114.9 3.8 conditional.8
  122.0 3.8 conditional.8
  129.2 3.8 conditional.8
  136.4 3.8 conditional.8
  143.5 3.8 conditional.8
  150.7 3.8 conditional.8
  157.8 3.8 conditional.8
  165.0 3.8 conditional.8
  170.8 385.6 %while.42 = (s32[]{:T(128)}, f32[512,1,6,128]{3,0,2,1:T(8,128)}, bf16[2,512,128]{2,1,0:T(8,128)(2,1)}, f32[2,512,128]{2,1,0:T(8,128)}, s32[]{:T(128)}, /*index=5...) while((s32[]{:T(128)}, f32[512,1,6,128]{3,0,2,1:T(8,128)}, ...), condition=%wide.region_14.15_spmd.clone, body=%wide.region_10.14_spmd.clone.sunk | while | flops 2030372352 | bytes 58393212 | solution.py:152
  173.9 7.1 conditional.9
  184.0 7.7 collective-permute-start
  191.7 3.3 collective-permute-done
  198.1 7.1 conditional.9
  207.1 2.6 collective-permute-start.1
  209.7 3.3 collective-permute-start
  212.9 5.9 collective-permute-done
  221.9 7.1 conditional.9
  230.9 2.6 collective-permute-start.1
  234.2 8.5 collective-permute-done
  245.7 7.1 conditional.9
  254.7 2.6 collective-permute-start.1
  257.9 9.0 %collective-permute-done = bf16[2,512,128]{2,1,0:T(8,128)(2,1)} collective-permute-done((bf16[2,512,128]{2,1,0:T(8,128)(2,1)S(1)}, bf16[2,512,128]{2,1,0:T(8,128)(2,1)}, u32[]{:S(2)}, u32[]{:S(2)}) %collective-permute-start) | collective-permute-done | bytes 262176 | tf_op jit(solution)/shard_map/while/body/eval_jaxpr/ppermute | solution.py:16
  270.5 7.1 conditional.9
  281.7 12.6 %collective-permute-done = bf16[2,512,128]{2,1,0:T(8,128)(2,1)} collective-permute-done((bf16[2,512,128]{2,1,0:T(8,128)(2,1)S(1)}, bf16[2,512,128]{2,1,0:T(8,128)(2,1)}, u32[]{:S(2)}, u32[]{:S(2)}) %collective-permute-start) | collective-permute-done | bytes 262176 | tf_op jit(solution)/shard_map/while/body/eval_jaxpr/ppermute | solution.py:16
  297.9 7.1 conditional.9
  306.9 14.8 %collective-permute-done = bf16[2,512,128]{2,1,0:T(8,128)(2,1)} collective-permute-done((bf16[2,512,128]{2,1,0:T(8,128)(2,1)S(1)}, bf16[2,512,128]{2,1,0:T(8,128)(2,1)}, u32[]{:S(2)}, u32[]{:S(2)}) %collective-permute-start) | collective-permute-done | bytes 262176 | tf_op jit(solution)/shard_map/while/body/eval_jaxpr/ppermute | solution.py:16
  325.3 7.1 conditional.9
  334.3 14.8 %collective-permute-done = bf16[2,512,128]{2,1,0:T(8,128)(2,1)} collective-permute-done((bf16[2,512,128]{2,1,0:T(8,128)(2,1)S(1)}, bf16[2,512,128]{2,1,0:T(8,128)(2,1)}, u32[]{:S(2)}, u32[]{:S(2)}) %collective-permute-start) | collective-permute-done | bytes 262176 | tf_op jit(solution)/shard_map/while/body/eval_jaxpr/ppermute | solution.py:16
  352.7 7.1 conditional.9
  361.7 14.8 %collective-permute-done = bf16[2,512,128]{2,1,0:T(8,128)(2,1)} collective-permute-done((bf16[2,512,128]{2,1,0:T(8,128)(2,1)S(1)}, bf16[2,512,128]{2,1,0:T(8,128)(2,1)}, u32[]{:S(2)}, u32[]{:S(2)}) %collective-permute-start) | collective-permute-done | bytes 262176 | tf_op jit(solution)/shard_map/while/body/eval_jaxpr/ppermute | solution.py:16
  380.1 7.1 conditional.9
  389.1 14.8 %collective-permute-done = bf16[2,512,128]{2,1,0:T(8,128)(2,1)} collective-permute-done((bf16[2,512,128]{2,1,0:T(8,128)(2,1)S(1)}, bf16[2,512,128]{2,1,0:T(8,128)(2,1)}, u32[]{:S(2)}, u32[]{:S(2)}) %collective-permute-start) | collective-permute-done | bytes 262176 | tf_op jit(solution)/shard_map/while/body/eval_jaxpr/ppermute | solution.py:16
  407.5 7.1 conditional.9
  416.5 9.1 %collective-permute-done = bf16[2,512,128]{2,1,0:T(8,128)(2,1)} collective-permute-done((bf16[2,512,128]{2,1,0:T(8,128)(2,1)S(1)}, bf16[2,512,128]{2,1,0:T(8,128)(2,1)}, u32[]{:S(2)}, u32[]{:S(2)}) %collective-permute-start) | collective-permute-done | bytes 262176 | tf_op jit(solution)/shard_map/while/body/eval_jaxpr/ppermute | solution.py:16
  430.7 9.6 %collective-permute-start.1 = (f32[2,512,128]{2,1,0:T(8,128)}, f32[2,512,128]{2,1,0:T(8,128)}, u32[]{:S(2)}, u32[]{:S(2)}) collective-permute-start(f32[2,512,128]{2,1,0:T(8,128)} %add.314), channel_id=1, source_target_pairs={{0,4},{4,8},{8,12},{12,16},{16,20},{20,24},{24,28},{28,32},{32,36}... | collective-permute-start | bytes 1572872 | tf_op jit(solution)/shard_map/while/body/eval_jaxpr/ppermute | solution.py:16
  440.4 12.2 %collective-permute-done = bf16[2,512,128]{2,1,0:T(8,128)(2,1)} collective-permute-done((bf16[2,512,128]{2,1,0:T(8,128)(2,1)S(1)}, bf16[2,512,128]{2,1,0:T(8,128)(2,1)}, u32[]{:S(2)}, u32[]{:S(2)}) %collective-permute-start) | collective-permute-done | bytes 262176 | tf_op jit(solution)/shard_map/while/body/eval_jaxpr/ppermute | solution.py:16
  456.1 7.1 conditional.9
  465.1 14.8 %collective-permute-done = bf16[2,512,128]{2,1,0:T(8,128)(2,1)} collective-permute-done((bf16[2,512,128]{2,1,0:T(8,128)(2,1)S(1)}, bf16[2,512,128]{2,1,0:T(8,128)(2,1)}, u32[]{:S(2)}, u32[]{:S(2)}) %collective-permute-start) | collective-permute-done | bytes 262176 | tf_op jit(solution)/shard_map/while/body/eval_jaxpr/ppermute | solution.py:16
  483.5 7.1 conditional.9
  492.5 14.8 %collective-permute-done = bf16[2,512,128]{2,1,0:T(8,128)(2,1)} collective-permute-done((bf16[2,512,128]{2,1,0:T(8,128)(2,1)S(1)}, bf16[2,512,128]{2,1,0:T(8,128)(2,1)}, u32[]{:S(2)}, u32[]{:S(2)}) %collective-permute-start) | collective-permute-done | bytes 262176 | tf_op jit(solution)/shard_map/while/body/eval_jaxpr/ppermute | solution.py:16
  510.9 7.1 conditional.9
  519.9 9.1 %collective-permute-done = bf16[2,512,128]{2,1,0:T(8,128)(2,1)} collective-permute-done((bf16[2,512,128]{2,1,0:T(8,128)(2,1)S(1)}, bf16[2,512,128]{2,1,0:T(8,128)(2,1)}, u32[]{:S(2)}, u32[]{:S(2)}) %collective-permute-start) | collective-permute-done | bytes 262176 | tf_op jit(solution)/shard_map/while/body/eval_jaxpr/ppermute | solution.py:16
  534.1 9.6 %collective-permute-start.1 = (f32[2,512,128]{2,1,0:T(8,128)}, f32[2,512,128]{2,1,0:T(8,128)}, u32[]{:S(2)}, u32[]{:S(2)}) collective-permute-start(f32[2,512,128]{2,1,0:T(8,128)} %add.314), channel_id=1, source_target_pairs={{0,4},{4,8},{8,12},{12,16},{16,20},{20,24},{24,28},{28,32},{32,36}... | collective-permute-start | bytes 1572872 | tf_op jit(solution)/shard_map/while/body/eval_jaxpr/ppermute | solution.py:16
  543.7 12.2 %collective-permute-done = bf16[2,512,128]{2,1,0:T(8,128)(2,1)} collective-permute-done((bf16[2,512,128]{2,1,0:T(8,128)(2,1)S(1)}, bf16[2,512,128]{2,1,0:T(8,128)(2,1)}, u32[]{:S(2)}, u32[]{:S(2)}) %collective-permute-start) | collective-permute-done | bytes 262176 | tf_op jit(solution)/shard_map/while/body/eval_jaxpr/ppermute | solution.py:16
  556.5 10.8 %conditional.3 = (f32[512,1,6,128]{3,0,2,1:T(8,128)}, f32[2,512,128]{2,1,0:T(8,128)S(1)}) conditional(s32[]{:T(128)} %convert_element_type.85, f32[512,1,6,128]{3,0,2,1:T(8,128)} %get-tuple-element.523, (s32[2,256]{1,0:T(2,128)S(1)}, s32[2,256]{1,0:T(2,128)S(1)}, bf16[2,512,128]{2,1,0:T(8,128)(2,1)}, bf16[512,1,6,128]{0,3,2,1:T(8,128)(2,1)}, ...), branch_computations={%region_15.16_spmd, %region_16.17_spmd} | conditional | flops 2030239744 | bytes 56279168 | solution.py:119
  559.0 3.2 fusion.47
  568.4 14.2 %collective-permute-done.2 = bf16[2,512,128]{2,1,0:T(8,128)(2,1)S(1)} collective-permute-done((bf16[2,512,128]{2,1,0:T(8,128)(2,1)S(1)}, bf16[2,512,128]{2,1,0:T(8,128)(2,1)S(1)}, u32[]{:S(2)}, u32[]{:S(2)}) %collective-permute-start.2) | collective-permute-done | bytes 262176 | tf_op jit(solution)/shard_map/ppermute | solution.py:16
  582.7 8.8 %convolution_bitcast_fusion.2 = f32[9216,256]{0,1:T(8,128)} fusion(bf16[1,512,9216]{2,1,0:T(8,128)(2,1)} %all-gather.4.cloned.1.call-done, bf16[512,128]{1,0:T(8,128)(2,1)S(1)} %get-tuple-element.705, bf16[512,128]{1,0:T(8,128)(2,1)S(1)} %get-tuple-element.704), kind=kOutput, calls=%fused_computation.87 | convolution fusion | flops 2416443392 | bytes 19136512 | tf_op jit(solution)/shard_map/dot_general | solution.py:174
  591.6 9.6 %copy.48 = f32[9216,256]{1,0:T(8,128)} copy(f32[9216,256]{0,1:T(8,128)} %convolution_bitcast_fusion.2) | data formatting | bytes 18874368
  601.3 7.8 fusion.79
  609.1 12.1 %add_convert_fusion = bf16[512,9216]{1,0:T(8,128)(2,1)} fusion(f32[512,9216]{1,0:T(8,128)} %fusion.79, bf16[9216,128]{1,0:T(8,128)(2,1)} %param.25, bf16[2,512,128]{2,1,0:T(8,128)(2,1)S(1)} %collective-permute-done.2), kind=kOutput, calls=%fused_computation.86 | convolution fusion | flops 1217396736 | bytes 30801920 | tf_op jit(solution)/shard_map/dot_general | solution.py:164
  624.1 123.6 %reduce-scatter.7.cloned.1.call-done = f32[288,256]{1,0:T(8,128)} async-done(((f32[9216,256]{1,0:T(8,128)}), f32[288,256]{1,0:T(8,128)}) %reduce-scatter.7.cloned.1.call-update) | async-done | bytes 294928
  750.3 94.3 %reduce-scatter.5.cloned.1.call-done = bf16[128,9216]{1,0:T(8,128)(2,1)} async-done(((bf16[512,9216]{1,0:T(8,128)(2,1)}), bf16[128,9216]{1,0:T(8,128)(2,1)}) %reduce-scatter.5.cloned.1.call-update) | async-done | bytes 2359312 | tf_op jit(solution)/shard_map/reduce_scatter | solution.py:170
  (572 shorter events, 259.2 us)
Async XLA Ops:
  7.2 594.1 %copy-start = (bf16[9216,128]{1,0:T(8,128)(2,1)S(1)}, bf16[9216,128]{1,0:T(8,128)(2,1)}, u32[]{:S(2)}) copy-start(bf16[9216,128]{1,0:T(8,128)(2,1)} %param.26) | copy-start | bytes 7077892
  7.2 15.7 %copy-start.8 = (bf16[1,512,128]{2,1,0:T(8,128)(2,1)S(1)}, bf16[1,512,128]{2,1,0:T(8,128)(2,1)}, u32[]{:S(2)}) copy-start(bf16[1,512,128]{2,1,0:T(8,128)(2,1)} %param.21) | copy-start | bytes 393220
  7.2 54.6 %copy-start.10 = (s32[32]{0:T(128)S(1)}, s32[32]{0:T(128)}, u32[]{:S(2)}) copy-start(s32[32]{0:T(128)} %param.27) | copy-start | bytes 388
  7.2 15.7 %copy-start.9 = (bf16[1,512,128]{2,1,0:T(8,128)(2,1)S(1)}, bf16[1,512,128]{2,1,0:T(8,128)(2,1)}, u32[]{:S(2)}) copy-start(bf16[1,512,128]{2,1,0:T(8,128)(2,1)} %param.22) | copy-start | bytes 393220
  7.2 54.5 %all-gather.6.cloned.1.call-start = ((), (), s32[]{:S(2)}) async-start(), calls=%async_computation.4 | async-start | bytes 2228224 | tf_op jit(solution)/shard_map/all_gather | solution.py:125
  7.9 574.8 %all-gather.4.cloned.1.call-start = ((), (), s32[]{:S(2)}) async-start(), calls=%async_computation.3 | async-start | bytes 11796480 | tf_op jit(solution)/shard_map/all_gather | solution.py:175
  8.7 739.0 %reduce-scatter.7.cloned.1.call-start = ((), (), s32[]{:S(2)}) async-start(), calls=%async_computation.5 | async-start | bytes 9732096
  174.9 2.5 copy-start.1
  178.7 2.2 copy-start.2
  182.9 12.2 %collective-permute-start.1 = (f32[2,512,128]{2,1,0:T(8,128)}, f32[2,512,128]{2,1,0:T(8,128)}, u32[]{:S(2)}, u32[]{:S(2)}) collective-permute-start(f32[2,512,128]{2,1,0:T(8,128)} %add.314), channel_id=1, source_target_pairs={{0,4},{4,8},{8,12},{12,16},{16,20},{20,24},{24,28},{28,32},{32,36}... | collective-permute-start | bytes 1572872 | tf_op jit(solution)/shard_map/while/body/eval_jaxpr/ppermute | solution.py:16
  184.0 11.1 %collective-permute-start = (bf16[2,512,128]{2,1,0:T(8,128)(2,1)S(1)}, bf16[2,512,128]{2,1,0:T(8,128)(2,1)}, u32[]{:S(2)}, u32[]{:S(2)}) collective-permute-start(bf16[2,512,128]{2,1,0:T(8,128)(2,1)S(1)} %copy.79), channel_id=1, source_target_pairs={{0,4},{4,8},{8,12},{12,16},{16,20},{20,24},{24,28},{28,32},{32,36}... | collective-permute-start | bytes 786440 | tf_op jit(solution)/shard_map/while/body/eval_jaxpr/ppermute | solution.py:16
  199.1 2.6 copy-start.1
  202.9 2.2 copy-start.2
  207.1 11.7 %collective-permute-start.1 = (f32[2,512,128]{2,1,0:T(8,128)}, f32[2,512,128]{2,1,0:T(8,128)}, u32[]{:S(2)}, u32[]{:S(2)}) collective-permute-start(f32[2,512,128]{2,1,0:T(8,128)} %add.314), channel_id=1, source_target_pairs={{0,4},{4,8},{8,12},{12,16},{16,20},{20,24},{24,28},{28,32},{32,36}... | collective-permute-start | bytes 1572872 | tf_op jit(solution)/shard_map/while/body/eval_jaxpr/ppermute | solution.py:16
  209.7 9.1 %collective-permute-start = (bf16[2,512,128]{2,1,0:T(8,128)(2,1)S(1)}, bf16[2,512,128]{2,1,0:T(8,128)(2,1)}, u32[]{:S(2)}, u32[]{:S(2)}) collective-permute-start(bf16[2,512,128]{2,1,0:T(8,128)(2,1)S(1)} %copy.79), channel_id=1, source_target_pairs={{0,4},{4,8},{8,12},{12,16},{16,20},{20,24},{24,28},{28,32},{32,36}... | collective-permute-start | bytes 786440 | tf_op jit(solution)/shard_map/while/body/eval_jaxpr/ppermute | solution.py:16
  222.9 2.5 copy-start.1
  226.7 2.2 copy-start.2
  230.9 11.7 %collective-permute-start.1 = (f32[2,512,128]{2,1,0:T(8,128)}, f32[2,512,128]{2,1,0:T(8,128)}, u32[]{:S(2)}, u32[]{:S(2)}) collective-permute-start(f32[2,512,128]{2,1,0:T(8,128)} %add.314), channel_id=1, source_target_pairs={{0,4},{4,8},{8,12},{12,16},{16,20},{20,24},{24,28},{28,32},{32,36}... | collective-permute-start | bytes 1572872 | tf_op jit(solution)/shard_map/while/body/eval_jaxpr/ppermute | solution.py:16
  233.5 9.1 %collective-permute-start = (bf16[2,512,128]{2,1,0:T(8,128)(2,1)S(1)}, bf16[2,512,128]{2,1,0:T(8,128)(2,1)}, u32[]{:S(2)}, u32[]{:S(2)}) collective-permute-start(bf16[2,512,128]{2,1,0:T(8,128)(2,1)S(1)} %copy.79), channel_id=1, source_target_pairs={{0,4},{4,8},{8,12},{12,16},{16,20},{20,24},{24,28},{28,32},{32,36}... | collective-permute-start | bytes 786440 | tf_op jit(solution)/shard_map/while/body/eval_jaxpr/ppermute | solution.py:16
  246.7 2.6 copy-start.1
  254.7 12.8 %collective-permute-start.1 = (f32[2,512,128]{2,1,0:T(8,128)}, f32[2,512,128]{2,1,0:T(8,128)}, u32[]{:S(2)}, u32[]{:S(2)}) collective-permute-start(f32[2,512,128]{2,1,0:T(8,128)} %add.314), channel_id=1, source_target_pairs={{0,4},{4,8},{8,12},{12,16},{16,20},{20,24},{24,28},{28,32},{32,36}... | collective-permute-start | bytes 1572872 | tf_op jit(solution)/shard_map/while/body/eval_jaxpr/ppermute | solution.py:16
  257.3 9.6 %collective-permute-start = (bf16[2,512,128]{2,1,0:T(8,128)(2,1)S(1)}, bf16[2,512,128]{2,1,0:T(8,128)(2,1)}, u32[]{:S(2)}, u32[]{:S(2)}) collective-permute-start(bf16[2,512,128]{2,1,0:T(8,128)(2,1)S(1)} %copy.79), channel_id=1, source_target_pairs={{0,4},{4,8},{8,12},{12,16},{16,20},{20,24},{24,28},{28,32},{32,36}... | collective-permute-start | bytes 786440 | tf_op jit(solution)/shard_map/while/body/eval_jaxpr/ppermute | solution.py:16
  271.5 2.6 copy-start.1
  275.3 2.2 copy-start.2
  279.5 15.3 %collective-permute-start.1 = (f32[2,512,128]{2,1,0:T(8,128)}, f32[2,512,128]{2,1,0:T(8,128)}, u32[]{:S(2)}, u32[]{:S(2)}) collective-permute-start(f32[2,512,128]{2,1,0:T(8,128)} %add.314), channel_id=1, source_target_pairs={{0,4},{4,8},{8,12},{12,16},{16,20},{20,24},{24,28},{28,32},{32,36}... | collective-permute-start | bytes 1572872 | tf_op jit(solution)/shard_map/while/body/eval_jaxpr/ppermute | solution.py:16
  281.0 13.3 %collective-permute-start = (bf16[2,512,128]{2,1,0:T(8,128)(2,1)S(1)}, bf16[2,512,128]{2,1,0:T(8,128)(2,1)}, u32[]{:S(2)}, u32[]{:S(2)}) collective-permute-start(bf16[2,512,128]{2,1,0:T(8,128)(2,1)S(1)} %copy.79), channel_id=1, source_target_pairs={{0,4},{4,8},{8,12},{12,16},{16,20},{20,24},{24,28},{28,32},{32,36}... | collective-permute-start | bytes 786440 | tf_op jit(solution)/shard_map/while/body/eval_jaxpr/ppermute | solution.py:16
  298.9 2.6 copy-start.1
  302.7 2.2 copy-start.2
  306.9 15.3 %collective-permute-start.1 = (f32[2,512,128]{2,1,0:T(8,128)}, f32[2,512,128]{2,1,0:T(8,128)}, u32[]{:S(2)}, u32[]{:S(2)}) collective-permute-start(f32[2,512,128]{2,1,0:T(8,128)} %add.314), channel_id=1, source_target_pairs={{0,4},{4,8},{8,12},{12,16},{16,20},{20,24},{24,28},{28,32},{32,36}... | collective-permute-start | bytes 1572872 | tf_op jit(solution)/shard_map/while/body/eval_jaxpr/ppermute | solution.py:16
  306.9 14.8 %collective-permute-start = (bf16[2,512,128]{2,1,0:T(8,128)(2,1)S(1)}, bf16[2,512,128]{2,1,0:T(8,128)(2,1)}, u32[]{:S(2)}, u32[]{:S(2)}) collective-permute-start(bf16[2,512,128]{2,1,0:T(8,128)(2,1)S(1)} %copy.79), channel_id=1, source_target_pairs={{0,4},{4,8},{8,12},{12,16},{16,20},{20,24},{24,28},{28,32},{32,36}... | collective-permute-start | bytes 786440 | tf_op jit(solution)/shard_map/while/body/eval_jaxpr/ppermute | solution.py:16
  326.3 2.6 copy-start.1
  330.1 2.2 copy-start.2
  334.3 15.3 %collective-permute-start.1 = (f32[2,512,128]{2,1,0:T(8,128)}, f32[2,512,128]{2,1,0:T(8,128)}, u32[]{:S(2)}, u32[]{:S(2)}) collective-permute-start(f32[2,512,128]{2,1,0:T(8,128)} %add.314), channel_id=1, source_target_pairs={{0,4},{4,8},{8,12},{12,16},{16,20},{20,24},{24,28},{28,32},{32,36}... | collective-permute-start | bytes 1572872 | tf_op jit(solution)/shard_map/while/body/eval_jaxpr/ppermute | solution.py:16
  334.3 14.8 %collective-permute-start = (bf16[2,512,128]{2,1,0:T(8,128)(2,1)S(1)}, bf16[2,512,128]{2,1,0:T(8,128)(2,1)}, u32[]{:S(2)}, u32[]{:S(2)}) collective-permute-start(bf16[2,512,128]{2,1,0:T(8,128)(2,1)S(1)} %copy.79), channel_id=1, source_target_pairs={{0,4},{4,8},{8,12},{12,16},{16,20},{20,24},{24,28},{28,32},{32,36}... | collective-permute-start | bytes 786440 | tf_op jit(solution)/shard_map/while/body/eval_jaxpr/ppermute | solution.py:16
  353.7 2.6 copy-start.1
  357.5 2.2 copy-start.2
  361.7 15.3 %collective-permute-start.1 = (f32[2,512,128]{2,1,0:T(8,128)}, f32[2,512,128]{2,1,0:T(8,128)}, u32[]{:S(2)}, u32[]{:S(2)}) collective-permute-start(f32[2,512,128]{2,1,0:T(8,128)} %add.314), channel_id=1, source_target_pairs={{0,4},{4,8},{8,12},{12,16},{16,20},{20,24},{24,28},{28,32},{32,36}... | collective-permute-start | bytes 1572872 | tf_op jit(solution)/shard_map/while/body/eval_jaxpr/ppermute | solution.py:16
  361.7 14.8 %collective-permute-start = (bf16[2,512,128]{2,1,0:T(8,128)(2,1)S(1)}, bf16[2,512,128]{2,1,0:T(8,128)(2,1)}, u32[]{:S(2)}, u32[]{:S(2)}) collective-permute-start(bf16[2,512,128]{2,1,0:T(8,128)(2,1)S(1)} %copy.79), channel_id=1, source_target_pairs={{0,4},{4,8},{8,12},{12,16},{16,20},{20,24},{24,28},{28,32},{32,36}... | collective-permute-start | bytes 786440 | tf_op jit(solution)/shard_map/while/body/eval_jaxpr/ppermute | solution.py:16
  381.1 2.6 copy-start.1
  384.9 2.2 copy-start.2
  389.1 15.3 %collective-permute-start.1 = (f32[2,512,128]{2,1,0:T(8,128)}, f32[2,512,128]{2,1,0:T(8,128)}, u32[]{:S(2)}, u32[]{:S(2)}) collective-permute-start(f32[2,512,128]{2,1,0:T(8,128)} %add.314), channel_id=1, source_target_pairs={{0,4},{4,8},{8,12},{12,16},{16,20},{20,24},{24,28},{28,32},{32,36}... | collective-permute-start | bytes 1572872 | tf_op jit(solution)/shard_map/while/body/eval_jaxpr/ppermute | solution.py:16
  389.1 14.8 %collective-permute-start = (bf16[2,512,128]{2,1,0:T(8,128)(2,1)S(1)}, bf16[2,512,128]{2,1,0:T(8,128)(2,1)}, u32[]{:S(2)}, u32[]{:S(2)}) collective-permute-start(bf16[2,512,128]{2,1,0:T(8,128)(2,1)S(1)} %copy.79), channel_id=1, source_target_pairs={{0,4},{4,8},{8,12},{12,16},{16,20},{20,24},{24,28},{28,32},{32,36}... | collective-permute-start | bytes 786440 | tf_op jit(solution)/shard_map/while/body/eval_jaxpr/ppermute | solution.py:16
  408.5 2.6 copy-start.1
  412.3 2.2 copy-start.2
  416.5 9.2 %collective-permute-start.1 = (f32[2,512,128]{2,1,0:T(8,128)}, f32[2,512,128]{2,1,0:T(8,128)}, u32[]{:S(2)}, u32[]{:S(2)}) collective-permute-start(f32[2,512,128]{2,1,0:T(8,128)} %add.314), channel_id=1, source_target_pairs={{0,4},{4,8},{8,12},{12,16},{16,20},{20,24},{24,28},{28,32},{32,36}... | collective-permute-start | bytes 1572872 | tf_op jit(solution)/shard_map/while/body/eval_jaxpr/ppermute | solution.py:16
  416.5 9.1 %collective-permute-start = (bf16[2,512,128]{2,1,0:T(8,128)(2,1)S(1)}, bf16[2,512,128]{2,1,0:T(8,128)(2,1)}, u32[]{:S(2)}, u32[]{:S(2)}) collective-permute-start(bf16[2,512,128]{2,1,0:T(8,128)(2,1)S(1)} %copy.79), channel_id=1, source_target_pairs={{0,4},{4,8},{8,12},{12,16},{16,20},{20,24},{24,28},{28,32},{32,36}... | collective-permute-start | bytes 786440 | tf_op jit(solution)/shard_map/while/body/eval_jaxpr/ppermute | solution.py:16
  430.7 22.4 %collective-permute-start.1 = (f32[2,512,128]{2,1,0:T(8,128)}, f32[2,512,128]{2,1,0:T(8,128)}, u32[]{:S(2)}, u32[]{:S(2)}) collective-permute-start(f32[2,512,128]{2,1,0:T(8,128)} %add.314), channel_id=1, source_target_pairs={{0,4},{4,8},{8,12},{12,16},{16,20},{20,24},{24,28},{28,32},{32,36}... | collective-permute-start | bytes 1572872 | tf_op jit(solution)/shard_map/while/body/eval_jaxpr/ppermute | solution.py:16
  440.3 12.2 %collective-permute-start = (bf16[2,512,128]{2,1,0:T(8,128)(2,1)S(1)}, bf16[2,512,128]{2,1,0:T(8,128)(2,1)}, u32[]{:S(2)}, u32[]{:S(2)}) collective-permute-start(bf16[2,512,128]{2,1,0:T(8,128)(2,1)S(1)} %copy.79), channel_id=1, source_target_pairs={{0,4},{4,8},{8,12},{12,16},{16,20},{20,24},{24,28},{28,32},{32,36}... | collective-permute-start | bytes 786440 | tf_op jit(solution)/shard_map/while/body/eval_jaxpr/ppermute | solution.py:16
  457.1 2.6 copy-start.1
  465.1 15.3 %collective-permute-start.1 = (f32[2,512,128]{2,1,0:T(8,128)}, f32[2,512,128]{2,1,0:T(8,128)}, u32[]{:S(2)}, u32[]{:S(2)}) collective-permute-start(f32[2,512,128]{2,1,0:T(8,128)} %add.314), channel_id=1, source_target_pairs={{0,4},{4,8},{8,12},{12,16},{16,20},{20,24},{24,28},{28,32},{32,36}... | collective-permute-start | bytes 1572872 | tf_op jit(solution)/shard_map/while/body/eval_jaxpr/ppermute | solution.py:16
  465.1 14.8 %collective-permute-start = (bf16[2,512,128]{2,1,0:T(8,128)(2,1)S(1)}, bf16[2,512,128]{2,1,0:T(8,128)(2,1)}, u32[]{:S(2)}, u32[]{:S(2)}) collective-permute-start(bf16[2,512,128]{2,1,0:T(8,128)(2,1)S(1)} %copy.79), channel_id=1, source_target_pairs={{0,4},{4,8},{8,12},{12,16},{16,20},{20,24},{24,28},{28,32},{32,36}... | collective-permute-start | bytes 786440 | tf_op jit(solution)/shard_map/while/body/eval_jaxpr/ppermute | solution.py:16
  484.5 2.6 copy-start.1
  492.5 15.3 %collective-permute-start.1 = (f32[2,512,128]{2,1,0:T(8,128)}, f32[2,512,128]{2,1,0:T(8,128)}, u32[]{:S(2)}, u32[]{:S(2)}) collective-permute-start(f32[2,512,128]{2,1,0:T(8,128)} %add.314), channel_id=1, source_target_pairs={{0,4},{4,8},{8,12},{12,16},{16,20},{20,24},{24,28},{28,32},{32,36}... | collective-permute-start | bytes 1572872 | tf_op jit(solution)/shard_map/while/body/eval_jaxpr/ppermute | solution.py:16
  492.5 14.8 %collective-permute-start = (bf16[2,512,128]{2,1,0:T(8,128)(2,1)S(1)}, bf16[2,512,128]{2,1,0:T(8,128)(2,1)}, u32[]{:S(2)}, u32[]{:S(2)}) collective-permute-start(bf16[2,512,128]{2,1,0:T(8,128)(2,1)S(1)} %copy.79), channel_id=1, source_target_pairs={{0,4},{4,8},{8,12},{12,16},{16,20},{20,24},{24,28},{28,32},{32,36}... | collective-permute-start | bytes 786440 | tf_op jit(solution)/shard_map/while/body/eval_jaxpr/ppermute | solution.py:16
  511.9 2.6 copy-start.1
  519.9 9.2 %collective-permute-start.1 = (f32[2,512,128]{2,1,0:T(8,128)}, f32[2,512,128]{2,1,0:T(8,128)}, u32[]{:S(2)}, u32[]{:S(2)}) collective-permute-start(f32[2,512,128]{2,1,0:T(8,128)} %add.314), channel_id=1, source_target_pairs={{0,4},{4,8},{8,12},{12,16},{16,20},{20,24},{24,28},{28,32},{32,36}... | collective-permute-start | bytes 1572872 | tf_op jit(solution)/shard_map/while/body/eval_jaxpr/ppermute | solution.py:16
  519.9 9.1 %collective-permute-start = (bf16[2,512,128]{2,1,0:T(8,128)(2,1)S(1)}, bf16[2,512,128]{2,1,0:T(8,128)(2,1)}, u32[]{:S(2)}, u32[]{:S(2)}) collective-permute-start(bf16[2,512,128]{2,1,0:T(8,128)(2,1)S(1)} %copy.79), channel_id=1, source_target_pairs={{0,4},{4,8},{8,12},{12,16},{16,20},{20,24},{24,28},{28,32},{32,36}... | collective-permute-start | bytes 786440 | tf_op jit(solution)/shard_map/while/body/eval_jaxpr/ppermute | solution.py:16
  534.1 22.4 %collective-permute-start.1 = (f32[2,512,128]{2,1,0:T(8,128)}, f32[2,512,128]{2,1,0:T(8,128)}, u32[]{:S(2)}, u32[]{:S(2)}) collective-permute-start(f32[2,512,128]{2,1,0:T(8,128)} %add.314), channel_id=1, source_target_pairs={{0,4},{4,8},{8,12},{12,16},{16,20},{20,24},{24,28},{28,32},{32,36}... | collective-permute-start | bytes 1572872 | tf_op jit(solution)/shard_map/while/body/eval_jaxpr/ppermute | solution.py:16
  543.7 12.2 %collective-permute-start = (bf16[2,512,128]{2,1,0:T(8,128)(2,1)S(1)}, bf16[2,512,128]{2,1,0:T(8,128)(2,1)}, u32[]{:S(2)}, u32[]{:S(2)}) collective-permute-start(bf16[2,512,128]{2,1,0:T(8,128)(2,1)S(1)} %copy.79), channel_id=1, source_target_pairs={{0,4},{4,8},{8,12},{12,16},{16,20},{20,24},{24,28},{28,32},{32,36}... | collective-permute-start | bytes 786440 | tf_op jit(solution)/shard_map/while/body/eval_jaxpr/ppermute | solution.py:16
  556.5 2.5 copy-start.6
  558.7 3.4 copy-start.3
  564.3 2.7 copy-start.4
  568.4 14.3 %collective-permute-start.2 = (bf16[2,512,128]{2,1,0:T(8,128)(2,1)S(1)}, bf16[2,512,128]{2,1,0:T(8,128)(2,1)S(1)}, u32[]{:S(2)}, u32[]{:S(2)}) collective-permute-start(bf16[2,512,128]{2,1,0:T(8,128)(2,1)S(1)} %add.200), channel_id=1, source_target_pairs={{0,4},{4,8},{8,12},{12,16},{16,20},{20,24},{24,28},{28,32},{32,36}... | collective-permute-start | bytes 786440 | tf_op jit(solution)/shard_map/ppermute | solution.py:16
  601.2 243.4 %reduce-scatter.5.cloned.1.call-start = ((), (), s32[]{:S(2)}) async-start(), calls=%async_computation.2 | async-start | bytes 11796480 | tf_op jit(solution)/shard_map/reduce_scatter | solution.py:170
  (18 other events, 27.5 us)
Sparse Core Ops, SparseCore 0:
  10.5 51.2 all-gather.5
  63.4 89.8 all-gather.3
  601.4 146.3 reduce-scatter.6
  750.6 93.9 reduce-scatter.4
where the time goes:
time: 856 us; the launch traced here: 851 us
  waiting for transfers between devices  446 us (52%)
  matrix products  154 us (18%)
  other arithmetic  87.9 us (10%)
  local copies, waits for them, and re-layouts  53.8 us (6%)
  loops' own time  51.3 us (6%)
  starting transfers between devices  43 us (5%)
  between operations  15.1 us (2%)
    ppermute x31, waiting for transfers between devices, passed_along(): lax.ppermute(shard, axis, [(i, (i + by) % peers) for i in range(peers)])  190 us
    unnamed x5, waiting for transfers between devices  125 us
    reduce_scatter x1, waiting for transfers between devices, per_device(): lax.psum_scatter((key_term + value_term).astype(jnp.bfloat16), 'tensor',...  94.3 us
    dot_general x28, matrix products, tile_scores(): jnp.einsum('rghd,ngd->ghrn', query_block, key_view, preferred_element_typ...  44.2 us
    ppermute x31, starting transfers between devices, passed_along(): lax.ppermute(shard, axis, [(i, (i + by) % peers) for i in range(peers)])  42.8 us
    all_gather x1, waiting for transfers between devices, per_device(): lax.all_gather(key_heads[0], 'ctx', axis=0, tiled=True)  36.5 us
    dot_general x14, matrix products, backward_compute(): jnp.einsum('rghd,ngd->ghrn', grad_block, value_view, preferred_element_ty...  32 us
    another operation x1, loops' own time, per_device(): lax.scan(over_tiles, (top_init, total_init), (tile_stack, jnp.arange(tile...  30.1 us
  transfers between devices with their start and end apart: 35, of which 29 were waited for; matrix products, arithmetic and copies ran while one was open for 32% of the time, Pallas kernels for 0%

commit v1 on v0

v1 whole, which is shorter than its diff:
```python
import functools

import jax
import jax.numpy as jnp
from jax import lax
from jax.experimental import pallas as pl
from jax.experimental.pallas import tpu as pltpu
from jax.sharding import PartitionSpec as P

HD = 128
HQ = 6
NH = 3
BLK = 256
NX = 4
LOG2E = 1.4426950408889634
NEG = -1e30
SC = HD ** (-0.5)
F32 = jnp.float32
BF = jnp.bfloat16

CORE_PERM = [(i, i ^ 1) for i in range(16)]
ZHI_PERM = [(i, i ^ 8) for i in range(16)]
CHIP_GROUPS = [[2 * i + c for i in range(8)] for c in range(2)]
ALL_CHIP_GROUPS = [[2 * i + c for i in range(16)] for c in range(2)]


def y_perm(by):
    return [(i, (i & 9) | (((((i >> 1) & 3) + by) & 3) << 1)) for i in range(16)]


def x_perm(by):
    return [(i, (i + by) % NX) for i in range(NX)]


def cx_perm(flip, by):
    return [(i, (((i >> 2) ^ flip) << 2) | ((i + by) & 3)) for i in range(64)]


def home_perm():
    pairs = []
    for i in range(128):
        dp, ctx, t = i >> 6, (i >> 2) & 15, i & 3
        core, piece = ctx & 1, dp * 8 + (ctx >> 1)
        row, dx = core * 16 + t * 4 + (piece >> 2), piece & 3
        pairs.append((i, row * 4 + ((t + dx) & 3)))
    return pairs


def load_pair(own, got, dst, core, sem, at):
    half = own.shape[0]
    cols = pl.ds(pl.multiple_of(core * (NH * HD), HD), NH * HD)
    copies = [
        pltpu.make_async_copy(own.at[:, cols], dst.at[0:half, :], sem.at[at]),
        pltpu.make_async_copy(got, dst.at[half : 2 * half, :], sem.at[at + 1]),
    ]
    for c in copies:
        c.start()
    return copies


def load_slots(refs, dst, cols, sem, at):
    copies = []
    row = 0
    for n, ref in enumerate(refs):
        r = pl.ds(row, ref.shape[0])
        copies.append(pltpu.make_async_copy(ref, dst.at[r, cols], sem.at[at + n]))
        copies[-1].start()
        row += ref.shape[0]
    return copies


def put_scores_side(qT, b, cw, q):
    scaled = q.astype(F32) * (SC * LOG2E)
    hi = scaled.astype(BF)
    lo = (scaled - hi.astype(F32)).astype(BF)
    qT[b, 0:HD, cw] = hi.T
    qT[b, HD : 2 * HD, cw] = lo.T


def scores(kaug, qT, b, kp):
    r = pl.ds(pl.multiple_of(kp * BLK, BLK), BLK)
    return jnp.dot(kaug[r, :], qT[b], preferred_element_type=F32)


def causal():
    key_i = lax.broadcasted_iota(jnp.int32, (BLK, NH * BLK), 0)
    qry_i = lax.broadcasted_iota(jnp.int32, (BLK, NH * BLK), 1) % BLK
    return key_i <= qry_i


def over_keys(rank, pos_ref, step, width):
    def one(j, _):
        step(j, False)
        return 0

    def wide(j, _):
        for u in range(width):
            step(width * j + u, False)
        return 0

    lax.fori_loop(0, rank // width, wide, 0)
    lax.fori_loop(width * (rank // width), rank, one, 0)
    step(rank, True)


def stats_kernel(rank_ref, pos_ref, core_ref, q_own, q_got, *rest, nq, n_slots):
    k_refs = rest[:n_slots]
    lse = rest[n_slots]
    qs, kaug, qT, m_s, l_s, sem, sem_k = rest[n_slots + 1 :]
    W = NH * BLK
    first = load_pair(q_own, q_got, qs, core_ref[0], sem, 0)
    copies = load_slots(k_refs, kaug, pl.ds(0, HD), sem_k, 0)
    copies += load_slots(k_refs, kaug, pl.ds(HD, HD), sem_k, n_slots)
    for c in first:
        c.wait()

    def prep(b, _):
        r = pl.ds(pl.multiple_of(b * BLK, BLK), BLK)
        for h in range(NH):
            put_scores_side(qT, b, pl.ds(h * BLK, BLK), qs[r, pl.ds(h * HD, HD)])
        return 0

    lax.fori_loop(0, nq, prep, 0)
    for c in copies:
        c.wait()
    allowed = causal()

    def q_loop(b, _):
        def step(j, diag):
            s = scores(kaug, qT, b, pos_ref[j])
            if diag:
                s = jnp.where(allowed, s, NEG)
            s3 = s.reshape(BLK // 8, 8, W)
            m0 = m_s[...]
            m1 = jnp.maximum(m0, jnp.max(s3, axis=0))
            l_s[...] = l_s[...] * jnp.exp2(m0 - m1) + jnp.sum(jnp.exp2(s3 - m1[None]), axis=0)
            m_s[...] = m1

        m_s[...] = jnp.full((8, W), NEG, F32)
        l_s[...] = jnp.zeros((8, W), F32)
        over_keys(rank_ref[b], pos_ref, step, 2)
        m = m_s[...]
        top = jnp.max(m, axis=0, keepdims=True)
        total = jnp.sum(l_s[...] * jnp.exp2(m - top), axis=0, keepdims=True)
        lse[b] = top + jnp.log2(total)
        return 0

    lax.fori_loop(0, nq, q_loop, 0)


def grads_kernel(
    rank_ref, pos_ref, to_ref, core_ref, lse, q_own, q_got, do_own, o_own, do_o_got, *rest, nq, n_slots
):
    k_refs = rest[:n_slots]
    v_refs = rest[n_slots : 2 * n_slots]
    dq_keep, dq_send, dkv0, dkv1 = rest[2 * n_slots : 2 * n_slots + 4]
    qs, dos, os, kaug, vaug, qT, doT, qn, don, dqT, dkv, sem, sem_kv = rest[2 * n_slots + 4 :]
    W = NH * BLK
    half = nq * BLK // 2
    nblk = kaug.shape[0] // BLK
    core = core_ref[0]
    first = load_pair(q_own, q_got, qs, core, sem, 0)
    first += load_pair(do_own, do_o_got.at[0], dos, core, sem, 2)
    first += load_pair(o_own, do_o_got.at[1], os, core, sem, 4)
    copies = load_slots(k_refs, kaug, pl.ds(0, HD), sem_kv, 0)
    copies += load_slots(k_refs, kaug, pl.ds(HD, HD), sem_kv, n_slots)
    copies += load_slots(v_refs, vaug, pl.ds(0, HD), sem_kv, 2 * n_slots)
    lane = lax.broadcasted_iota(jnp.int32, (BLK, HD), 1)
    ones = jnp.where(lane < 3, 1.0, 0.0).astype(BF)

    def init(i, _):
        r = pl.ds(pl.multiple_of(i * BLK, BLK), BLK)
        vaug[r, HD : 2 * HD] = ones
        dkv[r, :] = jnp.zeros((BLK, 2 * HD), F32)
        return 0

    lax.fori_loop(0, nblk, init, 0)
    for c in first:
        c.wait()

    def prep(b, _):
        r = pl.ds(pl.multiple_of(b * BLK, BLK), BLK)
        for h in range(NH):
            cq = pl.ds(h * HD, HD)
            cw = pl.ds(h * BLK, BLK)
            q = qs[r, cq]
            do = dos[r, cq]
            o = os[r, cq]
            qn[b, cw, :] = q
            don[b, cw, :] = do
            put_scores_side(qT, b, cw, q)
            doT[b, 0:HD, cw] = do.T
            d = -jnp.sum((do.astype(F32) * o.astype(F32)).T, axis=0, keepdims=True)
            d1 = d.astype(BF).astype(F32)
            d2 = (d - d1).astype(BF).astype(F32)
            d3 = d - d1 - d2
            sub = lax.broadcasted_iota(jnp.int32, (HD, BLK), 0)
            aug = jnp.where(sub == 0, d1, jnp.where(sub == 1, d2, jnp.where(sub == 2, d3, 0.0)))
            doT[b, HD : 2 * HD, cw] = aug.astype(BF)
        return 0

    lax.fori_loop(0, nq, prep, 0)
    for c in copies:
        c.wait()
    allowed = causal()

    def q_loop(b, _):
        def step(j, diag):
            kp = pos_ref[j]
            r = pl.ds(pl.multiple_of(kp * BLK, BLK), BLK)
            to = pl.ds(pl.multiple_of(to_ref[j] * BLK, BLK), BLK)
            p = jnp.exp2(scores(kaug, qT, b, kp) - lse[b])
            if diag:
                p = jnp.where(allowed, p, 0.0)
            dp = jnp.dot(vaug[r, :], doT[b], preferred_element_type=F32)
            p16 = p.astype(BF)
            ds16 = (p * dp).astype(BF)
            dkv[to, HD : 2 * HD] += jnp.dot(p16, don[b], preferred_element_type=F32)
            dkv[to, 0:HD] += jnp.dot(ds16, qn[b], preferred_element_type=F32)
            dqT[...] += lax.dot_general(
                kaug[r, 0:HD], ds16, (((0,), (0,)), ((), ())), preferred_element_type=F32
            )

        dqT[...] = jnp.zeros(dqT.shape, F32)
        over_keys(rank_ref[b], pos_ref, step, 2)
        for h in range(NH):
            qs[pl.ds(pl.multiple_of(b * BLK, BLK), BLK), pl.ds(h * HD, HD)] = (
                dqT[:, pl.ds(h * BLK, BLK)].T * SC
            ).astype(BF)
        return 0

    lax.fori_loop(0, nq, q_loop, 0)
    dq_keep[...] = qs[0:half, :]
    dq_send[...] = qs[half : 2 * half, :]

    def finish(i, _):
        r = pl.ds(pl.multiple_of(i * BLK, BLK), BLK)
        r1 = pl.ds(pl.multiple_of((i + nblk // 2) * BLK, BLK), BLK)
        dkv0[r, 0:HD] = (dkv[r, 0:HD] * SC).astype(BF)
        dkv0[r, HD : 2 * HD] = dkv[r, HD : 2 * HD].astype(BF)
        dkv1[r, 0:HD] = (dkv[r1, 0:HD] * SC).astype(BF)
        dkv1[r, HD : 2 * HD] = dkv[r1, HD : 2 * HD].astype(BF)
        return 0

    lax.fori_loop(0, nblk // 2, finish, 0)


VM = pl.BlockSpec(memory_space=pltpu.VMEM)
SM = pl.BlockSpec(memory_space=pltpu.SMEM)
HB = pl.BlockSpec(memory_space=pl.ANY)


BIG = 60 * 1024 * 1024


def softmax_stats(rank, pos, core, q, q_got, k_slots):
    half = q.shape[0]
    nq = 2 * half // BLK
    keys = sum(k.shape[0] for k in k_slots)
    W = NH * BLK
    n = len(k_slots)
    pairs = 66 * W * BLK
    return pl.pallas_call(
        functools.partial(stats_kernel, nq=nq, n_slots=n),
        out_shape=jax.ShapeDtypeStruct((nq, 1, W), F32),
        in_specs=[SM] * 3 + [HB] * (2 + n),
        out_specs=VM,
        scratch_shapes=[
            pltpu.VMEM((2 * half, NH * HD), BF),
            pltpu.VMEM((keys, 2 * HD), BF),
            pltpu.VMEM((nq, 2 * HD, W), BF),
            pltpu.VMEM((8, W), F32),
            pltpu.VMEM((8, W), F32),
            pltpu.SemaphoreType.DMA((2,)),
            pltpu.SemaphoreType.DMA((2 * n,)),
        ],
        compiler_params=pltpu.CompilerParams(vmem_limit_bytes=BIG),
        cost_estimate=pl.CostEstimate(
            flops=16 * pairs * HD, bytes_accessed=4 * 1024 * 1024, transcendentals=pairs
        ),
        name="softmax_stats",
    )(rank, pos, core, q, q_got, *k_slots)


def attention_grads(rank, pos, to, core, lse, q, q_got, do, o, do_o_got, k_slots, v_slots):
    half = q.shape[0]
    nq = 2 * half // BLK
    keys = sum(k.shape[0] for k in k_slots)
    W = NH * BLK
    n = len(k_slots)
    pairs = 66 * W * BLK
    return pl.pallas_call(
        functools.partial(grads_kernel, nq=nq, n_slots=n),
        out_shape=(
            jax.ShapeDtypeStruct((half, NH * HD), BF),
            jax.ShapeDtypeStruct((half, NH * HD), BF),
            jax.ShapeDtypeStruct((keys // 2, 2 * HD), BF),
            jax.ShapeDtypeStruct((keys // 2, 2 * HD), BF),
        ),
        in_specs=[SM] * 4 + [VM] + [HB] * (5 + 2 * n),
        out_specs=(VM,) * 4,
        scratch_shapes=[
            pltpu.VMEM((2 * half, NH * HD), BF),
            pltpu.VMEM((2 * half, NH * HD), BF),
            pltpu.VMEM((2 * half, NH * HD), BF),
            pltpu.VMEM((keys, 2 * HD), BF),
            pltpu.VMEM((keys, 2 * HD), BF),
            pltpu.VMEM((nq, 2 * HD, W), BF),
            pltpu.VMEM((nq, 2 * HD, W), BF),
            pltpu.VMEM((nq, W, HD), BF),
            pltpu.VMEM((nq, W, HD), BF),
            pltpu.VMEM((HD, W), F32),
            pltpu.VMEM((keys, 2 * HD), F32),
            pltpu.SemaphoreType.DMA((6,)),
            pltpu.SemaphoreType.DMA((3 * n,)),
        ],
        compiler_params=pltpu.CompilerParams(vmem_limit_bytes=BIG),
        cost_estimate=pl.CostEstimate(
            flops=32 * pairs * HD, bytes_accessed=16 * 1024 * 1024, transcendentals=pairs
        ),
        name="attention_grads",
    )(rank, pos, to, core, lse, q, q_got, do, o, do_o_got, *k_slots, *v_slots)


def load_grads(here, g_refs, g_all, sem):
    copies = []
    for cs in range(2):
        for dx in range(NX):
            for d in range(NX):
                chunk = (here + d) % NX
                n = (cs * NX + dx) * NX + d
                src = g_refs[cs][dx].at[pl.ds(pl.multiple_of(chunk * HD, HD), HD), :]
                dst = g_all.at[pl.ds((cs * NX + d) * HD, HD), pl.ds(dx * 2 * HD, 2 * HD)]
                copies.append(pltpu.make_async_copy(src, dst, sem.at[n]))
    for c in copies:
        c.start()
    return copies


def input_kernel(here_ref, *rest):
    here = here_ref[0]
    g_refs = (rest[0:4], rest[4:8])
    w_refs = rest[8:12]
    outs = rest[12:20]
    g_all, w_all, sem, sem_w = rest[20:]
    copies = load_grads(here, g_refs, g_all, sem)
    for n in range(8):
        dst = w_all.at[:, pl.ds(n * HD, HD)]
        copies.append(pltpu.make_async_copy(w_refs[n // 2].at[n % 2], dst, sem_w.at[n]))
        copies[-1].start()
    for c in copies:
        c.wait()
    cols = w_all.shape[0]
    for at in range(0, cols, 2 * HD):
        c = pl.ds(at, min(2 * HD, cols - at))
        block = lax.dot_general(
            g_all[...], w_all[c, :], (((1,), (1,)), ((), ())), preferred_element_type=F32
        ).astype(BF)
        for n, out in enumerate(outs):
            out[:, c] = block[n * HD : (n + 1) * HD]


def input_blocks(here, g_slots, w_slots):
    cols = w_slots[0].shape[1]
    return pl.pallas_call(
        input_kernel,
        out_shape=tuple(jax.ShapeDtypeStruct((HD, cols), BF) for _ in range(8)),
        in_specs=[SM] + [HB] * 12,
        out_specs=(VM,) * 8,
        scratch_shapes=[
            pltpu.VMEM((8 * HD, 8 * HD), BF),
            pltpu.VMEM((cols, 8 * HD), BF),
            pltpu.SemaphoreType.DMA((32,)),
            pltpu.SemaphoreType.DMA((8,)),
        ],
        compiler_params=pltpu.CompilerParams(vmem_limit_bytes=BIG),
        cost_estimate=pl.CostEstimate(
            flops=2 * 1024 * 1024 * cols, bytes_accessed=7 * 1024 * 1024, transcendentals=0
        ),
        name="input_blocks",
    )(here, *g_slots[0], *g_slots[1], *w_slots)


def turn_kernel(*rest):
    x_refs, out = rest[:NX], rest[NX]
    for cs in range(2):
        for d in range(NX):
            n = cs * NX + d
            out[:, pl.ds(n * HD, HD)] = x_refs[(-d) % NX][cs].T


def turn_columns(x_slots):
    cols = x_slots[0].shape[2]
    return pl.pallas_call(
        turn_kernel,
        out_shape=jax.ShapeDtypeStruct((cols, 8 * HD), BF),
        in_specs=[VM] * NX,
        out_specs=VM,
        compiler_params=pltpu.CompilerParams(vmem_limit_bytes=BIG),
        name="turn_columns",
    )(*x_slots)


def proj_kernel(here_ref, *rest):
    here = here_ref[0]
    g_refs = (rest[0:4], rest[4:8])
    x_turned, out, g_all, sem = rest[8:]
    for c in load_grads(here, g_refs, g_all, sem):
        c.wait()
    part = x_turned.shape[0] // 4
    for dx in range(NX):
        block = jnp.dot(
            x_turned[...], g_all[:, pl.ds(dx * 2 * HD, 2 * HD)], preferred_element_type=F32
        ).astype(BF)
        for i in range(4):
            out[i * 4 + dx] = block[i * part : (i + 1) * part]


def proj_parts(here, g_slots, x_turned):
    cols = x_turned.shape[0]
    return pl.pallas_call(
        proj_kernel,
        out_shape=jax.ShapeDtypeStruct((16, cols // 4, 2 * HD), BF),
        in_specs=[SM] + [HB] * 8 + [VM],
        out_specs=VM,
        scratch_shapes=[
            pltpu.VMEM((8 * HD, 8 * HD), BF),
            pltpu.SemaphoreType.DMA((32,)),
        ],
        compiler_params=pltpu.CompilerParams(vmem_limit_bytes=BIG),
        cost_estimate=pl.CostEstimate(
            flops=2 * 1024 * 1024 * cols, bytes_accessed=7 * 1024 * 1024, transcendentals=0
        ),
        name="proj_parts",
    )(here, *g_slots[0], *g_slots[1], x_turned)


def place_kernel(where_ref, *rest):
    core, here = where_ref[0], where_ref[1]
    parts, out = rest[:8], rest[8]
    cols = parts[0].shape[1]
    for cs in range(2):
        for dx in range(NX):
            at = ((core + cs) % 2) * (NX * cols) + ((here - dx + NX) % NX) * cols
            out[:, pl.ds(pl.multiple_of(at, HD), cols)] = parts[cs * NX + dx][...]


def place(where, parts):
    rows, cols = parts[0].shape
    return pl.pallas_call(
        place_kernel,
        out_shape=jax.ShapeDtypeStruct((rows, 8 * cols), BF),
        in_specs=[SM] + [VM] * 8,
        out_specs=VM,
        compiler_params=pltpu.CompilerParams(vmem_limit_bytes=BIG),
        name="place_columns",
    )(where, *parts)


def summed(*terms):
    total = terms[0].astype(F32)
    for term in terms[1:]:
        total = total + term.astype(F32)
    return total


def per_device(
    normed_input,
    queries,
    key_heads,
    value_heads,
    attn_out,
    out_grad,
    key_weight,
    value_weight,
    block_order,
):
    ctx = lax.axis_index("ctx")
    here = lax.axis_index("tensor")
    zh, y, core = ctx >> 3, (ctx >> 1) & 3, ctx & 1
    pp = lax.ppermute
    barrier = lax.optimization_barrier
    q_own, do_own, o_own = queries[0], out_grad[0], attn_out[0]

    half_cols = NH * HD

    def theirs(a):
        return lax.dynamic_slice_in_dim(a, (1 - core) * half_cols, half_cols, axis=1)

    def line_of(pair):
        return [pair] + [pp(pair, "ctx", y_perm(-k)) for k in range(1, 4)]

    def both_cores(line):
        return line + [pp(jnp.concatenate(line), "ctx", CORE_PERM)]

    def with_zhi(own):
        return jnp.concatenate([own, pp(own, "ctx", ZHI_PERM)])

    k_line = line_of(with_zhi(key_heads[0]))
    q_got = pp(theirs(q_own), "ctx", CORE_PERM)
    v_pair = with_zhi(value_heads[0])
    do_o_got = pp(jnp.stack([theirs(do_own), theirs(o_own)]), "ctx", CORE_PERM)

    blocks = jnp.arange(block_order.shape[0], dtype=jnp.int32)
    owner = blocks >> 1
    flip = ((owner & 1) ^ core) * 8
    from_slot = (flip + ((((owner >> 1) - y) & 3) * 2) + ((owner >> 3) ^ zh)) * 2 + (blocks & 1)
    to_slot = (flip + (owner >> 1)) * 2 + (blocks & 1)
    at_place = block_order[None, :] == blocks[:, None]
    pos = jnp.sum(jnp.where(at_place, from_slot[None, :], 0), axis=1)
    to = jnp.sum(jnp.where(at_place, to_slot[None, :], 0), axis=1)
    mine = jnp.stack([2 * ctx, 2 * ctx + 1, 2 * (ctx ^ 1), 2 * (ctx ^ 1) + 1])
    rank = jnp.sum(jnp.where(blocks[None, :] == mine[:, None], block_order[None, :], 0), axis=1)
    core1, here1 = core.reshape(1), here.reshape(1)

    cols = normed_input.shape[2] // 8
    x_own = normed_input[0]
    x_keep = lax.dynamic_slice_in_dim(x_own, core * NX * cols, NX * cols, axis=1)
    x_got = pp(
        lax.dynamic_slice_in_dim(x_own, (1 - core) * NX * cols, NX * cols, axis=1), "ctx", CORE_PERM
    )

    def x_for(dx):
        at = ((here + dx) & 3) * cols
        return jnp.stack([lax.dynamic_slice_in_dim(a, at, cols, axis=1) for a in (x_keep, x_got)])

    def w_for(dx):
        at = (core * NX + ((here - dx) & 3)) * cols
        return jnp.stack(
            [lax.dynamic_slice_in_dim(w, at, cols, axis=0) for w in (key_weight, value_weight)]
        )

    x_near = [x_for(d) for d in range(NX)]
    w_near = [w_for(d) for d in range(NX)]
    k_line, v_pair, x_near, w_near, do_o_got = barrier((k_line, v_pair, x_near, w_near, do_o_got))
    k_slots = both_cores(k_line)
    v_line = line_of(v_pair)
    w_slots = w_near[:1] + [pp(w_near[d], "tensor", x_perm(-d)) for d in range(1, NX)]
    x_slots = x_near[:1] + [pp(x_near[d], "tensor", x_perm(d)) for d in range(1, NX)]

    lse = softmax_stats(rank, pos, core1, q_own, q_got, k_slots)
    lse, v_line, w_slots = barrier((lse, v_line, w_slots))
    v_slots = both_cores(v_line)
    dq_keep, dq_send, dkv0, dkv1 = attention_grads(
        rank, pos, to, core1, lse, q_own, q_got, do_own, o_own, do_o_got, k_slots, v_slots
    )
    dkv1, x_slots = barrier((dkv1, x_slots))

    rows = key_heads.shape[1]
    x_turned = turn_columns(x_slots)
    chip = summed(dkv0, pp(dkv1, "ctx", CORE_PERM)).astype(BF).reshape(8, rows, 2 * HD)
    terms = lax.all_to_all(chip, "ctx", 0, 0, axis_index_groups=CHIP_GROUPS, tiled=True)
    grads = jnp.sum(terms.astype(F32), axis=0).astype(BF)

    dq_got = pp(dq_send, "ctx", CORE_PERM)
    query_grad = jnp.where(
        core == 0,
        jnp.concatenate([dq_keep, dq_got], axis=1),
        jnp.concatenate([dq_got, dq_keep], axis=1),
    )

    g_own = [grads] + [pp(grads, "tensor", x_perm(-dx)) for dx in range(1, NX)]
    g_slots = (g_own, [pp(g, "ctx", CORE_PERM) for g in g_own])

    pieces = proj_parts(here1, g_slots, x_turned)
    pieces, g_slots = barrier((pieces, g_slots))
    pieces = lax.all_to_all(
        pieces, ("dp", "ctx"), 0, 0, axis_index_groups=ALL_CHIP_GROUPS, tiled=True
    )
    outs = input_blocks(here1, g_slots, w_slots)
    got = [
        outs[n] if n == 0 else pp(outs[n], ("ctx", "tensor"), cx_perm(n // NX, n % NX))
        for n in range(8)
    ]
    proj = pp(
        jnp.sum(pieces.astype(F32), axis=0).astype(BF), ("dp", "ctx", "tensor"), home_perm()
    )
    input_grad = place(jnp.stack([core, here]), got)
    return (query_grad[None], input_grad[None], proj[:, :HD], proj[:, HD:])


def solution(mesh):
    in_specs = (
        P("dp", ("ctx", "tensor"), None),
        P("dp", "ctx", "tensor"),
        P("dp", "ctx", "tensor"),
        P("dp", "ctx", "tensor"),
        P("dp", "ctx", "tensor"),
        P("dp", "ctx", "tensor"),
        P(None, "tensor"),
        P(None, "tensor"),
        P(),
    )
    out_specs = (
        P("dp", "ctx", "tensor"),
        P("dp", ("ctx", "tensor"), None),
        P(("dp", "ctx"), "tensor"),
        P(("dp", "ctx"), "tensor"),
    )
    return jax.shard_map(
        per_device, mesh=mesh, in_specs=in_specs, out_specs=out_specs, check_vma=False
    )
```

time: 856 us -> 273 us (0.32)
  waiting for transfers between devices: 446 us -> 42.3 us
  matrix products: 154 us -> 0 us
  Pallas kernels: 0 us -> 93.1 us
  other arithmetic: 87.9 us -> 14.7 us
  loops' own time: 51.3 us -> 0 us
  blocking collectives: 0 us -> 49.9 us
  local copies, waits for them, and re-layouts: 53.8 us -> 10.1 us
  starting transfers between devices: 43 us -> 58.3 us
  between operations: 15.1 us -> 1.08 us
    ppermute x31 -> x36, waiting for transfers between devices: 190 us -> 32 us  [the longest x6 14.5 us: line_of(): return [pair] + [pp(pair, 'ctx', y_perm(-k)) for k in range(1, 4)]]
    dot_general x87 -> x0, matrix products: 154 us -> none  [the longest x28 44.2 us: tile_scores(): jnp.einsum('rghd,ngd->ghrn', query_block, key_view, preferred_element_typ...]
    unnamed x5 -> x0, waiting for transfers between devices: 125 us -> none
    reduce_scatter x1 -> x0, waiting for transfers between devices: 94.3 us -> none  [per_device(): lax.psum_scatter((key_term + value_term).astype(jnp.bfloat16), 'tensor',...]
    pallas_call x0 -> x6, Pallas kernels: none -> 93.1 us  [the longest x1 49.1 us: attention_grads(): pl.pallas_call(functools.partial(grads_kernel, nq=nq, n_slots=n), out_sha...]
    add x64 -> x1, other arithmetic: 55.5 us -> 0.01 us  [per_device(): to_slot = (flip + (owner >> 1)) * 2 + (blocks & 1)]
    another operation x34 -> x0, loops' own time: 51.3 us -> none  [the longest x1 30.1 us: per_device(): lax.scan(over_tiles, (top_init, total_init), (tile_stack, jnp.arange(tile...]
    all_to_all x0 -> x1, blocking collectives: none -> 49.9 us  [per_device(): lax.all_to_all(chip, 'ctx', 0, 0, axis_index_groups=CHIP_GROUPS, tiled=True)]
  transfers between devices with their start and end apart: 35 -> 37, of which waited for: 29 -> 10; matrix products, arithmetic and copies ran while one was open for 32% -> 6% of each run, Pallas kernels for 0% -> 32%
where the time goes in v1:
time: 273 us; the launch traced here: 269 us
  Pallas kernels  93.1 us (34%)
  starting transfers between devices  58.3 us (21%)
  blocking collectives  49.9 us (18%)
  waiting for transfers between devices  42.3 us (15%)
  other arithmetic  14.7 us (5%)
  local copies, waits for them, and re-layouts  10.1 us (4%)
    all_to_all x1, blocking collectives, per_device(): lax.all_to_all(chip, 'ctx', 0, 0, axis_index_groups=CHIP_GROUPS, tiled=True)  49.9 us
    pallas_call x1, Pallas kernels, attention_grads(): pl.pallas_call(functools.partial(grads_kernel, nq=nq, n_slots=n), out_sha...  49.1 us
    pallas_call x1, Pallas kernels, softmax_stats(): pl.pallas_call(functools.partial(stats_kernel, nq=nq, n_slots=n), out_sha...  22.8 us
    ppermute x7, starting transfers between devices, per_device(): pp(outs[n], ('ctx', 'tensor'), cx_perm(n // NX, n % NX))  16.1 us
    ppermute x6, waiting for transfers between devices, line_of(): return [pair] + [pp(pair, 'ctx', y_perm(-k)) for k in range(1, 4)]  14.5 us
    ppermute x4, starting transfers between devices, per_device(): g_slots = (g_own, [pp(g, 'ctx', CORE_PERM) for g in g_own])  11.4 us
    all_to_all x1, waiting for transfers between devices, per_device(): lax.all_to_all(pieces, ('dp', 'ctx'), 0, 0, axis_index_groups=ALL_CHIP_GR...  10.4 us
    pallas_call x1, Pallas kernels, proj_parts(): pl.pallas_call(proj_kernel, out_shape=jax.ShapeDtypeStruct((16, cols // 4...  7.52 us
  transfers between devices with their start and end apart: 37, of which 10 were waited for; matrix products, arithmetic and copies ran while one was open for 6% of the time, Pallas kernels for 32%

profile of v1, /device:TPU:5, one launch (start us, length us, event | category | flops | bytes accessed | tf_op | source)
XLA Modules:
  0.0 269.5 jit_solution(13758081560214076346)
XLA Ops:
  0.7 1.4 dynamic-slice_bitcast_fusion
  2.1 0.8 collective-permute-start.6
  2.8 1.1 constant_dynamic-slice_fusion
  3.9 1.0 pad_maximum_fusion.2
  4.9 3.6 %collective-permute-start.1 = (bf16[512,128]{1,0:T(8,128)(2,1)S(1)}, bf16[512,128]{1,0:T(8,128)(2,1)S(1)}, u32[]{:S(2)}, u32[]{:S(2)}) collective-permute-start(bf16[512,128]{1,0:T(8,128)(2,1)S(1)} %bitcast.51), channel_id=1, source_target_pairs={{0,32},{4,36},{8,40},{12,44},{16,48},{20,52},{24,56},{28,60},{32,0... | collective-permute-start | bytes 393224 | tf_op jit(solution)/shard_map/ppermute | solution.py:497
  8.6 1.7 dynamic-slice_bitcast_fusion.2
  10.4 0.9 pad_maximum_fusion.7.rest_8_
  11.3 0.9 pad_maximum_fusion.8
  12.2 0.9 constant_dynamic-slice_fusion.2
  13.1 0.9 pad_maximum_fusion.9
  14.0 2.8 %collective-permute-start.2 = (bf16[1024,128]{1,0:T(8,128)(2,1)S(1)}, bf16[1024,128]{1,0:T(8,128)(2,1)S(1)}, u32[]{:S(2)}, u32[]{:S(2)}) collective-permute-start(bf16[1024,128]{1,0:T(8,128)(2,1)S(1)} %pad_maximum_fusion.11.rest_0_), channel_id=1, source_target_pairs={{0,24},{4,28},{8,0},{12,4},{16,8},{20,12},{24,16},{28,20},{32,56},... | collective-permute-start | bytes 786440 | tf_op jit(solution)/shard_map/ppermute | solution.py:491
  17.2 0.6 copy-done.20
  17.8 0.7 collective-permute-start.4
  18.5 1.0 pad_maximum_fusion.12.rest_5_
  19.7 1.2 pad_maximum_fusion.5
  20.8 1.2 pad_maximum_fusion.3
  22.0 0.8 collective-permute-done.2.rest_1_
  22.8 2.4 collective-permute-done.3.rest_2_
  25.2 7.0 %collective-permute-done.4.rest_3_ = bf16[1024,128]{1,0:T(8,128)(2,1)S(1)} collective-permute-done((bf16[1024,128]{1,0:T(8,128)(2,1)S(1)}, bf16[1024,128]{1,0:T(8,128)(2,1)S(1)}, u32[]{:S(2)}, u32[]{:S(2)}) %collective-permute-start.4) | collective-permute-done | bytes 262176 | tf_op jit(solution)/shard_map/ppermute | solution.py:491
  32.3 0.6 collective-permute-start.8
  32.9 0.8 dynamic-slice_bitcast_fusion.1
  34.2 0.7 select_reduce_fusion
  34.9 0.7 select_reduce_fusion.2.rank_ref
  36.1 2.1 collective-permute-start.9
  38.5 4.3 %collective-permute-done.10.rest_7_ = bf16[1024,128]{1,0:T(8,128)(2,1)S(1)} collective-permute-done((bf16[1024,128]{1,0:T(8,128)(2,1)S(1)}, bf16[1024,128]{1,0:T(8,128)(2,1)S(1)}, u32[]{:S(2)}, u32[]{:S(2)}) %collective-permute-start.10) | collective-permute-done | bytes 262176 | tf_op jit(solution)/shard_map/ppermute | solution.py:491
  43.0 1.8 collective-permute-start.14
  44.8 22.8 %softmax_stats.1.lse = f32[4,1,768]{2,1,0:T(1,128)} custom-call(s32[4]{0:T(128)} %select_reduce_fusion.2.rank_ref, s32[32]{0:T(128)} %get-tuple-element.103.pos_ref, s32[1]{0:T(128)} %bitcast.4.core_ref, bf16[512,768]{1,0:T(8,128)(2,1)} %bitcast.47, bf16[512,384]{1,0:T(8,128)(2,1)} %collective-permute-done.q_got, bf16[1024,128]{1,0:T(8,128)(2,1)} %copy-done.1, ...), custom_call_target="tpu_custom_call" | custom-call | flops 26575110144 | bytes 4194304 | tf_op jit(solution)/shard_map/softmax_stats/pallas_call | solution.py:263
  67.7 2.8 %collective-permute-done.14.rest_11_ = bf16[2,1152,128]{2,1,0:T(8,128)(2,1)} collective-permute-done((bf16[2,1152,128]{2,1,0:T(8,128)(2,1)S(1)}, bf16[2,1152,128]{2,1,0:T(8,128)(2,1)}, u32[]{:S(2)}, u32[]{:S(2)}) %collective-permute-start.14) | collective-permute-done | bytes 589856 | tf_op jit(solution)/shard_map/ppermute | solution.py:538
  70.5 1.0 pad_maximum_fusion.1
  71.5 1.5 collective-permute-start.15
  73.3 2.1 collective-permute-start.18
  75.4 0.8 collective-permute-start.19
  76.2 1.0 copy-done.22
  77.2 49.1 %attention_grads.1 = (bf16[512,384]{1,0:T(8,128)(2,1)}, bf16[512,384]{1,0:T(8,128)(2,1)}, bf16[4096,256]{1,0:T(8,128)(2,1)}, bf16[4096,256]{1,0:T(8,128)(2,1)}) custom-call(s32[4]{0:T(128)} %select_reduce_fusion.2.rank_ref, s32[32]{0:T(128)} %get-tuple-element.103.pos_ref, s32[32]{0:T(128)} %get-tuple-element.102.to_ref, s32[1]{0:T(128)} %bitcast.4.core_ref, ...), custom_call_target="tpu_custom_call" | custom-call | flops 53150220288 | bytes 16777216 | tf_op jit(solution)/shard_map/attention_grads/pallas_call | solution.py:292
  126.4 0.9 collective-permute-start.20
  127.3 4.0 %collective-permute-done.20 = bf16[4096,256]{1,0:T(8,128)(2,1)S(1)} collective-permute-done((bf16[4096,256]{1,0:T(8,128)(2,1)}, bf16[4096,256]{1,0:T(8,128)(2,1)S(1)}, u32[]{:S(2)}, u32[]{:S(2)}) %collective-permute-start.20) | collective-permute-done | bytes 2097184 | tf_op jit(solution)/shard_map/ppermute | solution.py:551
  131.3 2.1 add_convert_fusion
  133.4 49.9 %all_to_all.10 = bf16[8,512,256]{2,1,0:T(8,128)(2,1)S(1)} all-to-all(bf16[8,512,256]{2,1,0:T(8,128)(2,1)S(1)} %bitcast.43), channel_id=1, replica_groups={{0,8,16,24,32,40,48,56},{4,12,20,28,36,44,52,60},{1,9,17,25,33,41,49,57..., dimensions={0} | all-to-all | bytes 4194304 | tf_op jit(solution)/shard_map/all_to_all | solution.py:552
  183.7 1.8 collective-permute-start.21
  185.5 1.2 collective-permute-start.22
  186.7 0.9 collective-permute-start.23
  187.5 2.4 collective-permute-start.24
  190.0 7.7 %collective-permute-start.25 = (bf16[512,256]{1,0:T(8,128)(2,1)S(1)}, bf16[512,256]{1,0:T(8,128)(2,1)S(1)}, u32[]{:S(2)}, u32[]{:S(2)}) collective-permute-start(bf16[512,256]{1,0:T(8,128)(2,1)S(1)} %collective-permute-done.21.rest_1_), channel_id=1, source_target_pairs={{0,4},{4,0},{8,12},{12,8},{16,20},{20,16},{24,28},{28,24},{32,36},... | collective-permute-start | bytes 786440 | tf_op jit(solution)/shard_map/ppermute | solution.py:563
  198.1 2.0 collective-permute-done.23.rest_3_
  200.1 0.9 collective-permute-start.27
  201.0 3.8 %turn_columns.1.rest_8_ = bf16[1152,1024]{1,0:T(8,128)(2,1)} custom-call(bf16[2,128,1152]{2,1,0:T(8,128)(2,1)} %get-tuple-element.77.rest_0_, bf16[2,128,1152]{2,1,0:T(8,128)(2,1)} %copy-done.3, bf16[2,128,1152]{2,1,0:T(8,128)(2,1)} %copy-done.4, bf16[2,128,1152]{2,1,0:T(8,128)(2,1)} %copy-done.5), custom_call_target="tpu_custom_call" | custom-call | tf_op jit(solution)/shard_map/turn_columns/pallas_call | solution.py:394
  204.9 0.6 copy-done.26
  205.8 7.5 %proj_parts.1 = bf16[16,288,256]{2,1,0:T(8,128)(2,1)} custom-call(s32[1]{0:T(128)} %bitcast.26.here_ref, bf16[512,256]{1,0:T(8,128)(2,1)} %copy-done.11, bf16[512,256]{1,0:T(8,128)(2,1)} %copy-done.23, bf16[512,256]{1,0:T(8,128)(2,1)} %copy-done.24, bf16[512,256]{1,0:T(8,128)(2,1)} %copy-done.25, bf16[512,256]{1,0:T(8,128)(2,1)} %copy-done.26, ...), custom_call_target="tpu_custom_call" | custom-call | flops 2415919104 | bytes 7340032 | tf_op jit(solution)/shard_map/proj_parts/pallas_call | solution.py:421
  213.4 3.7 %all-to-all-start.1 = ((bf16[16,288,256]{2,1,0:T(8,128)(2,1)}), bf16[16,288,256]{2,1,0:T(8,128)(2,1)S(1)}, u32[]{:S(2)}, u32[]{:S(2)}) async-start(bf16[16,288,256]{2,1,0:T(8,128)(2,1)} %proj_parts.1), calls=%async_computation.1 | async-start | bytes 4718592 | tf_op jit(solution)/shard_map/all_to_all | solution.py:567
  217.3 6.7 %input_blocks.1 = (bf16[128,1152]{1,0:T(8,128)(2,1)}, bf16[128,1152]{1,0:T(8,128)(2,1)}, bf16[128,1152]{1,0:T(8,128)(2,1)}, bf16[128,1152]{1,0:T(8,128)(2,1)}, b...) custom-call(s32[1]{0:T(128)} %bitcast.26.here_ref, ...), custom_call_target="tpu_custom_call" | custom-call | flops 2415919104 | bytes 7340032 | tf_op jit(solution)/shard_map/input_blocks/pallas_call | solution.py:365
  224.4 1.8 collective-permute-start.29
  226.2 1.8 collective-permute-start.30
  227.9 1.2 collective-permute-start.31
  229.2 3.6 %collective-permute-done.28.rest_1_ = bf16[128,1152]{1,0:T(8,128)(2,1)S(1)} collective-permute-done((bf16[128,1152]{1,0:T(8,128)(2,1)}, bf16[128,1152]{1,0:T(8,128)(2,1)S(1)}, u32[]{:S(2)}, u32[]{:S(2)}) %collective-permute-start.28) | collective-permute-done | bytes 294944 | tf_op jit(solution)/shard_map/ppermute | solution.py:572
  232.7 11.0 %collective-permute-start.33 = (bf16[128,1152]{1,0:T(8,128)(2,1)}, bf16[128,1152]{1,0:T(8,128)(2,1)}, u32[]{:S(2)}, u32[]{:S(2)}) collective-permute-start(bf16[128,1152]{1,0:T(8,128)(2,1)} %get-tuple-element.99), channel_id=1, source_target_pairs={{0,6},{1,7},{2,4},{3,5},{4,2},{5,3},{6,0},{7,1},{8,14},{9,15},{10,... | collective-permute-start | bytes 884744 | tf_op jit(solution)/shard_map/ppermute | solution.py:572
  243.7 0.7 copy-done.10
  244.4 10.4 %all-to-all-done.1 = bf16[16,288,256]{2,1,0:T(8,128)(2,1)S(1)} async-done(((bf16[16,288,256]{2,1,0:T(8,128)(2,1)}), bf16[16,288,256]{2,1,0:T(8,128)(2,1)S(1)}, u32[]{:S(2)}, u32[]{:S(2)}) %all-to-all-start.1) | async-done | bytes 2359328 | tf_op jit(solution)/shard_map/all_to_all | solution.py:567
  254.8 1.0 reduce_sum.55
  255.8 3.2 %collective-permute-start.35 = (bf16[288,256]{1,0:T(8,128)(2,1)}, bf16[288,256]{1,0:T(8,128)(2,1)S(1)}, u32[]{:S(2)}, u32[]{:S(2)}) collective-permute-start(bf16[288,256]{1,0:T(8,128)(2,1)} %reduce_sum.55), channel_id=1, source_target_pairs={{0,0},{1,17},{2,34},{3,51},{4,64},{5,81},{6,98},{7,115},{8,1},{9,1... | collective-permute-start | bytes 442376 | tf_op jit(solution)/shard_map/ppermute | solution.py:575
  259.0 0.6 pad_add_fusion.1.where_ref
  259.6 1.1 maximum_select_fusion
  260.6 3.2 %place_columns.1 = bf16[128,9216]{1,0:T(8,128)(2,1)} custom-call(s32[2]{0:T(128)} %pad_add_fusion.1.where_ref, bf16[128,1152]{1,0:T(8,128)(2,1)} %get-tuple-element.93.rest_0_, bf16[128,1152]{1,0:T(8,128)(2,1)} %copy-done.9, bf16[128,1152]{1,0:T(8,128)(2,1)} %copy-done.10, bf16[128,1152]{1,0:T(8,128)(2,1)} %collective-permute-done.30.rest_3_, ...), custom_call_target="tpu_custom_call" | custom-call | tf_op jit(solution)/shard_map/place_columns/pallas_call | solution.py:450
  263.8 5.0 %collective-permute-done.35 = bf16[288,256]{1,0:T(8,128)(2,1)S(1)} collective-permute-done((bf16[288,256]{1,0:T(8,128)(2,1)}, bf16[288,256]{1,0:T(8,128)(2,1)S(1)}, u32[]{:S(2)}, u32[]{:S(2)}) %collective-permute-start.35) | collective-permute-done | bytes 147488 | tf_op jit(solution)/shard_map/ppermute | solution.py:575
  268.8 0.7 fusion.2
  (104 shorter events, 4.5 us)
Async XLA Ops:
  0.6 2.2 copy-start.18
  2.1 2.9 %copy-start.19 = (bf16[1,512,128]{2,1,0:T(8,128)(2,1)S(1)}, bf16[1,512,128]{2,1,0:T(8,128)(2,1)}, u32[]{:S(2)}) copy-start(bf16[1,512,128]{2,1,0:T(8,128)(2,1)} %param.11) | copy-start | bytes 393220
  2.1 17.4 %collective-permute-start.6 = (bf16[128,4608]{1,0:T(8,128)(2,1)S(1)}, bf16[128,4608]{1,0:T(8,128)(2,1)S(1)}, u32[]{:S(2)}, u32[]{:S(2)}) collective-permute-start(bf16[128,4608]{1,0:T(8,128)(2,1)S(1)} %dynamic-slice_bitcast_fusion), channel_id=1, source_target_pairs={{0,4},{4,0},{8,12},{12,8},{16,20},{20,16},{24,28},{28,24},{32,36},... | collective-permute-start | bytes 3538952 | tf_op jit(solution)/shard_map/ppermute | solution.py:519
  4.9 27.3 %collective-permute-start.7 = (bf16[2,512,384]{2,1,0:T(8,128)(2,1)}, bf16[2,512,384]{2,1,0:T(8,128)(2,1)}, u32[]{:S(2)}, u32[]{:S(2)}) collective-permute-start(bf16[2,512,384]{2,1,0:T(8,128)(2,1)} %pad_maximum_fusion.2), channel_id=1, source_target_pairs={{0,4},{4,0},{8,12},{12,8},{16,20},{20,16},{24,28},{28,24},{32,36},... | collective-permute-start | bytes 2359304 | tf_op jit(solution)/shard_map/ppermute | solution.py:502
  4.9 9.1 %collective-permute-start.1 = (bf16[512,128]{1,0:T(8,128)(2,1)S(1)}, bf16[512,128]{1,0:T(8,128)(2,1)S(1)}, u32[]{:S(2)}, u32[]{:S(2)}) collective-permute-start(bf16[512,128]{1,0:T(8,128)(2,1)S(1)} %bitcast.51), channel_id=1, source_target_pairs={{0,32},{4,36},{8,40},{12,44},{16,48},{20,52},{24,56},{28,60},{32,0... | collective-permute-start | bytes 393224 | tf_op jit(solution)/shard_map/ppermute | solution.py:497
  8.5 8.7 %collective-permute-start.5 = (bf16[512,128]{1,0:T(8,128)(2,1)}, bf16[512,128]{1,0:T(8,128)(2,1)S(1)}, u32[]{:S(2)}, u32[]{:S(2)}) collective-permute-start(bf16[512,128]{1,0:T(8,128)(2,1)} %bitcast.8), channel_id=1, source_target_pairs={{0,32},{4,36},{8,40},{12,44},{16,48},{20,52},{24,56},{28,60},{32,0... | collective-permute-start | bytes 393224 | tf_op jit(solution)/shard_map/ppermute | solution.py:497
  10.3 1.9 copy-start
  14.0 18.2 %copy-start.1 = (bf16[1024,128]{1,0:T(8,128)(2,1)}, bf16[1024,128]{1,0:T(8,128)(2,1)S(1)}, u32[]{:S(2)}) copy-start(bf16[1024,128]{1,0:T(8,128)(2,1)S(1)} %pad_maximum_fusion.11.rest_0_) | copy-start | bytes 786436
  14.0 8.8 %collective-permute-start.2 = (bf16[1024,128]{1,0:T(8,128)(2,1)S(1)}, bf16[1024,128]{1,0:T(8,128)(2,1)S(1)}, u32[]{:S(2)}, u32[]{:S(2)}) collective-permute-start(bf16[1024,128]{1,0:T(8,128)(2,1)S(1)} %pad_maximum_fusion.11.rest_0_), channel_id=1, source_target_pairs={{0,24},{4,28},{8,0},{12,4},{16,8},{20,12},{24,16},{28,20},{32,56},... | collective-permute-start | bytes 786440 | tf_op jit(solution)/shard_map/ppermute | solution.py:491
  16.8 8.3 %collective-permute-start.3 = (bf16[1024,128]{1,0:T(8,128)(2,1)S(1)}, bf16[1024,128]{1,0:T(8,128)(2,1)S(1)}, u32[]{:S(2)}, u32[]{:S(2)}) collective-permute-start(bf16[1024,128]{1,0:T(8,128)(2,1)S(1)} %pad_maximum_fusion.11.rest_0_), channel_id=1, source_target_pairs={{0,16},{4,20},{8,24},{12,28},{16,0},{20,4},{24,8},{28,12},{32,48},... | collective-permute-start | bytes 786440 | tf_op jit(solution)/shard_map/ppermute | solution.py:491
  17.8 14.4 %collective-permute-start.4 = (bf16[1024,128]{1,0:T(8,128)(2,1)S(1)}, bf16[1024,128]{1,0:T(8,128)(2,1)S(1)}, u32[]{:S(2)}, u32[]{:S(2)}) collective-permute-start(bf16[1024,128]{1,0:T(8,128)(2,1)S(1)} %pad_maximum_fusion.11.rest_0_), channel_id=1, source_target_pairs={{0,8},{4,12},{8,16},{12,20},{16,24},{20,28},{24,0},{28,4},{32,40},... | collective-permute-start | bytes 786440 | tf_op jit(solution)/shard_map/ppermute | solution.py:491
  19.5 51.0 %copy-start.2 = (bf16[1024,128]{1,0:T(8,128)(2,1)}, bf16[1024,128]{1,0:T(8,128)(2,1)S(1)}, u32[]{:S(2)}) copy-start(bf16[1024,128]{1,0:T(8,128)(2,1)S(1)} %pad_maximum_fusion.12.rest_5_) | copy-start | bytes 786436
  20.8 12.0 %copy-start.17 = (bf16[1,512,768]{2,1,0:T(8,128)(2,1)S(1)}, bf16[1,512,768]{2,1,0:T(8,128)(2,1)}, u32[]{:S(2)}) copy-start(bf16[1,512,768]{2,1,0:T(8,128)(2,1)} %param.10) | copy-start | bytes 2359300
  20.8 13.4 %copy-start.21 = (s32[32]{0:T(128)S(1)}, s32[32]{0:T(128)}, u32[]{:S(2)}) copy-start(s32[32]{0:T(128)} %param.17) | copy-start | bytes 388
  20.8 17.4 %copy-start.6 = (bf16[2,1152,128]{2,1,0:T(8,128)(2,1)S(1)}, bf16[2,1152,128]{2,1,0:T(8,128)(2,1)}, u32[]{:S(2)}) copy-start(bf16[2,1152,128]{2,1,0:T(8,128)(2,1)} %pad_maximum_fusion.8) | copy-start | bytes 1769476
  20.8 22.0 %copy-start.7 = (bf16[2,1152,128]{2,1,0:T(8,128)(2,1)S(1)}, bf16[2,1152,128]{2,1,0:T(8,128)(2,1)}, u32[]{:S(2)}) copy-start(bf16[2,1152,128]{2,1,0:T(8,128)(2,1)} %pad_maximum_fusion.9) | copy-start | bytes 1769476
  22.8 22.0 %copy-start.12 = (bf16[1024,128]{1,0:T(8,128)(2,1)}, bf16[1024,128]{1,0:T(8,128)(2,1)S(1)}, u32[]{:S(2)}) copy-start(bf16[1024,128]{1,0:T(8,128)(2,1)S(1)} %collective-permute-done.2.rest_1_) | copy-start | bytes 786436
  25.2 7.7 %copy-start.13 = (bf16[1024,128]{1,0:T(8,128)(2,1)}, bf16[1024,128]{1,0:T(8,128)(2,1)S(1)}, u32[]{:S(2)}) copy-start(bf16[1024,128]{1,0:T(8,128)(2,1)S(1)} %collective-permute-done.3.rest_2_) | copy-start | bytes 786436
  32.2 1.5 copy-start.14
  32.3 10.7 %collective-permute-start.8 = (bf16[4096,128]{1,0:T(8,128)(2,1)S(1)}, bf16[4096,128]{1,0:T(8,128)(2,1)}, u32[]{:S(2)}, u32[]{:S(2)}) collective-permute-start(bf16[4096,128]{1,0:T(8,128)(2,1)S(1)} %pad_maximum_fusion), channel_id=1, source_target_pairs={{0,4},{4,0},{8,12},{12,8},{16,20},{20,16},{24,28},{28,24},{32,36},... | collective-permute-start | bytes 3145736 | tf_op jit(solution)/shard_map/ppermute | solution.py:494
  33.7 4.6 %collective-permute-start = (bf16[512,384]{1,0:T(8,128)(2,1)}, bf16[512,384]{1,0:T(8,128)(2,1)}, u32[]{:S(2)}, u32[]{:S(2)}) collective-permute-start(bf16[512,384]{1,0:T(8,128)(2,1)} %dynamic-slice_bitcast_fusion.1), channel_id=1, source_target_pairs={{0,4},{4,0},{8,12},{12,8},{16,20},{20,16},{24,28},{28,24},{32,36},... | collective-permute-start | bytes 1179656 | tf_op jit(solution)/shard_map/ppermute | solution.py:500
  33.7 9.1 %collective-permute-start.10 = (bf16[1024,128]{1,0:T(8,128)(2,1)S(1)}, bf16[1024,128]{1,0:T(8,128)(2,1)S(1)}, u32[]{:S(2)}, u32[]{:S(2)}) collective-permute-start(bf16[1024,128]{1,0:T(8,128)(2,1)S(1)} %pad_maximum_fusion.12.rest_5_), channel_id=1, source_target_pairs={{0,16},{4,20},{8,24},{12,28},{16,0},{20,4},{24,8},{28,12},{32,48},... | collective-permute-start | bytes 786440 | tf_op jit(solution)/shard_map/ppermute | solution.py:491
  35.6 32.1 %collective-permute-start.11 = (bf16[1024,128]{1,0:T(8,128)(2,1)S(1)}, bf16[1024,128]{1,0:T(8,128)(2,1)S(1)}, u32[]{:S(2)}, u32[]{:S(2)}) collective-permute-start(bf16[1024,128]{1,0:T(8,128)(2,1)S(1)} %pad_maximum_fusion.12.rest_5_), channel_id=1, source_target_pairs={{0,8},{4,12},{8,16},{12,20},{16,24},{20,28},{24,0},{28,4},{32,40},... | collective-permute-start | bytes 786440 | tf_op jit(solution)/shard_map/ppermute | solution.py:491
  36.1 31.5 %collective-permute-start.9 = (bf16[1024,128]{1,0:T(8,128)(2,1)S(1)}, bf16[1024,128]{1,0:T(8,128)(2,1)}, u32[]{:S(2)}, u32[]{:S(2)}) collective-permute-start(bf16[1024,128]{1,0:T(8,128)(2,1)S(1)} %pad_maximum_fusion.12.rest_5_), channel_id=1, source_target_pairs={{0,24},{4,28},{8,0},{12,4},{16,8},{20,12},{24,16},{28,20},{32,56},... | collective-permute-start | bytes 786440 | tf_op jit(solution)/shard_map/ppermute | solution.py:491
  38.2 29.4 %collective-permute-start.12 = (bf16[2,1152,128]{2,1,0:T(8,128)(2,1)S(1)}, bf16[2,1152,128]{2,1,0:T(8,128)(2,1)}, u32[]{:S(2)}, u32[]{:S(2)}) collective-permute-start(bf16[2,1152,128]{2,1,0:T(8,128)(2,1)S(1)} %copy-done.6), channel_id=1, source_target_pairs={{0,3},{1,0},{2,1},{3,2},{4,7},{5,4},{6,5},{7,6},{8,11},{9,8},{10,9... | collective-permute-start | bytes 1769480 | tf_op jit(solution)/shard_map/ppermute | solution.py:538
  42.8 27.7 %copy-start.15 = (bf16[1024,128]{1,0:T(8,128)(2,1)}, bf16[1024,128]{1,0:T(8,128)(2,1)S(1)}, u32[]{:S(2)}) copy-start(bf16[1024,128]{1,0:T(8,128)(2,1)S(1)} %collective-permute-done.10.rest_7_) | copy-start | bytes 786436
  42.8 24.9 %collective-permute-start.13 = (bf16[2,1152,128]{2,1,0:T(8,128)(2,1)S(1)}, bf16[2,1152,128]{2,1,0:T(8,128)(2,1)}, u32[]{:S(2)}, u32[]{:S(2)}) collective-permute-start(bf16[2,1152,128]{2,1,0:T(8,128)(2,1)S(1)} %copy-done.7), channel_id=1, source_target_pairs={{0,2},{1,3},{2,0},{3,1},{4,6},{5,7},{6,4},{7,5},{8,10},{9,11},{10,... | collective-permute-start | bytes 1769480 | tf_op jit(solution)/shard_map/ppermute | solution.py:538
  43.0 27.5 %collective-permute-start.14 = (bf16[2,1152,128]{2,1,0:T(8,128)(2,1)S(1)}, bf16[2,1152,128]{2,1,0:T(8,128)(2,1)}, u32[]{:S(2)}, u32[]{:S(2)}) collective-permute-start(bf16[2,1152,128]{2,1,0:T(8,128)(2,1)S(1)} %pad_maximum_fusion.10), channel_id=1, source_target_pairs={{0,1},{1,2},{2,3},{3,0},{4,5},{5,6},{6,7},{7,4},{8,9},{9,10},{10,1... | collective-permute-start | bytes 1769480 | tf_op jit(solution)/shard_map/ppermute | solution.py:538
  67.6 3.9 %copy-start.16 = (bf16[1024,128]{1,0:T(8,128)(2,1)}, bf16[1024,128]{1,0:T(8,128)(2,1)S(1)}, u32[]{:S(2)}) copy-start(bf16[1024,128]{1,0:T(8,128)(2,1)S(1)} %collective-permute-done.11.rest_8_) | copy-start | bytes 786436
  71.5 4.7 %collective-permute-start.15 = (bf16[4096,128]{1,0:T(8,128)(2,1)S(1)}, bf16[4096,128]{1,0:T(8,128)(2,1)S(1)}, u32[]{:S(2)}, u32[]{:S(2)}) collective-permute-start(bf16[4096,128]{1,0:T(8,128)(2,1)S(1)} %pad_maximum_fusion.1), channel_id=1, source_target_pairs={{0,4},{4,0},{8,12},{12,8},{16,20},{20,16},{24,28},{28,24},{32,36},... | collective-permute-start | bytes 3145736 | tf_op jit(solution)/shard_map/ppermute | solution.py:494
  73.0 53.3 %collective-permute-start.17 = (bf16[2,128,1152]{2,1,0:T(8,128)(2,1)}, bf16[2,128,1152]{2,1,0:T(8,128)(2,1)S(1)}, u32[]{:S(2)}, u32[]{:S(2)}) collective-permute-start(bf16[2,128,1152]{2,1,0:T(8,128)(2,1)} %get-tuple-element.73), channel_id=1, source_target_pairs={{0,1},{1,2},{2,3},{3,0},{4,5},{5,6},{6,7},{7,4},{8,9},{9,10},{10,1... | collective-permute-start | bytes 1769480 | tf_op jit(solution)/shard_map/ppermute | solution.py:539
  73.3 53.0 %collective-permute-start.18 = (bf16[2,128,1152]{2,1,0:T(8,128)(2,1)}, bf16[2,128,1152]{2,1,0:T(8,128)(2,1)S(1)}, u32[]{:S(2)}, u32[]{:S(2)}) collective-permute-start(bf16[2,128,1152]{2,1,0:T(8,128)(2,1)} %get-tuple-element.74), channel_id=1, source_target_pairs={{0,2},{1,3},{2,0},{3,1},{4,6},{5,7},{6,4},{7,5},{8,10},{9,11},{10,... | collective-permute-start | bytes 1769480 | tf_op jit(solution)/shard_map/ppermute | solution.py:539
  75.4 50.9 %collective-permute-start.19 = (bf16[2,128,1152]{2,1,0:T(8,128)(2,1)}, bf16[2,128,1152]{2,1,0:T(8,128)(2,1)S(1)}, u32[]{:S(2)}, u32[]{:S(2)}) collective-permute-start(bf16[2,128,1152]{2,1,0:T(8,128)(2,1)} %get-tuple-element.75), channel_id=1, source_target_pairs={{0,3},{1,0},{2,1},{3,2},{4,7},{5,4},{6,5},{7,6},{8,11},{9,8},{10,9... | collective-permute-start | bytes 1769480 | tf_op jit(solution)/shard_map/ppermute | solution.py:539
  76.2 1.0 copy-start.22
  126.3 7.0 %copy-start.3 = (bf16[2,128,1152]{2,1,0:T(8,128)(2,1)}, bf16[2,128,1152]{2,1,0:T(8,128)(2,1)S(1)}, u32[]{:S(2)}) copy-start(bf16[2,128,1152]{2,1,0:T(8,128)(2,1)S(1)} %collective-permute-done.17.rest_1_) | copy-start | bytes 1769476
  126.4 7.0 %copy-start.4 = (bf16[2,128,1152]{2,1,0:T(8,128)(2,1)}, bf16[2,128,1152]{2,1,0:T(8,128)(2,1)S(1)}, u32[]{:S(2)}) copy-start(bf16[2,128,1152]{2,1,0:T(8,128)(2,1)S(1)} %collective-permute-done.18.rest_2_) | copy-start | bytes 1769476
  126.4 7.0 %copy-start.5 = (bf16[2,128,1152]{2,1,0:T(8,128)(2,1)}, bf16[2,128,1152]{2,1,0:T(8,128)(2,1)S(1)}, u32[]{:S(2)}) copy-start(bf16[2,128,1152]{2,1,0:T(8,128)(2,1)S(1)} %collective-permute-done.19.rest_3_) | copy-start | bytes 1769476
  126.4 4.9 %collective-permute-start.20 = (bf16[4096,256]{1,0:T(8,128)(2,1)}, bf16[4096,256]{1,0:T(8,128)(2,1)S(1)}, u32[]{:S(2)}, u32[]{:S(2)}) collective-permute-start(bf16[4096,256]{1,0:T(8,128)(2,1)} %get-tuple-element.76), channel_id=1, source_target_pairs={{0,4},{4,0},{8,12},{12,8},{16,20},{20,16},{24,28},{28,24},{32,36},... | collective-permute-start | bytes 6291464 | tf_op jit(solution)/shard_map/ppermute | solution.py:551
  183.7 21.1 %copy-start.11 = (bf16[512,256]{1,0:T(8,128)(2,1)}, bf16[512,256]{1,0:T(8,128)(2,1)S(1)}, u32[]{:S(2)}) copy-start(bf16[512,256]{1,0:T(8,128)(2,1)S(1)} %reduce_sum.54.rest_0_) | copy-start | bytes 786436
  183.7 6.3 %collective-permute-start.21 = (bf16[512,256]{1,0:T(8,128)(2,1)S(1)}, bf16[512,256]{1,0:T(8,128)(2,1)S(1)}, u32[]{:S(2)}, u32[]{:S(2)}) collective-permute-start(bf16[512,256]{1,0:T(8,128)(2,1)S(1)} %reduce_sum.54.rest_0_), channel_id=1, source_target_pairs={{0,3},{1,0},{2,1},{3,2},{4,7},{5,4},{6,5},{7,6},{8,11},{9,8},{10,9... | collective-permute-start | bytes 786440 | tf_op jit(solution)/shard_map/ppermute | solution.py:562
  185.5 12.2 %collective-permute-start.22 = (bf16[512,256]{1,0:T(8,128)(2,1)S(1)}, bf16[512,256]{1,0:T(8,128)(2,1)S(1)}, u32[]{:S(2)}, u32[]{:S(2)}) collective-permute-start(bf16[512,256]{1,0:T(8,128)(2,1)S(1)} %reduce_sum.54.rest_0_), channel_id=1, source_target_pairs={{0,2},{1,3},{2,0},{3,1},{4,6},{5,7},{6,4},{7,5},{8,10},{9,11},{10,... | collective-permute-start | bytes 786440 | tf_op jit(solution)/shard_map/ppermute | solution.py:562
  186.7 13.5 %collective-permute-start.23 = (bf16[512,256]{1,0:T(8,128)(2,1)S(1)}, bf16[512,256]{1,0:T(8,128)(2,1)S(1)}, u32[]{:S(2)}, u32[]{:S(2)}) collective-permute-start(bf16[512,256]{1,0:T(8,128)(2,1)S(1)} %reduce_sum.54.rest_0_), channel_id=1, source_target_pairs={{0,1},{1,2},{2,3},{3,0},{4,5},{5,6},{6,7},{7,4},{8,9},{9,10},{10,1... | collective-permute-start | bytes 786440 | tf_op jit(solution)/shard_map/ppermute | solution.py:562
  187.5 17.3 %collective-permute-start.24 = (bf16[512,256]{1,0:T(8,128)(2,1)S(1)}, bf16[512,256]{1,0:T(8,128)(2,1)S(1)}, u32[]{:S(2)}, u32[]{:S(2)}) collective-permute-start(bf16[512,256]{1,0:T(8,128)(2,1)S(1)} %reduce_sum.54.rest_0_), channel_id=1, source_target_pairs={{0,4},{4,0},{8,12},{12,8},{16,20},{20,16},{24,28},{28,24},{32,36},... | collective-permute-start | bytes 786440 | tf_op jit(solution)/shard_map/ppermute | solution.py:563
  190.0 14.8 %copy-start.23 = (bf16[512,256]{1,0:T(8,128)(2,1)}, bf16[512,256]{1,0:T(8,128)(2,1)S(1)}, u32[]{:S(2)}) copy-start(bf16[512,256]{1,0:T(8,128)(2,1)S(1)} %collective-permute-done.21.rest_1_) | copy-start | bytes 786436
  190.0 14.8 %collective-permute-start.25 = (bf16[512,256]{1,0:T(8,128)(2,1)S(1)}, bf16[512,256]{1,0:T(8,128)(2,1)S(1)}, u32[]{:S(2)}, u32[]{:S(2)}) collective-permute-start(bf16[512,256]{1,0:T(8,128)(2,1)S(1)} %collective-permute-done.21.rest_1_), channel_id=1, source_target_pairs={{0,4},{4,0},{8,12},{12,8},{16,20},{20,16},{24,28},{28,24},{32,36},... | collective-permute-start | bytes 786440 | tf_op jit(solution)/shard_map/ppermute | solution.py:563
  197.7 7.1 %copy-start.24 = (bf16[512,256]{1,0:T(8,128)(2,1)}, bf16[512,256]{1,0:T(8,128)(2,1)S(1)}, u32[]{:S(2)}) copy-start(bf16[512,256]{1,0:T(8,128)(2,1)S(1)} %collective-permute-done.22.rest_2_) | copy-start | bytes 786436
  197.7 7.2 %collective-permute-start.26 = (bf16[512,256]{1,0:T(8,128)(2,1)S(1)}, bf16[512,256]{1,0:T(8,128)(2,1)S(1)}, u32[]{:S(2)}, u32[]{:S(2)}) collective-permute-start(bf16[512,256]{1,0:T(8,128)(2,1)S(1)} %collective-permute-done.22.rest_2_), channel_id=1, source_target_pairs={{0,4},{4,0},{8,12},{12,8},{16,20},{20,16},{24,28},{28,24},{32,36},... | collective-permute-start | bytes 786440 | tf_op jit(solution)/shard_map/ppermute | solution.py:563
  200.1 4.7 %copy-start.25 = (bf16[512,256]{1,0:T(8,128)(2,1)}, bf16[512,256]{1,0:T(8,128)(2,1)S(1)}, u32[]{:S(2)}) copy-start(bf16[512,256]{1,0:T(8,128)(2,1)S(1)} %collective-permute-done.23.rest_3_) | copy-start | bytes 786436
  200.1 4.7 %collective-permute-start.27 = (bf16[512,256]{1,0:T(8,128)(2,1)S(1)}, bf16[512,256]{1,0:T(8,128)(2,1)S(1)}, u32[]{:S(2)}, u32[]{:S(2)}) collective-permute-start(bf16[512,256]{1,0:T(8,128)(2,1)S(1)} %collective-permute-done.23.rest_3_), channel_id=1, source_target_pairs={{0,4},{4,0},{8,12},{12,8},{16,20},{20,16},{24,28},{28,24},{32,36},... | collective-permute-start | bytes 786440 | tf_op jit(solution)/shard_map/ppermute | solution.py:563
  204.8 0.8 copy-start.27
  204.8 0.9 copy-start.28
  204.9 1.0 copy-start.29
  213.4 41.4 %all-to-all-start.1 = ((bf16[16,288,256]{2,1,0:T(8,128)(2,1)}), bf16[16,288,256]{2,1,0:T(8,128)(2,1)S(1)}, u32[]{:S(2)}, u32[]{:S(2)}) async-start(bf16[16,288,256]{2,1,0:T(8,128)(2,1)} %proj_parts.1), calls=%async_computation.1 | async-start | bytes 4718592 | tf_op jit(solution)/shard_map/all_to_all | solution.py:567
  217.1 12.1 %collective-permute-start.16 = (bf16[512,384]{1,0:T(8,128)(2,1)}, bf16[512,384]{1,0:T(8,128)(2,1)S(1)}, u32[]{:S(2)}, u32[]{:S(2)}) collective-permute-start(bf16[512,384]{1,0:T(8,128)(2,1)} %get-tuple-element.69), channel_id=1, source_target_pairs={{0,4},{4,0},{8,12},{12,8},{16,20},{20,16},{24,28},{28,24},{32,36},... | collective-permute-start | bytes 1179656 | tf_op jit(solution)/shard_map/ppermute | solution.py:555
  224.0 35.5 %copy-start.8 = (bf16[512,384]{1,0:T(8,128)(2,1)S(1)}, bf16[512,384]{1,0:T(8,128)(2,1)}, u32[]{:S(2)}) copy-start(bf16[512,384]{1,0:T(8,128)(2,1)} %get-tuple-element.68) | copy-start | bytes 1179652
  224.0 8.7 %collective-permute-start.28 = (bf16[128,1152]{1,0:T(8,128)(2,1)}, bf16[128,1152]{1,0:T(8,128)(2,1)S(1)}, u32[]{:S(2)}, u32[]{:S(2)}) collective-permute-start(bf16[128,1152]{1,0:T(8,128)(2,1)} %get-tuple-element.94), channel_id=1, source_target_pairs={{0,1},{1,2},{2,3},{3,0},{4,5},{5,6},{6,7},{7,4},{8,9},{9,10},{10,1... | collective-permute-start | bytes 884744 | tf_op jit(solution)/shard_map/ppermute | solution.py:572
  224.4 19.4 %collective-permute-start.29 = (bf16[128,1152]{1,0:T(8,128)(2,1)}, bf16[128,1152]{1,0:T(8,128)(2,1)S(1)}, u32[]{:S(2)}, u32[]{:S(2)}) collective-permute-start(bf16[128,1152]{1,0:T(8,128)(2,1)} %get-tuple-element.95), channel_id=1, source_target_pairs={{0,2},{1,3},{2,0},{3,1},{4,6},{5,7},{6,4},{7,5},{8,10},{9,11},{10,... | collective-permute-start | bytes 884744 | tf_op jit(solution)/shard_map/ppermute | solution.py:572
  226.2 29.6 %collective-permute-start.30 = (bf16[128,1152]{1,0:T(8,128)(2,1)}, bf16[128,1152]{1,0:T(8,128)(2,1)}, u32[]{:S(2)}, u32[]{:S(2)}) collective-permute-start(bf16[128,1152]{1,0:T(8,128)(2,1)} %get-tuple-element.96), channel_id=1, source_target_pairs={{0,3},{1,0},{2,1},{3,2},{4,7},{5,4},{6,5},{7,6},{8,11},{9,8},{10,9... | collective-permute-start | bytes 884744 | tf_op jit(solution)/shard_map/ppermute | solution.py:572
  227.9 32.7 %collective-permute-start.31 = (bf16[128,1152]{1,0:T(8,128)(2,1)}, bf16[128,1152]{1,0:T(8,128)(2,1)}, u32[]{:S(2)}, u32[]{:S(2)}) collective-permute-start(bf16[128,1152]{1,0:T(8,128)(2,1)} %get-tuple-element.97), channel_id=1, source_target_pairs={{0,4},{1,5},{2,6},{3,7},{4,0},{5,1},{6,2},{7,3},{8,12},{9,13},{10,... | collective-permute-start | bytes 884744 | tf_op jit(solution)/shard_map/ppermute | solution.py:572
  229.2 31.5 %collective-permute-start.32 = (bf16[128,1152]{1,0:T(8,128)(2,1)}, bf16[128,1152]{1,0:T(8,128)(2,1)}, u32[]{:S(2)}, u32[]{:S(2)}) collective-permute-start(bf16[128,1152]{1,0:T(8,128)(2,1)} %get-tuple-element.98), channel_id=1, source_target_pairs={{0,5},{1,6},{2,7},{3,4},{4,1},{5,2},{6,3},{7,0},{8,13},{9,14},{10,... | collective-permute-start | bytes 884744 | tf_op jit(solution)/shard_map/ppermute | solution.py:572
  232.7 27.9 %copy-start.9 = (bf16[128,1152]{1,0:T(8,128)(2,1)}, bf16[128,1152]{1,0:T(8,128)(2,1)S(1)}, u32[]{:S(2)}) copy-start(bf16[128,1152]{1,0:T(8,128)(2,1)S(1)} %collective-permute-done.28.rest_1_) | copy-start | bytes 884740
  232.7 27.9 %collective-permute-start.33 = (bf16[128,1152]{1,0:T(8,128)(2,1)}, bf16[128,1152]{1,0:T(8,128)(2,1)}, u32[]{:S(2)}, u32[]{:S(2)}) collective-permute-start(bf16[128,1152]{1,0:T(8,128)(2,1)} %get-tuple-element.99), channel_id=1, source_target_pairs={{0,6},{1,7},{2,4},{3,5},{4,2},{5,3},{6,0},{7,1},{8,14},{9,15},{10,... | collective-permute-start | bytes 884744 | tf_op jit(solution)/shard_map/ppermute | solution.py:572
  244.4 16.2 %collective-permute-start.34 = (bf16[128,1152]{1,0:T(8,128)(2,1)}, bf16[128,1152]{1,0:T(8,128)(2,1)}, u32[]{:S(2)}, u32[]{:S(2)}) collective-permute-start(bf16[128,1152]{1,0:T(8,128)(2,1)} %get-tuple-element.100), channel_id=1, source_target_pairs={{0,7},{1,4},{2,5},{3,6},{4,3},{5,0},{6,1},{7,2},{8,15},{9,12},{10,... | collective-permute-start | bytes 884744 | tf_op jit(solution)/shard_map/ppermute | solution.py:572
  255.8 13.0 %collective-permute-start.35 = (bf16[288,256]{1,0:T(8,128)(2,1)}, bf16[288,256]{1,0:T(8,128)(2,1)S(1)}, u32[]{:S(2)}, u32[]{:S(2)}) collective-permute-start(bf16[288,256]{1,0:T(8,128)(2,1)} %reduce_sum.55), channel_id=1, source_target_pairs={{0,0},{1,17},{2,34},{3,51},{4,64},{5,81},{6,98},{7,115},{8,1},{9,1... | collective-permute-start | bytes 442376 | tf_op jit(solution)/shard_map/ppermute | solution.py:575
  (3 other events, 2.0 us)

commit v2 on v1

v2 whole, which is shorter than its diff:
```python
import functools

import jax
import jax.numpy as jnp
from jax import lax
from jax.experimental import pallas as pl
from jax.experimental.pallas import tpu as pltpu
from jax.sharding import PartitionSpec as P

HD = 128
HQ = 6
NH = 3
BLK = 256
NX = 4
LOG2E = 1.4426950408889634
NEG = -1e30
SC = HD ** (-0.5)
F32 = jnp.float32
BF = jnp.bfloat16

CORE_PERM = [(i, i ^ 1) for i in range(16)]
ZHI_PERM = [(i, i ^ 8) for i in range(16)]
CHIP_GROUPS = [[2 * i + c for i in range(8)] for c in range(2)]
ALL_CHIP_GROUPS = [[2 * i + c for i in range(16)] for c in range(2)]


def y_perm(by):
    return [(i, (i & 9) | (((((i >> 1) & 3) + by) & 3) << 1)) for i in range(16)]


def x_perm(by):
    return [(i, (i + by) % NX) for i in range(NX)]


def cx_perm(flip, by):
    return [(i, (((i >> 2) ^ flip) << 2) | ((i + by) & 3)) for i in range(64)]


def load_blocks(refs, dst, place_ref, sem, at):
    copies = []
    n = 0
    for ref in refs:
        for row in range(0, ref.shape[0], HD):
            for col in range(0, ref.shape[1], BLK):
                to = pl.ds(pl.multiple_of(place_ref[n] * BLK, BLK), BLK)
                src = ref.at[pl.ds(row, HD), pl.ds(col, BLK)]
                copies.append(pltpu.make_async_copy(src, dst.at[:, to], sem.at[at + n]))
                copies[-1].start()
                n += 1
    return copies


def turn_kernel(core_ref, q_own, q_got, do_own, o_own, do_o_got, qaug, doaug, qT, doT):
    blocks = q_own.shape[0] // BLK
    base = core_ref[0] * (NH * HD)
    lane = lax.broadcasted_iota(jnp.int32, (BLK, HD), 1)
    for b in range(2 * blocks):
        for h in range(NH):
            w = pl.ds(h * BLK, BLK)
            r = pl.ds((b % blocks) * BLK, BLK)
            if b < blocks:
                c = pl.ds(pl.multiple_of(base + h * HD, HD), HD)
                q, do, o = q_own[r, c], do_own[r, c], o_own[r, c]
            else:
                c = pl.ds(h * HD, HD)
                q, do, o = q_got[r, c], do_o_got[0, r, c], do_o_got[1, r, c]
            scaled = q.astype(F32) * (SC * LOG2E)
            hi = scaled.astype(BF)
            qaug[b, w, 0:HD] = hi
            qaug[b, w, HD : 2 * HD] = (scaled - hi.astype(F32)).astype(BF)
            qT[b, :, w] = q.T
            doT[b, :, w] = do.T
            doaug[b, w, 0:HD] = do
            d = -jnp.sum(do.astype(F32) * o.astype(F32), axis=1, keepdims=True)
            d1 = d.astype(BF).astype(F32)
            d2 = (d - d1).astype(BF).astype(F32)
            d3 = d - d1 - d2
            aug = jnp.where(lane == 0, d1, jnp.where(lane == 1, d2, jnp.where(lane == 2, d3, 0.0)))
            doaug[b, w, HD : 2 * HD] = aug.astype(BF)


def causal():
    qry_i = lax.broadcasted_iota(jnp.int32, (NH * BLK, BLK), 0) % BLK
    key_i = lax.broadcasted_iota(jnp.int32, (NH * BLK, BLK), 1)
    return key_i <= qry_i


def over_keys(rank, step):
    def four(j, _):
        step(j * (4 * BLK), 4 * BLK, False)
        return 0

    lax.fori_loop(0, rank // 4, four, 0)
    done = 4 * (rank // 4)

    @pl.when(rank - done >= 2)
    def _():
        step(done * BLK, 2 * BLK, False)

    @pl.when(rank % 2 == 1)
    def _():
        step((rank - 1) * BLK, BLK, False)

    step(rank * BLK, BLK, True)


def stats_kernel(rank_ref, place_ref, qaug_hbm, *rest, n_slots):
    k_refs, lse = rest[:n_slots], rest[n_slots]
    kT, qaug, m_s, l_s, sem = rest[n_slots + 1 :]
    nblk = kT.shape[1] // BLK
    load_q = pltpu.make_async_copy(qaug_hbm, qaug, sem.at[2 * nblk])
    load_q.start()
    copies = load_blocks(k_refs, kT.at[0:HD, :], place_ref, sem, 0)
    copies += load_blocks(k_refs, kT.at[HD : 2 * HD, :], place_ref, sem, nblk)
    load_q.wait()
    for c in copies:
        c.wait()
    allowed = causal()

    def q_loop(b, _):
        def step(at, rows, diag):
            keys = kT[:, pl.ds(pl.multiple_of(at, BLK), rows)]
            s = jnp.dot(qaug[b], keys, preferred_element_type=F32)
            if diag:
                s = jnp.where(allowed, s, NEG)
            parts = [s[:, i : i + HD] for i in range(0, rows, HD)]
            m0 = m_s[...]
            m1 = m0
            for part in parts:
                m1 = jnp.maximum(m1, part)
            total = l_s[...] * jnp.exp2(m0 - m1)
            for part in parts:
                total = total + jnp.exp2(part - m1)
            l_s[...] = total
            m_s[...] = m1

        m_s[...] = jnp.full(m_s.shape, NEG, F32)
        l_s[...] = jnp.zeros(l_s.shape, F32)
        over_keys(rank_ref[b], step)
        m = m_s[...]
        top = jnp.max(m, axis=1, keepdims=True)
        total = jnp.sum(l_s[...] * jnp.exp2(m - top), axis=1, keepdims=True)
        lse[b] = jnp.broadcast_to(top + jnp.log2(total), m.shape)
        return 0

    lax.fori_loop(0, qaug.shape[0], q_loop, 0)


def grads_kernel(rank_ref, place_ref, v_place_ref, out_place_ref, *rest, n_k, n_v):
    sides, k_refs, v_refs = rest[:5], rest[5 : 5 + n_k], rest[5 + n_k : 5 + n_k + n_v]
    rest = rest[5 + n_k + n_v :]
    dq_out, dkv_out = rest[:2], rest[2:4]
    kT, vT, kn, dq, dkvT, dqs, dkvs, lse, qaug, doaug, qT, doT, sem, sem_side, sem_out = rest[4:]
    nq = qaug.shape[0]
    nblk = kT.shape[1] // BLK
    loads = []
    for n, (src, dst) in enumerate(zip(sides, (lse, qaug, doaug, qT, doT))):
        loads.append(pltpu.make_async_copy(src, dst, sem_side.at[n]))
    copies = load_blocks(k_refs, kT.at[0:HD, :], place_ref, sem, 0)
    copies += load_blocks(k_refs, kT.at[HD : 2 * HD, :], place_ref, sem, nblk)
    v_copies = load_blocks(v_refs, vT.at[0:HD, :], v_place_ref, sem, 2 * nblk)
    for c in loads:
        c.start()
    row = lax.broadcasted_iota(jnp.int32, (HD, BLK), 0)
    ones = jnp.where(row < 3, 1.0, 0.0).astype(BF)

    def init(i, _):
        r = pl.ds(pl.multiple_of(i * BLK, BLK), BLK)
        vT[HD : 2 * HD, r] = ones
        dkvT[:, r] = jnp.zeros((2 * HD, BLK), F32)
        return 0

    lax.fori_loop(0, nblk, init, 0)
    for c in copies:
        c.wait()

    def turn(i, _):
        r = pl.ds(pl.multiple_of(i * BLK, BLK), BLK)
        kn[r, :] = kT[0:HD, r].T
        return 0

    lax.fori_loop(0, nblk, turn, 0)
    for c in v_copies + loads:
        c.wait()
    allowed = causal()

    def q_loop(b, _):
        def step(at, rows, diag):
            r = pl.ds(pl.multiple_of(at, BLK), rows)
            total = jnp.concatenate([lse[b]] * (rows // HD), axis=1)
            p = jnp.exp2(jnp.dot(qaug[b], kT[:, r], preferred_element_type=F32) - total)
            if diag:
                p = jnp.where(allowed, p, 0.0)
            dp = jnp.dot(doaug[b], vT[:, r], preferred_element_type=F32)
            p16 = p.astype(BF)
            ds16 = (p * dp).astype(BF)
            dkvT[HD : 2 * HD, r] += jnp.dot(doT[b], p16, preferred_element_type=F32)
            dkvT[0:HD, r] += jnp.dot(qT[b], ds16, preferred_element_type=F32)
            dq[...] += jnp.dot(ds16, kn[r, :], preferred_element_type=F32)

        dq[...] = jnp.zeros(dq.shape, F32)
        over_keys(rank_ref[b], step)
        for h in range(NH):
            dqs[b, :, pl.ds(h * HD, HD)] = (dq[pl.ds(h * BLK, BLK), :] * SC).astype(BF)
        return 0

    lax.fori_loop(0, nq, q_loop, 0)
    stores = []
    for b in range(nq):
        dst = dq_out[b // (nq // 2)].at[pl.ds((b % (nq // 2)) * BLK, BLK), :]
        stores.append(pltpu.make_async_copy(dqs.at[b], dst, sem_out.at[b]))
        stores[-1].start()
    slots = nblk // 4
    for side in (1, 0):
        for i in range(slots):
            for n in range(2):
                at = out_place_ref[side * (nblk // 2) + 2 * i + n]
                c = pl.ds(pl.multiple_of(at * BLK, BLK), BLK)
                m = side * slots + i
                dkvs[m, 0:HD, pl.ds(n * BLK, BLK)] = (dkvT[0:HD, c] * SC).astype(BF)
                dkvs[m, HD : 2 * HD, pl.ds(n * BLK, BLK)] = dkvT[HD : 2 * HD, c].astype(BF)
            stores.append(pltpu.make_async_copy(dkvs.at[m], dkv_out[side].at[i], sem_out.at[nq + m]))
            stores[-1].start()
    for c in stores:
        c.wait()


VM = pl.BlockSpec(memory_space=pltpu.VMEM)
SM = pl.BlockSpec(memory_space=pltpu.SMEM)
HB = pl.BlockSpec(memory_space=pl.ANY)


BIG = 60 * 1024 * 1024


def turned(core, q, q_got, do, o, do_o_got):
    nq = 2 * q.shape[0] // BLK
    W = NH * BLK
    return pl.pallas_call(
        turn_kernel,
        out_shape=(
            jax.ShapeDtypeStruct((nq, W, 2 * HD), BF),
            jax.ShapeDtypeStruct((nq, W, 2 * HD), BF),
            jax.ShapeDtypeStruct((nq, HD, W), BF),
            jax.ShapeDtypeStruct((nq, HD, W), BF),
        ),
        in_specs=[SM] + [VM] * 5,
        out_specs=(VM,) * 4,
        compiler_params=pltpu.CompilerParams(vmem_limit_bytes=BIG),
        name="turned_queries",
    )(core, q, q_got, do, o, do_o_got)


def softmax_stats(rank, place, qaug, k_slots):
    nq, W, _ = qaug.shape
    nblk = place.shape[0]
    keys = nblk * BLK
    n = len(k_slots)
    pairs = 66 * W * BLK
    return pl.pallas_call(
        functools.partial(stats_kernel, n_slots=n),
        out_shape=jax.ShapeDtypeStruct((nq, W, HD), F32),
        in_specs=[SM] * 2 + [HB] * (1 + n),
        out_specs=VM,
        scratch_shapes=[
            pltpu.VMEM((2 * HD, keys), BF),
            pltpu.VMEM((nq, W, 2 * HD), BF),
            pltpu.VMEM((W, HD), F32),
            pltpu.VMEM((W, HD), F32),
            pltpu.SemaphoreType.DMA((2 * nblk + 1,)),
        ],
        compiler_params=pltpu.CompilerParams(vmem_limit_bytes=BIG),
        cost_estimate=pl.CostEstimate(
            flops=16 * pairs * HD, bytes_accessed=4 * 1024 * 1024, transcendentals=pairs
        ),
        name="softmax_stats",
    )(rank, place, qaug, *k_slots)


def attention_grads(rank, places, lse, qaug, doaug, qT, doT, k_slots, v_slots):
    nq, W, _ = qaug.shape
    half = nq * BLK // 2
    nblk = places.shape[1]
    keys = nblk * BLK
    n = len(k_slots)
    pairs = 66 * W * BLK
    return pl.pallas_call(
        functools.partial(grads_kernel, n_k=n, n_v=len(v_slots)),
        out_shape=(
            jax.ShapeDtypeStruct((half, NH * HD), BF),
            jax.ShapeDtypeStruct((half, NH * HD), BF),
            jax.ShapeDtypeStruct((nblk // 4, 2 * HD, 2 * BLK), BF),
            jax.ShapeDtypeStruct((nblk // 4, 2 * HD, 2 * BLK), BF),
        ),
        in_specs=[SM] * 4 + [HB] * (5 + n + len(v_slots)),
        out_specs=(HB,) * 4,
        scratch_shapes=[
            pltpu.VMEM((2 * HD, keys), BF),
            pltpu.VMEM((2 * HD, keys), BF),
            pltpu.VMEM((keys, HD), BF),
            pltpu.VMEM((W, HD), F32),
            pltpu.VMEM((2 * HD, keys), F32),
            pltpu.VMEM((nq, BLK, NH * HD), BF),
            pltpu.VMEM((nblk // 2, 2 * HD, 2 * BLK), BF),
            pltpu.VMEM(lse.shape, F32),
            pltpu.VMEM(qaug.shape, BF),
            pltpu.VMEM(doaug.shape, BF),
            pltpu.VMEM(qT.shape, BF),
            pltpu.VMEM(doT.shape, BF),
            pltpu.SemaphoreType.DMA((3 * nblk,)),
            pltpu.SemaphoreType.DMA((5,)),
            pltpu.SemaphoreType.DMA((nq + nblk // 2,)),
        ],
        compiler_params=pltpu.CompilerParams(vmem_limit_bytes=BIG),
        cost_estimate=pl.CostEstimate(
            flops=32 * pairs * HD, bytes_accessed=16 * 1024 * 1024, transcendentals=pairs
        ),
        name="attention_grads",
    )(rank, *places, lse, qaug, doaug, qT, doT, *k_slots, *v_slots)


def load_grads(here, g_refs, g_all, sem):
    copies = []
    rows = g_refs[0][0].shape[0]
    for cs in range(2):
        for dx in range(NX):
            at = ((here + dx) % NX) * (2 * HD)
            dst = g_all.at[pl.ds(cs * rows, rows), pl.ds(pl.multiple_of(at, 2 * HD), 2 * HD)]
            copies.append(pltpu.make_async_copy(g_refs[cs][dx], dst, sem.at[cs * NX + dx]))
            copies[-1].start()
    return copies


def input_kernel(here_ref, *rest):
    here = here_ref[0]
    g_refs = (rest[0:4], rest[4:8])
    w_refs, outs = rest[8:12], rest[12:20]
    g_all, w_all, result, sem, sem_w = rest[20:]
    copies = load_grads(here, g_refs, g_all, sem)
    for n in range(8):
        at = ((here + n // 2) % NX) * (2 * HD) + (n % 2) * HD
        dst = w_all.at[:, pl.ds(pl.multiple_of(at, HD), HD)]
        copies.append(pltpu.make_async_copy(w_refs[n // 2].at[n % 2], dst, sem_w.at[n]))
        copies[-1].start()
    for c in copies:
        c.wait()
    cols = w_all.shape[0]
    for at in range(0, cols, 2 * HD):
        c = pl.ds(at, min(2 * HD, cols - at))
        block = lax.dot_general(
            g_all[...], w_all[c, :], (((1,), (1,)), ((), ())), preferred_element_type=F32
        ).astype(BF)
        result[:, c] = block
    for n, out in enumerate(outs):
        row = (n // NX) * (NX * HD) + ((here + n) % NX) * HD
        out[...] = result[pl.ds(pl.multiple_of(row, HD), HD), :]


def input_blocks(here, g_slots, w_slots):
    cols = w_slots[0].shape[1]
    return pl.pallas_call(
        input_kernel,
        out_shape=tuple(jax.ShapeDtypeStruct((HD, cols), BF) for _ in range(8)),
        in_specs=[SM] + [HB] * 12,
        out_specs=(VM,) * 8,
        scratch_shapes=[
            pltpu.VMEM((8 * HD, 8 * HD), BF),
            pltpu.VMEM((cols, 8 * HD), BF),
            pltpu.VMEM((8 * HD, cols), BF),
            pltpu.SemaphoreType.DMA((8,)),
            pltpu.SemaphoreType.DMA((8,)),
        ],
        compiler_params=pltpu.CompilerParams(vmem_limit_bytes=BIG),
        cost_estimate=pl.CostEstimate(
            flops=2 * 1024 * 1024 * cols, bytes_accessed=7 * 1024 * 1024, transcendentals=0
        ),
        name="input_blocks",
    )(here, *g_slots[0], *g_slots[1], *w_slots)


def proj_kernel(x_ref, g0, g1, out, x_all, g_all, total, sem_x, sem_g, sem_out):
    rows = g0.shape[0]
    pieces, part = out.shape[0], out.shape[1]
    chunk = x_all.shape[0] // 4
    loads = []
    for n, g in enumerate((g0, g1)):
        loads.append(pltpu.make_async_copy(g, g_all.at[pl.ds(n * rows, rows), :], sem_g.at[n]))
        loads[-1].start()
    x_loads = []
    for j in range(4):
        r = pl.ds(j * chunk, chunk)
        for n in range(8):
            src = x_ref.at[n % NX, n // NX, r, :]
            dst = x_all.at[r, pl.ds(n * HD, HD)]
            x_loads.append(pltpu.make_async_copy(src, dst, sem_x.at[j * 8 + n]))
            x_loads[-1].start()
    for c in loads:
        c.wait()
    stores = []
    for j in range(4):
        for c in x_loads[j * 8 : j * 8 + 8]:
            c.wait()
        halves = [pl.ds(j * chunk + n * (chunk // 2), chunk // 2) for n in range(2)]
        sums = [jnp.dot(x_all[h, :], g_all[...], preferred_element_type=F32) for h in halves]
        for h, part_sum in zip(halves, sums):
            total[h, :] = part_sum.astype(BF)
        for n in range(j * pieces // 4, (j + 1) * pieces // 4):
            src = total.at[pl.ds(n * part, part), :]
            stores.append(pltpu.make_async_copy(src, out.at[n], sem_out.at[n]))
            stores[-1].start()
    for c in stores:
        c.wait()


def proj_parts(x_turned, g0, g1):
    cols = x_turned.shape[2]
    return pl.pallas_call(
        proj_kernel,
        out_shape=jax.ShapeDtypeStruct((16, cols // 16, 2 * HD), BF),
        in_specs=[HB] * 3,
        out_specs=HB,
        scratch_shapes=[
            pltpu.VMEM((cols, 8 * HD), BF),
            pltpu.VMEM((8 * HD, 2 * HD), BF),
            pltpu.VMEM((cols, 2 * HD), BF),
            pltpu.SemaphoreType.DMA((32,)),
            pltpu.SemaphoreType.DMA((2,)),
            pltpu.SemaphoreType.DMA((16,)),
        ],
        compiler_params=pltpu.CompilerParams(vmem_limit_bytes=BIG),
        cost_estimate=pl.CostEstimate(
            flops=2 * 1024 * 256 * cols, bytes_accessed=13 * 1024 * 1024, transcendentals=0
        ),
        name="proj_parts",
    )(x_turned, g0, g1)


def place_kernel(where_ref, *rest):
    core, here = where_ref[0], where_ref[1]
    parts, out = rest[:8], rest[8]
    cols = parts[0].shape[1]
    for cs in range(2):
        for dx in range(NX):
            at = ((core + cs) % 2) * (NX * cols) + ((here - dx + NX) % NX) * cols
            out[:, pl.ds(pl.multiple_of(at, HD), cols)] = parts[cs * NX + dx][...]


def place(where, parts):
    rows, cols = parts[0].shape
    return pl.pallas_call(
        place_kernel,
        out_shape=jax.ShapeDtypeStruct((rows, 8 * cols), BF),
        in_specs=[SM] + [VM] * 8,
        out_specs=VM,
        compiler_params=pltpu.CompilerParams(vmem_limit_bytes=BIG),
        name="place_columns",
    )(where, *parts)


def summed(*terms):
    total = terms[0].astype(F32)
    for term in terms[1:]:
        total = total + term.astype(F32)
    return total


def per_device(
    normed_input,
    queries,
    key_heads,
    value_heads,
    attn_out,
    out_grad,
    key_weight,
    value_weight,
    block_order,
):
    ctx = lax.axis_index("ctx")
    here = lax.axis_index("tensor")
    zh, y, core = ctx >> 3, (ctx >> 1) & 3, ctx & 1
    pp = lax.ppermute
    barrier = lax.optimization_barrier
    q_own, do_own, o_own = queries[0], out_grad[0], attn_out[0]

    half_cols = NH * HD

    def theirs(a):
        return lax.dynamic_slice_in_dim(a, (1 - core) * half_cols, half_cols, axis=1)

    def to_each(a, n):
        return jnp.broadcast_to(a[None], (n,) + a.shape).reshape(n * a.shape[0], a.shape[1])

    def exchange(a, axes, groups=None):
        return lax.all_to_all(a, axes, 0, 0, axis_index_groups=groups, tiled=True)

    q_got = pp(theirs(q_own), "ctx", CORE_PERM)
    k_mine = exchange(to_each(key_heads[0].T, 8), "ctx", CHIP_GROUPS)
    v_all = lax.all_gather(value_heads[0].T, "ctx", axis=0, tiled=True)
    q_got, do_own, o_own, x_own, key_weight, value_weight = barrier(
        (q_got, do_own, o_own, normed_input[0], key_weight, value_weight)
    )
    do_o_got = pp(jnp.stack([theirs(do_own), theirs(o_own)]), "ctx", CORE_PERM)

    blocks = jnp.arange(block_order.shape[0], dtype=jnp.int32)
    owner = blocks >> 1
    k_slot = ((((owner & 1) ^ core) * 8) + (owner >> 1)) * 2 + (blocks & 1)
    v_slot = blocks
    to_slot = k_slot
    slots = jnp.concatenate([k_slot, v_slot, to_slot]).reshape(3, 1, -1)
    places = jnp.sum(jnp.where(slots == blocks[:, None], block_order, 0), axis=2)
    mine = jnp.stack([2 * ctx, 2 * ctx + 1, 2 * (ctx ^ 1), 2 * (ctx ^ 1) + 1])
    rank = jnp.sum(jnp.where(blocks[None, :] == mine[:, None], block_order[None, :], 0), axis=1)
    core1, here1 = core.reshape(1), here.reshape(1)

    cols = normed_input.shape[2] // 8
    x_halves = x_own.T.reshape(16, 2, -1, x_own.shape[0])

    def x_half(c):
        return lax.dynamic_index_in_dim(x_halves, c, 1, keepdims=False).reshape(NX * cols, -1)

    x_chip = jnp.stack([x_half(core), pp(x_half(1 - core), "ctx", CORE_PERM)])
    w_near = []
    for dx in range(NX):
        at = (core * NX + ((here - dx) & 3)) * cols
        w_near.append(
            jnp.stack([lax.dynamic_slice_in_dim(w, at, cols, axis=0) for w in (key_weight, value_weight)])
        )
    w_slots = w_near[:1] + [pp(w_near[d], "tensor", x_perm(-d)) for d in range(1, NX)]
    qaug, doaug, qT, doT = turned(core1, q_own, q_got, do_own, o_own, do_o_got)
    k_mine, qaug, x_chip = barrier((k_mine, qaug, x_chip))
    x_all = lax.all_gather(x_chip, "tensor")
    k_slots = [k_mine, pp(k_mine, "ctx", CORE_PERM)]
    lse = softmax_stats(rank, places[0], qaug, k_slots)
    lse, w_slots = barrier((lse, w_slots))
    v_slots = [v_all]
    dq_keep, dq_send, dkv0, dkv1 = attention_grads(
        rank, places, lse, qaug, doaug, qT, doT, k_slots, v_slots
    )

    chip = summed(dkv0, pp(dkv1, "ctx", CORE_PERM)).astype(BF)
    terms = lax.all_to_all(chip, "ctx", 0, 0, axis_index_groups=CHIP_GROUPS, tiled=True)
    grads = jnp.sum(terms.astype(F32), axis=0).astype(BF).T

    dq_got = pp(dq_send, "ctx", CORE_PERM)
    query_grad = jnp.where(
        core == 0,
        jnp.concatenate([dq_keep, dq_got], axis=1),
        jnp.concatenate([dq_got, dq_keep], axis=1),
    )

    grads, query_grad = barrier((grads, query_grad))
    g_own = [grads] + [pp(grads, "tensor", x_perm(-dx)) for dx in range(1, NX)]
    g_other = pp(grads, "ctx", CORE_PERM)
    pieces = proj_parts(x_all, grads, g_other)
    pieces, g_own = barrier((pieces, g_own))
    g_slots = (g_own, [g_other] + [pp(g, "ctx", CORE_PERM) for g in g_own[1:]])
    pieces = lax.all_to_all(
        pieces, ("dp", "ctx"), 0, 0, axis_index_groups=ALL_CHIP_GROUPS, tiled=True
    )
    outs = input_blocks(here1, g_slots, w_slots)
    got = [
        outs[n] if n == 0 else pp(outs[n], ("ctx", "tensor"), cx_perm(n // NX, n % NX))
        for n in range(8)
    ]
    input_grad = place(jnp.stack([core, here]), got)
    pieces, input_grad = barrier((pieces, input_grad))
    proj = jnp.sum(pieces.astype(F32), axis=0).astype(BF)
    return (query_grad[None], input_grad[None], proj[:, :HD], proj[:, HD:])


def solution(mesh):
    in_specs = (
        P("dp", ("ctx", "tensor"), None),
        P("dp", "ctx", "tensor"),
        P("dp", "ctx", "tensor"),
        P("dp", "ctx", "tensor"),
        P("dp", "ctx", "tensor"),
        P("dp", "ctx", "tensor"),
        P(None, "tensor"),
        P(None, "tensor"),
        P(),
    )
    out_specs = (
        P("dp", "ctx", "tensor"),
        P("dp", ("ctx", "tensor"), None),
        P(("dp", "ctx"), "tensor"),
        P(("dp", "ctx"), "tensor"),
    )
    return jax.shard_map(
        per_device, mesh=mesh, in_specs=in_specs, out_specs=out_specs, check_vma=False
    )
```

time: 273 us -> 250 us (0.916)
  blocking collectives: 49.9 us -> 0 us
  waiting for transfers between devices: 42.3 us -> 69.9 us
  Pallas kernels: 93.1 us -> 71.7 us
  between operations: 1.08 us -> 14.4 us
  starting transfers between devices: 58.3 us -> 66.4 us
  local copies, waits for them, and re-layouts: 10.1 us -> 15.4 us
  other arithmetic: 14.7 us -> 10.4 us
    all_to_all x1 -> x0, blocking collectives: 49.9 us -> none  [per_device(): lax.all_to_all(chip, 'ctx', 0, 0, axis_index_groups=CHIP_GROUPS, tiled=True)]
    all_to_all x0 -> x2, waiting for transfers between devices: none -> 36.8 us  [the longest x1 25.4 us: per_device(): lax.all_to_all(chip, 'ctx', 0, 0, axis_index_groups=CHIP_GROUPS, tiled=True)]
    all_to_all x0 -> x2, starting transfers between devices: none -> 31 us  [the longest x1 23.5 us: per_device(): lax.all_to_all(chip, 'ctx', 0, 0, axis_index_groups=CHIP_GROUPS, tiled=True)]
    ppermute x20 -> x7, starting transfers between devices: 32 us -> 3.5 us  [the longest x3 1.36 us: per_device(): g_slots = (g_own, [g_other] + [pp(g, 'ctx', CORE_PERM) for g in g_own[1:]])]
    pallas_call x4, Pallas kernels: 83.2 us -> 61.8 us  [the longest x1 32 us: attention_grads(): pl.pallas_call(functools.partial(grads_kernel, n_k=n, n_v=len(v_slots)),...]
    ppermute x20 -> x7, waiting for transfers between devices: 23.5 us -> 5.61 us  [the longest x1 4 us: per_device(): chip = summed(dkv0, pp(dkv1, 'ctx', CORE_PERM)).astype(BF)]
    all_to_all x1, waiting for transfers between devices: 10.4 us -> 0.01 us  [per_device(): lax.all_to_all(pieces, ('dp', 'ctx'), 0, 0, axis_index_groups=ALL_CHIP_GR...]
    ppermute x7, waiting for transfers between devices: 3.57 us -> 12.8 us  [per_device(): pp(outs[n], ('ctx', 'tensor'), cx_perm(n // NX, n % NX))]
  transfers between devices with their start and end apart: 37 -> 28, of which waited for: 10 -> 13; matrix products, arithmetic and copies ran while one was open for 6% -> 8% of each run, Pallas kernels for 32% -> 29%
where the time goes in v2:
time: 250 us; the launch traced here: 248 us
  Pallas kernels  71.7 us (29%)
  waiting for transfers between devices  69.9 us (28%)
  starting transfers between devices  66.4 us (27%)
  local copies, waits for them, and re-layouts  15.4 us (6%)
  between operations  14.4 us (6%)
  other arithmetic  10.4 us (4%)
    pallas_call x1, Pallas kernels, attention_grads(): pl.pallas_call(functools.partial(grads_kernel, n_k=n, n_v=len(v_slots)),...  32 us
    all_to_all x1, waiting for transfers between devices, per_device(): lax.all_to_all(chip, 'ctx', 0, 0, axis_index_groups=CHIP_GROUPS, tiled=True)  25.4 us
    all_to_all x1, starting transfers between devices, per_device(): lax.all_to_all(chip, 'ctx', 0, 0, axis_index_groups=CHIP_GROUPS, tiled=True)  23.5 us
    ppermute x7, starting transfers between devices, per_device(): pp(outs[n], ('ctx', 'tensor'), cx_perm(n // NX, n % NX))  16.5 us
    pallas_call x1, Pallas kernels, softmax_stats(): pl.pallas_call(functools.partial(stats_kernel, n_slots=n), out_shape=jax....  16.3 us
    ppermute x7, waiting for transfers between devices, per_device(): pp(outs[n], ('ctx', 'tensor'), cx_perm(n // NX, n % NX))  12.8 us
    all_to_all x1, waiting for transfers between devices, exchange(): return lax.all_to_all(a, axes, 0, 0, axis_index_groups=groups, tiled=True)  11.4 us
    unnamed x50, local copies, waits for them, and re-layouts  9.15 us
  transfers between devices with their start and end apart: 28, of which 13 were waited for; matrix products, arithmetic and copies ran while one was open for 8% of the time, Pallas kernels for 29%

profile of v2, /device:TPU:5, one launch (start us, length us, event | category | flops | bytes accessed | tf_op | source)
XLA Modules:
  0.0 248.1 jit_solution(14346691198145095174)
XLA Ops:
  7.2 1.6 copy.26
  8.9 1.0 dynamic-slice_bitcast_fusion.2
  9.9 0.8 collective-permute-start
  10.7 3.0 %copy.25 = bf16[1,128,9216]{1,2,0:T(8,128)(2,1)S(1)} copy(bf16[1,128,9216]{2,1,0:T(8,128)(2,1)} %param.9) | data formatting | bytes 4718592 | tf_op args[0]
  13.8 0.7 copy-done.6
  14.5 1.2 constant_dynamic-slice_fusion.1
  15.8 0.5 copy-done.1
  16.4 1.0 pad_maximum_fusion.1
  17.5 1.1 broadcast_in_dim.39
  18.6 7.5 %all-to-all-start = ((bf16[8,128,512]{2,1,0:T(8,128)(2,1)}), bf16[8,128,512]{2,1,0:T(8,128)(2,1)S(1)}, u32[]{:S(2)}, u32[]{:S(2)}) async-start(bf16[8,128,512]{2,1,0:T(8,128)(2,1)} %broadcast_in_dim.39), calls=%async_computation | async-start | bytes 2097152 | tf_op jit(solution)/shard_map/all_to_all | solution.py:494
  26.2 5.4 %turned_queries.1 = (bf16[4,768,256]{2,1,0:T(8,128)(2,1)}, bf16[4,768,256]{2,1,0:T(8,128)(2,1)}, bf16[4,128,768]{2,1,0:T(8,128)(2,1)}, bf16[4,128,768]{2,1,0:T(8,128)(2,1)}) custom-call(s32[1]{0:T(128)} %bitcast.11.core_ref, bf16[512,768]{1,0:T(8,128)(2,1)} %bitcast.61, bf16[512,384]{1,0:T(8,128)(2,1)} %copy-done.6, bf16[512,768]{1,0:T(8,128)(2,1)} %bitcast.62, ...), custom_call_target="tpu_custom_call" | custom-call | tf_op jit(solution)/shard_map/turned_queries/pallas_call | solution.py:239
  31.6 1.6 pad_maximum_fusion
  33.2 11.4 %all-to-all-done = bf16[8,128,512]{2,1,0:T(8,128)(2,1)S(1)} async-done(((bf16[8,128,512]{2,1,0:T(8,128)(2,1)}), bf16[8,128,512]{2,1,0:T(8,128)(2,1)S(1)}, u32[]{:S(2)}, u32[]{:S(2)}) %all-to-all-start) | async-done | bytes 1048608 | tf_op jit(solution)/shard_map/all_to_all | solution.py:494
  44.8 0.1 select_reduce_fusion
  44.9 0.7 select_reduce_fusion.1.rank_ref
  45.6 0.5 slice_bitcast_fusion
  46.1 0.7 collective-permute-start.3
  46.8 1.4 dynamic-slice_bitcast_fusion.3
  48.2 0.3 collective-permute-start.4
  48.6 2.5 %collective-permute-start.5 = (bf16[2,1152,128]{2,1,0:T(8,128)(2,1)S(1)}, bf16[2,1152,128]{2,1,0:T(8,128)(2,1)}, u32[]{:S(2)}, u32[]{:S(2)}) collective-permute-start(bf16[2,1152,128]{2,1,0:T(8,128)(2,1)S(1)} %pad_maximum_fusion.4), channel_id=1, source_target_pairs={{0,2},{1,3},{2,0},{3,1},{4,6},{5,7},{6,4},{7,5},{8,10},{9,11},{10,... | collective-permute-start | bytes 1769480 | tf_op jit(solution)/shard_map/ppermute | solution.py:528
  51.2 0.3 collective-permute-start.6
  51.5 0.9 pad_maximum_fusion.2.rest_8_
  52.3 1.0 copy-done.15
  53.3 16.3 %softmax_stats.1.rest_0_ = f32[4,768,128]{2,1,0:T(8,128)} custom-call(s32[4]{0:T(128)} %select_reduce_fusion.1.rank_ref, s32[32]{0:T(128)} %get-tuple-element.96.place_ref, bf16[4,768,256]{2,1,0:T(8,128)(2,1)} %get-tuple-element.48.qaug_hbm.rest_1_, bf16[1024,512]{1,0:T(8,128)(2,1)} %bitcast.74, bf16[1024,512]{1,0:T(8,128)(2,1)} %copy-done.15), custom_call_target="tpu_custom_call" | custom-call | flops 26575110144 | bytes 4194304 | tf_op jit(solution)/shard_map/softmax_stats/pallas_call | solution.py:260
  69.7 8.5 %collective-permute-done.6.rest_11_ = bf16[2,1152,128]{2,1,0:T(8,128)(2,1)} collective-permute-done((bf16[2,1152,128]{2,1,0:T(8,128)(2,1)S(1)}, bf16[2,1152,128]{2,1,0:T(8,128)(2,1)}, u32[]{:S(2)}, u32[]{:S(2)}) %collective-permute-start.6) | collective-permute-done | bytes 589856 | tf_op jit(solution)/shard_map/ppermute | solution.py:528
  78.2 32.0 %attention_grads.1 = (bf16[512,384]{1,0:T(8,128)(2,1)}, bf16[512,384]{1,0:T(8,128)(2,1)}, bf16[8,256,512]{2,1,0:T(8,128)(2,1)}, bf16[8,256,512]{2,1,0:T(8,128)(2,1)}) custom-call(s32[4]{0:T(128)} %select_reduce_fusion.1.rank_ref, s32[32]{0:T(128)} %get-tuple-element.96.place_ref, s32[32]{0:T(128)} %get-tuple-element.95.v_place_ref, ...), custom_call_target="tpu_custom_call" | custom-call | flops 53150220288 | bytes 16777216 | tf_op jit(solution)/shard_map/attention_grads/pallas_call | solution.py:287
  110.2 0.6 collective-permute-start.7
  110.8 4.0 %collective-permute-done.7 = bf16[8,256,512]{2,1,0:T(8,128)(2,1)S(1)} collective-permute-done((bf16[8,256,512]{2,1,0:T(8,128)(2,1)}, bf16[8,256,512]{2,1,0:T(8,128)(2,1)S(1)}, u32[]{:S(2)}, u32[]{:S(2)}) %collective-permute-start.7) | collective-permute-done | bytes 2097184 | tf_op jit(solution)/shard_map/ppermute | solution.py:540
  114.8 3.5 %add_convert_fusion = bf16[8,256,512]{2,1,0:T(8,128)(2,1)} fusion(bf16[8,256,512]{2,1,0:T(8,128)(2,1)S(1)} %collective-permute-done.7, bf16[8,256,512]{2,1,0:T(8,128)(2,1)} %get-tuple-element.56), kind=kLoop, calls=%fused_computation | loop fusion | flops 4194304 | bytes 6291456 | tf_op jit(solution)/shard_map/convert_element_type | solution.py:540
  118.3 23.5 %all-to-all-start.1 = ((bf16[8,256,512]{2,1,0:T(8,128)(2,1)}), bf16[8,256,512]{2,1,0:T(8,128)(2,1)S(1)}, u32[]{:S(2)}, u32[]{:S(2)}) async-start(bf16[8,256,512]{2,1,0:T(8,128)(2,1)} %add_convert_fusion), calls=%async_computation.1 | async-start | bytes 4194304 | tf_op jit(solution)/shard_map/all_to_all | solution.py:541
  141.9 0.7 collective-permute-start.8
  142.6 1.3 collective-permute-done.8
  143.9 1.1 maximum_select_fusion
  145.0 25.4 %all-to-all-done.1 = bf16[8,256,512]{2,1,0:T(8,128)(2,1)S(1)} async-done(((bf16[8,256,512]{2,1,0:T(8,128)(2,1)}), bf16[8,256,512]{2,1,0:T(8,128)(2,1)S(1)}, u32[]{:S(2)}, u32[]{:S(2)}) %all-to-all-start.1) | async-done | bytes 2097184 | tf_op jit(solution)/shard_map/all_to_all | solution.py:541
  170.4 0.4 reduce_sum.44
  170.8 0.1 copy.27
  171.0 0.9 collective-permute-start.9
  171.9 1.6 collective-permute-start.10
  173.5 1.8 collective-permute-start.11
  175.4 0.7 copy-done.12
  176.0 8.1 %proj_parts.1 = bf16[16,288,256]{2,1,0:T(8,128)(2,1)} custom-call(bf16[4,2,4608,128]{3,2,1,0:T(8,128)(2,1)} %bitcast.58, bf16[512,256]{1,0:T(8,128)(2,1)} %bitcast.71, bf16[512,256]{1,0:T(8,128)(2,1)} %copy-done.12), custom_call_target="tpu_custom_call" | custom-call | flops 2415919104 | bytes 13631488 | tf_op jit(solution)/shard_map/proj_parts/pallas_call | solution.py:417
  184.2 4.6 %collective-permute-done.12.rest_3_ = bf16[512,256]{1,0:T(8,128)(2,1)S(1)} collective-permute-done((bf16[512,256]{1,0:T(8,128)(2,1)S(1)}, bf16[512,256]{1,0:T(8,128)(2,1)S(1)}, u32[]{:S(2)}, u32[]{:S(2)}) %collective-permute-start.12) | collective-permute-done | bytes 262176 | tf_op jit(solution)/shard_map/ppermute | solution.py:552
  188.8 0.7 copy-done.20
  189.5 7.2 %all-to-all-start.2 = ((bf16[16,288,256]{2,1,0:T(8,128)(2,1)}), bf16[16,288,256]{2,1,0:T(8,128)(2,1)S(1)}, u32[]{:S(2)}, u32[]{:S(2)}) async-start(bf16[16,288,256]{2,1,0:T(8,128)(2,1)} %proj_parts.1), calls=%async_computation.2 | async-start | bytes 4718592 | tf_op jit(solution)/shard_map/all_to_all | solution.py:557
  196.8 0.9 collective-permute-start.13
  197.7 0.4 collective-permute-start.15
  198.1 0.6 collective-permute-done.13.rest_5_
  198.8 0.4 collective-permute-done.14.rest_6_
  199.2 0.6 collective-permute-done.15.rest_7_
  199.9 0.6 copy-done.23
  200.5 6.7 %input_blocks.1 = (bf16[128,1152]{1,0:T(8,128)(2,1)}, bf16[128,1152]{1,0:T(8,128)(2,1)}, bf16[128,1152]{1,0:T(8,128)(2,1)}, bf16[128,1152]{1,0:T(8,128)(2,1)}, b...) custom-call(s32[1]{0:T(128)} %bitcast.38.here_ref, ...), custom_call_target="tpu_custom_call" | custom-call | flops 2415919104 | bytes 7340032 | tf_op jit(solution)/shard_map/input_blocks/pallas_call | solution.py:361
  207.1 0.5 collective-permute-start.16
  207.6 1.6 collective-permute-start.17
  209.2 2.0 collective-permute-start.18
  211.1 1.2 collective-permute-start.19
  212.3 3.3 %collective-permute-done.16.rest_1_ = bf16[128,1152]{1,0:T(8,128)(2,1)S(1)} collective-permute-done((bf16[128,1152]{1,0:T(8,128)(2,1)}, bf16[128,1152]{1,0:T(8,128)(2,1)S(1)}, u32[]{:S(2)}, u32[]{:S(2)}) %collective-permute-start.16) | collective-permute-done | bytes 294944 | tf_op jit(solution)/shard_map/ppermute | solution.py:562
  215.6 11.3 %collective-permute-start.21 = (bf16[128,1152]{1,0:T(8,128)(2,1)}, bf16[128,1152]{1,0:T(8,128)(2,1)}, u32[]{:S(2)}, u32[]{:S(2)}) collective-permute-start(bf16[128,1152]{1,0:T(8,128)(2,1)} %get-tuple-element.78), channel_id=1, source_target_pairs={{0,6},{1,7},{2,4},{3,5},{4,2},{5,3},{6,0},{7,1},{8,14},{9,15},{10,... | collective-permute-start | bytes 884744 | tf_op jit(solution)/shard_map/ppermute | solution.py:562
  226.9 0.6 pad_add_fusion.1.where_ref
  227.5 1.7 collective-permute-done.20.rest_5_
  229.2 6.4 %collective-permute-done.21.rest_6_ = bf16[128,1152]{1,0:T(8,128)(2,1)} collective-permute-done((bf16[128,1152]{1,0:T(8,128)(2,1)}, bf16[128,1152]{1,0:T(8,128)(2,1)}, u32[]{:S(2)}, u32[]{:S(2)}) %collective-permute-start.21) | collective-permute-done | bytes 294944 | tf_op jit(solution)/shard_map/ppermute | solution.py:562
  235.7 1.4 collective-permute-done.22.rest_7_
  237.1 3.2 %place_columns.1 = bf16[128,9216]{1,0:T(8,128)(2,1)} custom-call(s32[2]{0:T(128)} %pad_add_fusion.1.where_ref, bf16[128,1152]{1,0:T(8,128)(2,1)} %get-tuple-element.72.rest_0_, bf16[128,1152]{1,0:T(8,128)(2,1)} %copy-done.7, bf16[128,1152]{1,0:T(8,128)(2,1)} %copy-done.8, bf16[128,1152]{1,0:T(8,128)(2,1)} %copy-done.9, bf16[128,1152]{1,0:T(8,128)(2,1)} %copy-done.10, ...), custom_call_target="tpu_custom_call" | custom-call | tf_op jit(solution)/shard_map/place_columns/pallas_call | solution.py:450
  240.3 0.3 reduce_sum.45
  240.6 0.7 fusion
  (76 shorter events, 1.1 us)
Async XLA Ops:
  7.2 71.1 %all-gather.4.cloned.1.call-start = ((), (), s32[]{:S(2)}) async-start(), calls=%async_computation.3 | async-start | bytes 2228224 | tf_op jit(solution)/shard_map/all_gather | solution.py:498
  9.9 3.8 %collective-permute-start = (bf16[512,384]{1,0:T(8,128)(2,1)S(1)}, bf16[512,384]{1,0:T(8,128)(2,1)S(1)}, u32[]{:S(2)}, u32[]{:S(2)}) collective-permute-start(bf16[512,384]{1,0:T(8,128)(2,1)S(1)} %dynamic-slice_bitcast_fusion.2), channel_id=1, source_target_pairs={{0,4},{4,0},{8,12},{12,8},{16,20},{20,16},{24,28},{28,24},{32,36},... | collective-permute-start | bytes 1179656 | tf_op jit(solution)/shard_map/ppermute | solution.py:496
  13.7 0.8 copy-start.6
  14.5 1.3 copy-start
  14.5 1.8 copy-start.1
  15.7 1.7 copy-start.13
  15.7 15.9 %collective-permute-start.2 = (bf16[4608,128]{1,0:T(8,128)(2,1)}, bf16[4608,128]{1,0:T(8,128)(2,1)S(1)}, u32[]{:S(2)}, u32[]{:S(2)}) collective-permute-start(bf16[4608,128]{1,0:T(8,128)(2,1)} %bitcast.23), channel_id=1, source_target_pairs={{0,4},{4,0},{8,12},{12,8},{16,20},{20,16},{24,28},{28,24},{32,36},... | collective-permute-start | bytes 3538952 | tf_op jit(solution)/shard_map/ppermute | solution.py:521
  17.4 8.9 %collective-permute-start.1 = (bf16[2,512,384]{2,1,0:T(8,128)(2,1)}, bf16[2,512,384]{2,1,0:T(8,128)(2,1)}, u32[]{:S(2)}, u32[]{:S(2)}) collective-permute-start(bf16[2,512,384]{2,1,0:T(8,128)(2,1)} %pad_maximum_fusion.1), channel_id=1, source_target_pairs={{0,4},{4,0},{8,12},{12,8},{16,20},{20,16},{24,28},{28,24},{32,36},... | collective-permute-start | bytes 2359304 | tf_op jit(solution)/shard_map/ppermute | solution.py:502
  18.6 26.0 %all-to-all-start = ((bf16[8,128,512]{2,1,0:T(8,128)(2,1)}), bf16[8,128,512]{2,1,0:T(8,128)(2,1)S(1)}, u32[]{:S(2)}, u32[]{:S(2)}) async-start(bf16[8,128,512]{2,1,0:T(8,128)(2,1)} %broadcast_in_dim.39), calls=%async_computation | async-start | bytes 2097152 | tf_op jit(solution)/shard_map/all_to_all | solution.py:494
  26.1 149.2 %all-gather.6.cloned.1.call-start = ((), (), s32[]{:S(2)}) async-start(), calls=%async_computation.4 | async-start | bytes 11796480 | tf_op jit(solution)/shard_map/all_gather | solution.py:531
  33.2 11.5 %copy-start.14 = (s32[32]{0:T(128)S(1)}, s32[32]{0:T(128)}, u32[]{:S(2)}) copy-start(s32[32]{0:T(128)} %param.17) | copy-start | bytes 388
  33.2 13.6 %copy-start.4 = (bf16[9216,128]{1,0:T(8,128)(2,1)S(1)}, bf16[9216,128]{1,0:T(8,128)(2,1)}, u32[]{:S(2)}) copy-start(bf16[9216,128]{1,0:T(8,128)(2,1)} %param.16) | copy-start | bytes 7077892
  44.6 3.6 %copy-start.3 = (bf16[8,128,512]{2,1,0:T(8,128)(2,1)}, bf16[8,128,512]{2,1,0:T(8,128)(2,1)S(1)}, u32[]{:S(2)}) copy-start(bf16[8,128,512]{2,1,0:T(8,128)(2,1)S(1)} %all-to-all-done) | copy-start | bytes 3145732
  46.1 6.2 %collective-permute-start.3 = (bf16[1024,512]{1,0:T(8,128)(2,1)S(1)}, bf16[1024,512]{1,0:T(8,128)(2,1)S(1)}, u32[]{:S(2)}, u32[]{:S(2)}) collective-permute-start(bf16[1024,512]{1,0:T(8,128)(2,1)S(1)} %bitcast.73), channel_id=1, source_target_pairs={{0,4},{4,0},{8,12},{12,8},{16,20},{20,16},{24,28},{28,24},{32,36},... | collective-permute-start | bytes 3145736 | tf_op jit(solution)/shard_map/ppermute | solution.py:532
  48.2 21.4 %collective-permute-start.4 = (bf16[2,1152,128]{2,1,0:T(8,128)(2,1)S(1)}, bf16[2,1152,128]{2,1,0:T(8,128)(2,1)S(1)}, u32[]{:S(2)}, u32[]{:S(2)}) collective-permute-start(bf16[2,1152,128]{2,1,0:T(8,128)(2,1)S(1)} %pad_maximum_fusion.3), channel_id=1, source_target_pairs={{0,3},{1,0},{2,1},{3,2},{4,7},{5,4},{6,5},{7,6},{8,11},{9,8},{10,9... | collective-permute-start | bytes 1769480 | tf_op jit(solution)/shard_map/ppermute | solution.py:528
  48.6 21.0 %collective-permute-start.5 = (bf16[2,1152,128]{2,1,0:T(8,128)(2,1)S(1)}, bf16[2,1152,128]{2,1,0:T(8,128)(2,1)}, u32[]{:S(2)}, u32[]{:S(2)}) collective-permute-start(bf16[2,1152,128]{2,1,0:T(8,128)(2,1)S(1)} %pad_maximum_fusion.4), channel_id=1, source_target_pairs={{0,2},{1,3},{2,0},{3,1},{4,6},{5,7},{6,4},{7,5},{8,10},{9,11},{10,... | collective-permute-start | bytes 1769480 | tf_op jit(solution)/shard_map/ppermute | solution.py:528
  51.2 27.0 %collective-permute-start.6 = (bf16[2,1152,128]{2,1,0:T(8,128)(2,1)S(1)}, bf16[2,1152,128]{2,1,0:T(8,128)(2,1)}, u32[]{:S(2)}, u32[]{:S(2)}) collective-permute-start(bf16[2,1152,128]{2,1,0:T(8,128)(2,1)S(1)} %pad_maximum_fusion.5), channel_id=1, source_target_pairs={{0,1},{1,2},{2,3},{3,0},{4,5},{5,6},{6,7},{7,4},{8,9},{9,10},{10,1... | collective-permute-start | bytes 1769480 | tf_op jit(solution)/shard_map/ppermute | solution.py:528
  52.3 1.0 copy-start.15
  69.7 40.6 %copy-start.16 = (bf16[2,1152,128]{2,1,0:T(8,128)(2,1)}, bf16[2,1152,128]{2,1,0:T(8,128)(2,1)S(1)}, u32[]{:S(2)}) copy-start(bf16[2,1152,128]{2,1,0:T(8,128)(2,1)S(1)} %collective-permute-done.4.rest_9_) | copy-start | bytes 1769476
  110.2 4.6 %collective-permute-start.7 = (bf16[8,256,512]{2,1,0:T(8,128)(2,1)}, bf16[8,256,512]{2,1,0:T(8,128)(2,1)S(1)}, u32[]{:S(2)}, u32[]{:S(2)}) collective-permute-start(bf16[8,256,512]{2,1,0:T(8,128)(2,1)} %get-tuple-element.57), channel_id=1, source_target_pairs={{0,4},{4,0},{8,12},{12,8},{16,20},{20,16},{24,28},{28,24},{32,36},... | collective-permute-start | bytes 6291464 | tf_op jit(solution)/shard_map/ppermute | solution.py:540
  118.3 23.5 %copy-start.17 = (bf16[512,384]{1,0:T(8,128)(2,1)S(1)}, bf16[512,384]{1,0:T(8,128)(2,1)}, u32[]{:S(2)}) copy-start(bf16[512,384]{1,0:T(8,128)(2,1)} %get-tuple-element.59) | copy-start | bytes 1179652
  118.3 25.6 %copy-start.5 = (bf16[512,384]{1,0:T(8,128)(2,1)S(1)}, bf16[512,384]{1,0:T(8,128)(2,1)}, u32[]{:S(2)}) copy-start(bf16[512,384]{1,0:T(8,128)(2,1)} %get-tuple-element.58) | copy-start | bytes 1179652
  118.3 52.1 %all-to-all-start.1 = ((bf16[8,256,512]{2,1,0:T(8,128)(2,1)}), bf16[8,256,512]{2,1,0:T(8,128)(2,1)S(1)}, u32[]{:S(2)}, u32[]{:S(2)}) async-start(bf16[8,256,512]{2,1,0:T(8,128)(2,1)} %add_convert_fusion), calls=%async_computation.1 | async-start | bytes 4194304 | tf_op jit(solution)/shard_map/all_to_all | solution.py:541
  141.9 2.1 collective-permute-start.8
  171.0 4.4 %copy-start.2 = (bf16[256,512]{0,1:T(8,128)(2,1)}, bf16[256,512]{0,1:T(8,128)(2,1)S(1)}, u32[]{:S(2)}) copy-start(bf16[256,512]{0,1:T(8,128)(2,1)S(1)} %copy.27) | copy-start | bytes 786436
  171.0 4.3 %collective-permute-start.9 = (bf16[512,256]{1,0:T(8,128)(2,1)S(1)}, bf16[512,256]{1,0:T(8,128)(2,1)S(1)}, u32[]{:S(2)}, u32[]{:S(2)}) collective-permute-start(bf16[512,256]{1,0:T(8,128)(2,1)S(1)} %bitcast.67), channel_id=1, source_target_pairs={{0,4},{4,0},{8,12},{12,8},{16,20},{20,16},{24,28},{28,24},{32,36},... | collective-permute-start | bytes 786440 | tf_op jit(solution)/shard_map/ppermute | solution.py:553
  171.9 12.3 %collective-permute-start.10 = (bf16[512,256]{1,0:T(8,128)(2,1)S(1)}, bf16[512,256]{1,0:T(8,128)(2,1)S(1)}, u32[]{:S(2)}, u32[]{:S(2)}) collective-permute-start(bf16[512,256]{1,0:T(8,128)(2,1)S(1)} %bitcast.68), channel_id=1, source_target_pairs={{0,3},{1,0},{2,1},{3,2},{4,7},{5,4},{6,5},{7,6},{8,11},{9,8},{10,9... | collective-permute-start | bytes 786440 | tf_op jit(solution)/shard_map/ppermute | solution.py:552
  173.5 10.7 %collective-permute-start.11 = (bf16[512,256]{1,0:T(8,128)(2,1)S(1)}, bf16[512,256]{1,0:T(8,128)(2,1)S(1)}, u32[]{:S(2)}, u32[]{:S(2)}) collective-permute-start(bf16[512,256]{1,0:T(8,128)(2,1)S(1)} %bitcast.69), channel_id=1, source_target_pairs={{0,2},{1,3},{2,0},{3,1},{4,6},{5,7},{6,4},{7,5},{8,10},{9,11},{10,... | collective-permute-start | bytes 786440 | tf_op jit(solution)/shard_map/ppermute | solution.py:552
  175.3 13.5 %collective-permute-start.12 = (bf16[512,256]{1,0:T(8,128)(2,1)S(1)}, bf16[512,256]{1,0:T(8,128)(2,1)S(1)}, u32[]{:S(2)}, u32[]{:S(2)}) collective-permute-start(bf16[512,256]{1,0:T(8,128)(2,1)S(1)} %bitcast.70), channel_id=1, source_target_pairs={{0,1},{1,2},{2,3},{3,0},{4,5},{5,6},{6,7},{7,4},{8,9},{9,10},{10,1... | collective-permute-start | bytes 786440 | tf_op jit(solution)/shard_map/ppermute | solution.py:552
  175.3 0.7 copy-start.12
  184.2 12.6 %copy-start.18 = (bf16[512,256]{1,0:T(8,128)(2,1)}, bf16[512,256]{1,0:T(8,128)(2,1)S(1)}, u32[]{:S(2)}) copy-start(bf16[512,256]{1,0:T(8,128)(2,1)S(1)} %collective-permute-done.10.rest_1_) | copy-start | bytes 786436
  184.2 13.4 %copy-start.19 = (bf16[512,256]{1,0:T(8,128)(2,1)}, bf16[512,256]{1,0:T(8,128)(2,1)S(1)}, u32[]{:S(2)}) copy-start(bf16[512,256]{1,0:T(8,128)(2,1)S(1)} %collective-permute-done.11.rest_2_) | copy-start | bytes 786436
  188.8 0.7 copy-start.20
  189.5 50.8 %all-to-all-start.2 = ((bf16[16,288,256]{2,1,0:T(8,128)(2,1)}), bf16[16,288,256]{2,1,0:T(8,128)(2,1)S(1)}, u32[]{:S(2)}, u32[]{:S(2)}) async-start(bf16[16,288,256]{2,1,0:T(8,128)(2,1)} %proj_parts.1), calls=%async_computation.2 | async-start | bytes 4718592 | tf_op jit(solution)/shard_map/all_to_all | solution.py:557
  196.8 2.0 collective-permute-start.13
  197.6 1.5 collective-permute-start.14
  197.7 2.0 collective-permute-start.15
  198.8 1.0 copy-start.21
  199.2 0.7 copy-start.22
  199.8 0.7 copy-start.23
  207.1 8.5 %collective-permute-start.16 = (bf16[128,1152]{1,0:T(8,128)(2,1)}, bf16[128,1152]{1,0:T(8,128)(2,1)S(1)}, u32[]{:S(2)}, u32[]{:S(2)}) collective-permute-start(bf16[128,1152]{1,0:T(8,128)(2,1)} %get-tuple-element.73), channel_id=1, source_target_pairs={{0,1},{1,2},{2,3},{3,0},{4,5},{5,6},{6,7},{7,4},{8,9},{9,10},{10,1... | collective-permute-start | bytes 884744 | tf_op jit(solution)/shard_map/ppermute | solution.py:562
  207.6 19.3 %collective-permute-start.17 = (bf16[128,1152]{1,0:T(8,128)(2,1)}, bf16[128,1152]{1,0:T(8,128)(2,1)S(1)}, u32[]{:S(2)}, u32[]{:S(2)}) collective-permute-start(bf16[128,1152]{1,0:T(8,128)(2,1)} %get-tuple-element.74), channel_id=1, source_target_pairs={{0,2},{1,3},{2,0},{3,1},{4,6},{5,7},{6,4},{7,5},{8,10},{9,11},{10,... | collective-permute-start | bytes 884744 | tf_op jit(solution)/shard_map/ppermute | solution.py:562
  209.2 18.4 %collective-permute-start.18 = (bf16[128,1152]{1,0:T(8,128)(2,1)}, bf16[128,1152]{1,0:T(8,128)(2,1)S(1)}, u32[]{:S(2)}, u32[]{:S(2)}) collective-permute-start(bf16[128,1152]{1,0:T(8,128)(2,1)} %get-tuple-element.75), channel_id=1, source_target_pairs={{0,3},{1,0},{2,1},{3,2},{4,7},{5,4},{6,5},{7,6},{8,11},{9,8},{10,9... | collective-permute-start | bytes 884744 | tf_op jit(solution)/shard_map/ppermute | solution.py:562
  211.1 16.4 %collective-permute-start.19 = (bf16[128,1152]{1,0:T(8,128)(2,1)}, bf16[128,1152]{1,0:T(8,128)(2,1)S(1)}, u32[]{:S(2)}, u32[]{:S(2)}) collective-permute-start(bf16[128,1152]{1,0:T(8,128)(2,1)} %get-tuple-element.76), channel_id=1, source_target_pairs={{0,4},{1,5},{2,6},{3,7},{4,0},{5,1},{6,2},{7,3},{8,12},{9,13},{10,... | collective-permute-start | bytes 884744 | tf_op jit(solution)/shard_map/ppermute | solution.py:562
  212.3 16.9 %collective-permute-start.20 = (bf16[128,1152]{1,0:T(8,128)(2,1)}, bf16[128,1152]{1,0:T(8,128)(2,1)S(1)}, u32[]{:S(2)}, u32[]{:S(2)}) collective-permute-start(bf16[128,1152]{1,0:T(8,128)(2,1)} %get-tuple-element.77), channel_id=1, source_target_pairs={{0,5},{1,6},{2,7},{3,4},{4,1},{5,2},{6,3},{7,0},{8,13},{9,14},{10,... | collective-permute-start | bytes 884744 | tf_op jit(solution)/shard_map/ppermute | solution.py:562
  215.6 21.4 %copy-start.7 = (bf16[128,1152]{1,0:T(8,128)(2,1)}, bf16[128,1152]{1,0:T(8,128)(2,1)S(1)}, u32[]{:S(2)}) copy-start(bf16[128,1152]{1,0:T(8,128)(2,1)S(1)} %collective-permute-done.16.rest_1_) | copy-start | bytes 884740
  215.6 20.0 %collective-permute-start.21 = (bf16[128,1152]{1,0:T(8,128)(2,1)}, bf16[128,1152]{1,0:T(8,128)(2,1)}, u32[]{:S(2)}, u32[]{:S(2)}) collective-permute-start(bf16[128,1152]{1,0:T(8,128)(2,1)} %get-tuple-element.78), channel_id=1, source_target_pairs={{0,6},{1,7},{2,4},{3,5},{4,2},{5,3},{6,0},{7,1},{8,14},{9,15},{10,... | collective-permute-start | bytes 884744 | tf_op jit(solution)/shard_map/ppermute | solution.py:562
  226.9 10.1 %copy-start.8 = (bf16[128,1152]{1,0:T(8,128)(2,1)}, bf16[128,1152]{1,0:T(8,128)(2,1)S(1)}, u32[]{:S(2)}) copy-start(bf16[128,1152]{1,0:T(8,128)(2,1)S(1)} %collective-permute-done.17.rest_2_) | copy-start | bytes 884740
  226.9 10.1 %collective-permute-start.22 = (bf16[128,1152]{1,0:T(8,128)(2,1)}, bf16[128,1152]{1,0:T(8,128)(2,1)}, u32[]{:S(2)}, u32[]{:S(2)}) collective-permute-start(bf16[128,1152]{1,0:T(8,128)(2,1)} %get-tuple-element.79), channel_id=1, source_target_pairs={{0,7},{1,4},{2,5},{3,6},{4,3},{5,0},{6,1},{7,2},{8,15},{9,12},{10,... | collective-permute-start | bytes 884744 | tf_op jit(solution)/shard_map/ppermute | solution.py:562
  227.5 9.5 %copy-start.9 = (bf16[128,1152]{1,0:T(8,128)(2,1)}, bf16[128,1152]{1,0:T(8,128)(2,1)S(1)}, u32[]{:S(2)}) copy-start(bf16[128,1152]{1,0:T(8,128)(2,1)S(1)} %collective-permute-done.18.rest_3_) | copy-start | bytes 884740
  227.5 9.5 %copy-start.10 = (bf16[128,1152]{1,0:T(8,128)(2,1)}, bf16[128,1152]{1,0:T(8,128)(2,1)S(1)}, u32[]{:S(2)}) copy-start(bf16[128,1152]{1,0:T(8,128)(2,1)S(1)} %collective-permute-done.19.rest_4_) | copy-start | bytes 884740
  229.2 7.8 %copy-start.11 = (bf16[128,1152]{1,0:T(8,128)(2,1)}, bf16[128,1152]{1,0:T(8,128)(2,1)S(1)}, u32[]{:S(2)}) copy-start(bf16[128,1152]{1,0:T(8,128)(2,1)S(1)} %collective-permute-done.20.rest_5_) | copy-start | bytes 884740
Sparse Core Ops, SparseCore 0:
  10.4 57.2 all-gather.3
  70.0 89.9 all-gather.5

commit v3 on v2

--- a/solution.py
+++ b/solution.py
@@ -493,9 +493,10 @@
     def exchange(a, axes, groups=None):
         return lax.all_to_all(a, axes, 0, 0, axis_index_groups=groups, tiled=True)
 
-    q_got = pp(theirs(q_own), "ctx", CORE_PERM)
-    k_mine = exchange(to_each(key_heads[0].T, 8), "ctx", CHIP_GROUPS)
-    v_all = lax.all_gather(value_heads[0].T, "ctx", axis=0, tiled=True)
+    k_out, q_first, v_own = barrier((to_each(key_heads[0].T, 8), q_own, value_heads[0]))
+    q_got = pp(theirs(q_first), "ctx", CORE_PERM)
+    k_mine = exchange(k_out, "ctx", CHIP_GROUPS)
+    v_all = lax.all_gather(v_own.T, "ctx", axis=0, tiled=True)
     q_got, do_own, o_own, x_own, key_weight, value_weight = barrier(
         (q_got, do_own, o_own, normed_input[0], key_weight, value_weight)
     )

time: 250 us -> 260 us (1.040); the launches traced: 248 us -> 261 us
  Pallas kernels: 71.7 us -> 91.5 us
  waiting for transfers between devices: 69.9 us -> 63.8 us
    pallas_call x1, Pallas kernels: 32 us -> 45.5 us  [attention_grads(): pl.pallas_call(functools.partial(grads_kernel, n_k=n, n_v=len(v_slots)),...]
    pallas_call x1, Pallas kernels: 16.3 us -> 22.6 us  [softmax_stats(): pl.pallas_call(functools.partial(stats_kernel, n_slots=n), out_shape=jax....]
    ppermute x3, waiting for transfers between devices: 8.55 us -> 2.24 us  [per_device(): pp(w_near[d], 'tensor', x_perm(-d))]
  transfers between devices with their start and end apart: 28 -> 28, of which waited for: 13 -> 13; matrix products, arithmetic and copies ran while one was open for 8% -> 6% of each run, Pallas kernels for 29% -> 35%
where the time goes in v3:
time: 260 us; the launch traced here: 261 us
  Pallas kernels  91.5 us (35%)
  starting transfers between devices  66 us (25%)
  waiting for transfers between devices  63.8 us (25%)
  local copies, waits for them, and re-layouts  15.4 us (6%)
  between operations  14.4 us (6%)
  other arithmetic  10.4 us (4%)
    pallas_call x1, Pallas kernels, attention_grads(): pl.pallas_call(functools.partial(grads_kernel, n_k=n, n_v=len(v_slots)),...  45.5 us
    all_to_all x1, waiting for transfers between devices, per_device(): lax.all_to_all(chip, 'ctx', 0, 0, axis_index_groups=CHIP_GROUPS, tiled=True)  25.4 us
    all_to_all x1, starting transfers between devices, per_device(): lax.all_to_all(chip, 'ctx', 0, 0, axis_index_groups=CHIP_GROUPS, tiled=True)  23.3 us
    pallas_call x1, Pallas kernels, softmax_stats(): pl.pallas_call(functools.partial(stats_kernel, n_slots=n), out_shape=jax....  22.6 us
    ppermute x7, starting transfers between devices, per_device(): pp(outs[n], ('ctx', 'tensor'), cx_perm(n // NX, n % NX))  16.7 us
    ppermute x7, waiting for transfers between devices, per_device(): pp(outs[n], ('ctx', 'tensor'), cx_perm(n // NX, n % NX))  12.6 us
    all_to_all x1, waiting for transfers between devices, exchange(): return lax.all_to_all(a, axes, 0, 0, axis_index_groups=groups, tiled=True)  11.9 us
    unnamed x50, local copies, waits for them, and re-layouts  9.15 us
  transfers between devices with their start and end apart: 28, of which 13 were waited for; matrix products, arithmetic and copies ran while one was open for 6% of the time, Pallas kernels for 35%

profile of v3, /device:TPU:5, one launch (start us, length us, event | category | flops | bytes accessed | tf_op | source)
XLA Modules:
  0.0 261.5 jit_solution(8148253588204876161)
XLA Ops:
  7.2 1.1 copy.24
  8.3 1.6 copy.25
  9.9 1.1 broadcast_in_dim.39
  11.2 0.8 collective-permute-start
  11.9 3.0 %copy.26 = bf16[1,128,9216]{1,2,0:T(8,128)(2,1)S(1)} copy(bf16[1,128,9216]{2,1,0:T(8,128)(2,1)} %param.9) | data formatting | bytes 4718592 | tf_op args[0]
  15.0 0.7 copy-done.7
  15.8 1.2 constant_dynamic-slice_fusion.1
  17.0 0.5 copy-done.2
  17.6 1.0 pad_maximum_fusion.1
  18.6 7.5 %all-to-all-start = ((bf16[8,128,512]{2,1,0:T(8,128)(2,1)}), bf16[8,128,512]{2,1,0:T(8,128)(2,1)S(1)}, u32[]{:S(2)}, u32[]{:S(2)}) async-start(bf16[8,128,512]{2,1,0:T(8,128)(2,1)} %bitcast.13), calls=%async_computation | async-start | bytes 2097152 | tf_op jit(solution)/shard_map/all_to_all | solution.py:494
  26.2 5.4 %turned_queries.1 = (bf16[4,768,256]{2,1,0:T(8,128)(2,1)}, bf16[4,768,256]{2,1,0:T(8,128)(2,1)}, bf16[4,128,768]{2,1,0:T(8,128)(2,1)}, bf16[4,128,768]{2,1,0:T(8,128)(2,1)}) custom-call(s32[1]{0:T(128)} %bitcast.15.core_ref, bf16[512,768]{1,0:T(8,128)(2,1)} %bitcast.60, bf16[512,384]{1,0:T(8,128)(2,1)} %copy-done.7, bf16[512,768]{1,0:T(8,128)(2,1)} %bitcast.62, ...), custom_call_target="tpu_custom_call" | custom-call | tf_op jit(solution)/shard_map/turned_queries/pallas_call | solution.py:239
  31.6 1.6 pad_maximum_fusion
  33.2 11.9 %all-to-all-done = bf16[8,128,512]{2,1,0:T(8,128)(2,1)S(1)} async-done(((bf16[8,128,512]{2,1,0:T(8,128)(2,1)}), bf16[8,128,512]{2,1,0:T(8,128)(2,1)S(1)}, u32[]{:S(2)}, u32[]{:S(2)}) %all-to-all-start) | async-done | bytes 1048608 | tf_op jit(solution)/shard_map/all_to_all | solution.py:494
  45.2 0.1 select_reduce_fusion
  45.4 0.7 select_reduce_fusion.1.rank_ref
  46.1 0.5 slice_bitcast_fusion
  46.6 0.5 collective-permute-start.3
  47.1 1.4 dynamic-slice_bitcast_fusion.2
  48.6 0.3 collective-permute-start.4
  49.0 2.5 collective-permute-start.5
  51.5 0.3 collective-permute-start.6
  51.8 0.9 pad_maximum_fusion.2.rest_8_
  52.7 1.0 copy-done.15
  53.6 22.6 %softmax_stats.1.rest_0_ = f32[4,768,128]{2,1,0:T(8,128)} custom-call(s32[4]{0:T(128)} %select_reduce_fusion.1.rank_ref, s32[32]{0:T(128)} %get-tuple-element.102.place_ref, bf16[4,768,256]{2,1,0:T(8,128)(2,1)} %get-tuple-element.53.qaug_hbm.rest_1_, bf16[1024,512]{1,0:T(8,128)(2,1)} %bitcast.74, bf16[1024,512]{1,0:T(8,128)(2,1)} %copy-done.15), custom_call_target="tpu_custom_call" | custom-call | flops 26575110144 | bytes 4194304 | tf_op jit(solution)/shard_map/softmax_stats/pallas_call | solution.py:260
  76.3 2.2 collective-permute-done.6.rest_11_
  78.5 45.5 %attention_grads.1 = (bf16[512,384]{1,0:T(8,128)(2,1)}, bf16[512,384]{1,0:T(8,128)(2,1)}, bf16[8,256,512]{2,1,0:T(8,128)(2,1)}, bf16[8,256,512]{2,1,0:T(8,128)(2,1)}) custom-call(s32[4]{0:T(128)} %select_reduce_fusion.1.rank_ref, s32[32]{0:T(128)} %get-tuple-element.102.place_ref, s32[32]{0:T(128)} %get-tuple-element.101.v_place_ref, ...), custom_call_target="tpu_custom_call" | custom-call | flops 53150220288 | bytes 16777216 | tf_op jit(solution)/shard_map/attention_grads/pallas_call | solution.py:287
  124.1 0.5 collective-permute-start.7
  124.6 4.0 %collective-permute-done.7 = bf16[8,256,512]{2,1,0:T(8,128)(2,1)S(1)} collective-permute-done((bf16[8,256,512]{2,1,0:T(8,128)(2,1)}, bf16[8,256,512]{2,1,0:T(8,128)(2,1)S(1)}, u32[]{:S(2)}, u32[]{:S(2)}) %collective-permute-start.7) | collective-permute-done | bytes 2097184 | tf_op jit(solution)/shard_map/ppermute | solution.py:541
  128.6 3.5 %add_convert_fusion = bf16[8,256,512]{2,1,0:T(8,128)(2,1)} fusion(bf16[8,256,512]{2,1,0:T(8,128)(2,1)S(1)} %collective-permute-done.7, bf16[8,256,512]{2,1,0:T(8,128)(2,1)} %get-tuple-element.62), kind=kLoop, calls=%fused_computation | loop fusion | flops 4194304 | bytes 6291456 | tf_op jit(solution)/shard_map/convert_element_type | solution.py:541
  132.1 23.3 %all-to-all-start.1 = ((bf16[8,256,512]{2,1,0:T(8,128)(2,1)}), bf16[8,256,512]{2,1,0:T(8,128)(2,1)S(1)}, u32[]{:S(2)}, u32[]{:S(2)}) async-start(bf16[8,256,512]{2,1,0:T(8,128)(2,1)} %add_convert_fusion), calls=%async_computation.1 | async-start | bytes 4194304 | tf_op jit(solution)/shard_map/all_to_all | solution.py:542
  155.4 0.7 collective-permute-start.8
  156.2 1.3 collective-permute-done.8
  157.5 1.1 maximum_select_fusion
  158.6 25.4 %all-to-all-done.1 = bf16[8,256,512]{2,1,0:T(8,128)(2,1)S(1)} async-done(((bf16[8,256,512]{2,1,0:T(8,128)(2,1)}), bf16[8,256,512]{2,1,0:T(8,128)(2,1)S(1)}, u32[]{:S(2)}, u32[]{:S(2)}) %all-to-all-start.1) | async-done | bytes 2097184 | tf_op jit(solution)/shard_map/all_to_all | solution.py:542
  184.0 0.4 reduce_sum.44
  184.4 0.1 copy.27
  184.6 0.9 collective-permute-start.9
  185.4 1.4 collective-permute-start.10
  186.8 1.9 collective-permute-start.11
  188.8 0.7 copy-done.13
  189.5 8.1 %proj_parts.1 = bf16[16,288,256]{2,1,0:T(8,128)(2,1)} custom-call(bf16[4,2,4608,128]{3,2,1,0:T(8,128)(2,1)} %bitcast.57, bf16[512,256]{1,0:T(8,128)(2,1)} %bitcast.71, bf16[512,256]{1,0:T(8,128)(2,1)} %copy-done.13), custom_call_target="tpu_custom_call" | custom-call | flops 2415919104 | bytes 13631488 | tf_op jit(solution)/shard_map/proj_parts/pallas_call | solution.py:417
  197.7 4.5 %collective-permute-done.12.rest_3_ = bf16[512,256]{1,0:T(8,128)(2,1)S(1)} collective-permute-done((bf16[512,256]{1,0:T(8,128)(2,1)S(1)}, bf16[512,256]{1,0:T(8,128)(2,1)S(1)}, u32[]{:S(2)}, u32[]{:S(2)}) %collective-permute-start.12) | collective-permute-done | bytes 262176 | tf_op jit(solution)/shard_map/ppermute | solution.py:553
  202.2 0.7 copy-done.20
  202.9 7.2 %all-to-all-start.2 = ((bf16[16,288,256]{2,1,0:T(8,128)(2,1)}), bf16[16,288,256]{2,1,0:T(8,128)(2,1)S(1)}, u32[]{:S(2)}, u32[]{:S(2)}) async-start(bf16[16,288,256]{2,1,0:T(8,128)(2,1)} %proj_parts.1), calls=%async_computation.2 | async-start | bytes 4718592 | tf_op jit(solution)/shard_map/all_to_all | solution.py:558
  210.1 0.9 collective-permute-start.13
  211.1 0.4 collective-permute-start.15
  211.5 0.6 collective-permute-done.13.rest_5_
  212.1 0.4 collective-permute-done.14.rest_6_
  212.5 0.6 collective-permute-done.15.rest_7_
  213.2 0.6 copy-done.23
  213.8 6.7 %input_blocks.1 = (bf16[128,1152]{1,0:T(8,128)(2,1)}, bf16[128,1152]{1,0:T(8,128)(2,1)}, bf16[128,1152]{1,0:T(8,128)(2,1)}, bf16[128,1152]{1,0:T(8,128)(2,1)}, b...) custom-call(s32[1]{0:T(128)} %bitcast.39.here_ref, ...), custom_call_target="tpu_custom_call" | custom-call | flops 2415919104 | bytes 7340032 | tf_op jit(solution)/shard_map/input_blocks/pallas_call | solution.py:361
  220.5 0.6 collective-permute-start.16
  221.0 1.6 collective-permute-start.17
  222.6 2.0 collective-permute-start.18
  224.6 1.2 collective-permute-start.19
  225.8 3.2 %collective-permute-done.16.rest_1_ = bf16[128,1152]{1,0:T(8,128)(2,1)S(1)} collective-permute-done((bf16[128,1152]{1,0:T(8,128)(2,1)}, bf16[128,1152]{1,0:T(8,128)(2,1)S(1)}, u32[]{:S(2)}, u32[]{:S(2)}) %collective-permute-start.16) | collective-permute-done | bytes 294944 | tf_op jit(solution)/shard_map/ppermute | solution.py:563
  229.0 11.4 %collective-permute-start.21 = (bf16[128,1152]{1,0:T(8,128)(2,1)}, bf16[128,1152]{1,0:T(8,128)(2,1)}, u32[]{:S(2)}, u32[]{:S(2)}) collective-permute-start(bf16[128,1152]{1,0:T(8,128)(2,1)} %get-tuple-element.84), channel_id=1, source_target_pairs={{0,6},{1,7},{2,4},{3,5},{4,2},{5,3},{6,0},{7,1},{8,14},{9,15},{10,... | collective-permute-start | bytes 884744 | tf_op jit(solution)/shard_map/ppermute | solution.py:563
  240.4 0.6 pad_add_fusion.1.where_ref
  241.0 1.2 collective-permute-done.20.rest_5_
  242.1 7.0 %collective-permute-done.21.rest_6_ = bf16[128,1152]{1,0:T(8,128)(2,1)} collective-permute-done((bf16[128,1152]{1,0:T(8,128)(2,1)}, bf16[128,1152]{1,0:T(8,128)(2,1)}, u32[]{:S(2)}, u32[]{:S(2)}) %collective-permute-start.21) | collective-permute-done | bytes 294944 | tf_op jit(solution)/shard_map/ppermute | solution.py:563
  249.1 1.3 collective-permute-done.22.rest_7_
  250.4 3.2 %place_columns.1 = bf16[128,9216]{1,0:T(8,128)(2,1)} custom-call(s32[2]{0:T(128)} %pad_add_fusion.1.where_ref, bf16[128,1152]{1,0:T(8,128)(2,1)} %get-tuple-element.78.rest_0_, bf16[128,1152]{1,0:T(8,128)(2,1)} %copy-done.8, bf16[128,1152]{1,0:T(8,128)(2,1)} %copy-done.9, bf16[128,1152]{1,0:T(8,128)(2,1)} %copy-done.10, bf16[128,1152]{1,0:T(8,128)(2,1)} %copy-done.11, ...), custom_call_target="tpu_custom_call" | custom-call | tf_op jit(solution)/shard_map/place_columns/pallas_call | solution.py:450
  253.6 0.3 reduce_sum.45
  253.9 0.7 fusion
  (76 shorter events, 1.0 us)
Async XLA Ops:
  7.2 4.0 %copy-start = (bf16[1,512,768]{2,1,0:T(8,128)(2,1)S(1)}, bf16[1,512,768]{2,1,0:T(8,128)(2,1)}, u32[]{:S(2)}) copy-start(bf16[1,512,768]{2,1,0:T(8,128)(2,1)} %param.10) | copy-start | bytes 2359300
  7.2 71.4 %all-gather.4.cloned.1.call-start = ((), (), s32[]{:S(2)}) async-start(), calls=%async_computation.3 | async-start | bytes 2228224 | tf_op jit(solution)/shard_map/all_gather | solution.py:499
  11.2 3.8 %collective-permute-start = (bf16[512,384]{1,0:T(8,128)(2,1)S(1)}, bf16[512,384]{1,0:T(8,128)(2,1)S(1)}, u32[]{:S(2)}, u32[]{:S(2)}) collective-permute-start(bf16[512,384]{1,0:T(8,128)(2,1)S(1)} %constant_dynamic-slice_fusion.2), channel_id=1, source_target_pairs={{0,4},{4,0},{8,12},{12,8},{16,20},{20,16},{24,28},{28,24},{32,36},... | collective-permute-start | bytes 1179656 | tf_op jit(solution)/shard_map/ppermute | solution.py:497
  15.0 0.8 copy-start.7
  15.7 1.3 copy-start.1
  15.7 1.8 copy-start.2
  16.9 14.6 %collective-permute-start.2 = (bf16[4608,128]{1,0:T(8,128)(2,1)}, bf16[4608,128]{1,0:T(8,128)(2,1)S(1)}, u32[]{:S(2)}, u32[]{:S(2)}) collective-permute-start(bf16[4608,128]{1,0:T(8,128)(2,1)} %bitcast.25), channel_id=1, source_target_pairs={{0,4},{4,0},{8,12},{12,8},{16,20},{20,16},{24,28},{28,24},{32,36},... | collective-permute-start | bytes 3538952 | tf_op jit(solution)/shard_map/ppermute | solution.py:522
  18.6 7.6 %collective-permute-start.1 = (bf16[2,512,384]{2,1,0:T(8,128)(2,1)}, bf16[2,512,384]{2,1,0:T(8,128)(2,1)}, u32[]{:S(2)}, u32[]{:S(2)}) collective-permute-start(bf16[2,512,384]{2,1,0:T(8,128)(2,1)} %pad_maximum_fusion.1), channel_id=1, source_target_pairs={{0,4},{4,0},{8,12},{12,8},{16,20},{20,16},{24,28},{28,24},{32,36},... | collective-permute-start | bytes 2359304 | tf_op jit(solution)/shard_map/ppermute | solution.py:503
  18.6 26.5 %all-to-all-start = ((bf16[8,128,512]{2,1,0:T(8,128)(2,1)}), bf16[8,128,512]{2,1,0:T(8,128)(2,1)S(1)}, u32[]{:S(2)}, u32[]{:S(2)}) async-start(bf16[8,128,512]{2,1,0:T(8,128)(2,1)} %bitcast.13), calls=%async_computation | async-start | bytes 2097152 | tf_op jit(solution)/shard_map/all_to_all | solution.py:494
  26.1 162.7 %all-gather.6.cloned.1.call-start = ((), (), s32[]{:S(2)}) async-start(), calls=%async_computation.4 | async-start | bytes 11796480 | tf_op jit(solution)/shard_map/all_gather | solution.py:532
  33.2 12.1 %copy-start.14 = (s32[32]{0:T(128)S(1)}, s32[32]{0:T(128)}, u32[]{:S(2)}) copy-start(s32[32]{0:T(128)} %param.17) | copy-start | bytes 388
  33.2 13.9 %copy-start.5 = (bf16[9216,128]{1,0:T(8,128)(2,1)S(1)}, bf16[9216,128]{1,0:T(8,128)(2,1)}, u32[]{:S(2)}) copy-start(bf16[9216,128]{1,0:T(8,128)(2,1)} %param.16) | copy-start | bytes 7077892
  45.1 3.4 %copy-start.4 = (bf16[8,128,512]{2,1,0:T(8,128)(2,1)}, bf16[8,128,512]{2,1,0:T(8,128)(2,1)S(1)}, u32[]{:S(2)}) copy-start(bf16[8,128,512]{2,1,0:T(8,128)(2,1)S(1)} %all-to-all-done) | copy-start | bytes 3145732
  46.6 6.0 %collective-permute-start.3 = (bf16[1024,512]{1,0:T(8,128)(2,1)S(1)}, bf16[1024,512]{1,0:T(8,128)(2,1)S(1)}, u32[]{:S(2)}, u32[]{:S(2)}) collective-permute-start(bf16[1024,512]{1,0:T(8,128)(2,1)S(1)} %bitcast.73), channel_id=1, source_target_pairs={{0,4},{4,0},{8,12},{12,8},{16,20},{20,16},{24,28},{28,24},{32,36},... | collective-permute-start | bytes 3145736 | tf_op jit(solution)/shard_map/ppermute | solution.py:533
  48.6 27.7 %collective-permute-start.4 = (bf16[2,1152,128]{2,1,0:T(8,128)(2,1)S(1)}, bf16[2,1152,128]{2,1,0:T(8,128)(2,1)S(1)}, u32[]{:S(2)}, u32[]{:S(2)}) collective-permute-start(bf16[2,1152,128]{2,1,0:T(8,128)(2,1)S(1)} %pad_maximum_fusion.3), channel_id=1, source_target_pairs={{0,3},{1,0},{2,1},{3,2},{4,7},{5,4},{6,5},{7,6},{8,11},{9,8},{10,9... | collective-permute-start | bytes 1769480 | tf_op jit(solution)/shard_map/ppermute | solution.py:529
  49.0 27.3 %collective-permute-start.5 = (bf16[2,1152,128]{2,1,0:T(8,128)(2,1)S(1)}, bf16[2,1152,128]{2,1,0:T(8,128)(2,1)}, u32[]{:S(2)}, u32[]{:S(2)}) collective-permute-start(bf16[2,1152,128]{2,1,0:T(8,128)(2,1)S(1)} %pad_maximum_fusion.4), channel_id=1, source_target_pairs={{0,2},{1,3},{2,0},{3,1},{4,6},{5,7},{6,4},{7,5},{8,10},{9,11},{10,... | collective-permute-start | bytes 1769480 | tf_op jit(solution)/shard_map/ppermute | solution.py:529
  51.5 27.0 %collective-permute-start.6 = (bf16[2,1152,128]{2,1,0:T(8,128)(2,1)S(1)}, bf16[2,1152,128]{2,1,0:T(8,128)(2,1)}, u32[]{:S(2)}, u32[]{:S(2)}) collective-permute-start(bf16[2,1152,128]{2,1,0:T(8,128)(2,1)S(1)} %pad_maximum_fusion.5), channel_id=1, source_target_pairs={{0,1},{1,2},{2,3},{3,0},{4,5},{5,6},{6,7},{7,4},{8,9},{9,10},{10,1... | collective-permute-start | bytes 1769480 | tf_op jit(solution)/shard_map/ppermute | solution.py:529
  52.7 1.0 copy-start.15
  76.3 47.8 %copy-start.16 = (bf16[2,1152,128]{2,1,0:T(8,128)(2,1)}, bf16[2,1152,128]{2,1,0:T(8,128)(2,1)S(1)}, u32[]{:S(2)}) copy-start(bf16[2,1152,128]{2,1,0:T(8,128)(2,1)S(1)} %collective-permute-done.4.rest_9_) | copy-start | bytes 1769476
  124.1 4.5 %collective-permute-start.7 = (bf16[8,256,512]{2,1,0:T(8,128)(2,1)}, bf16[8,256,512]{2,1,0:T(8,128)(2,1)S(1)}, u32[]{:S(2)}, u32[]{:S(2)}) collective-permute-start(bf16[8,256,512]{2,1,0:T(8,128)(2,1)} %get-tuple-element.63), channel_id=1, source_target_pairs={{0,4},{4,0},{8,12},{12,8},{16,20},{20,16},{24,28},{28,24},{32,36},... | collective-permute-start | bytes 6291464 | tf_op jit(solution)/shard_map/ppermute | solution.py:541
  132.1 23.3 %copy-start.17 = (bf16[512,384]{1,0:T(8,128)(2,1)S(1)}, bf16[512,384]{1,0:T(8,128)(2,1)}, u32[]{:S(2)}) copy-start(bf16[512,384]{1,0:T(8,128)(2,1)} %get-tuple-element.65) | copy-start | bytes 1179652
  132.1 25.4 %copy-start.6 = (bf16[512,384]{1,0:T(8,128)(2,1)S(1)}, bf16[512,384]{1,0:T(8,128)(2,1)}, u32[]{:S(2)}) copy-start(bf16[512,384]{1,0:T(8,128)(2,1)} %get-tuple-element.64) | copy-start | bytes 1179652
  132.1 51.9 %all-to-all-start.1 = ((bf16[8,256,512]{2,1,0:T(8,128)(2,1)}), bf16[8,256,512]{2,1,0:T(8,128)(2,1)S(1)}, u32[]{:S(2)}, u32[]{:S(2)}) async-start(bf16[8,256,512]{2,1,0:T(8,128)(2,1)} %add_convert_fusion), calls=%async_computation.1 | async-start | bytes 4194304 | tf_op jit(solution)/shard_map/all_to_all | solution.py:542
  155.4 2.1 collective-permute-start.8
  184.6 4.2 %copy-start.3 = (bf16[256,512]{0,1:T(8,128)(2,1)}, bf16[256,512]{0,1:T(8,128)(2,1)S(1)}, u32[]{:S(2)}) copy-start(bf16[256,512]{0,1:T(8,128)(2,1)S(1)} %copy.27) | copy-start | bytes 786436
  184.6 4.2 %collective-permute-start.9 = (bf16[512,256]{1,0:T(8,128)(2,1)S(1)}, bf16[512,256]{1,0:T(8,128)(2,1)S(1)}, u32[]{:S(2)}, u32[]{:S(2)}) collective-permute-start(bf16[512,256]{1,0:T(8,128)(2,1)S(1)} %bitcast.67), channel_id=1, source_target_pairs={{0,4},{4,0},{8,12},{12,8},{16,20},{20,16},{24,28},{28,24},{32,36},... | collective-permute-start | bytes 786440 | tf_op jit(solution)/shard_map/ppermute | solution.py:554
  185.4 12.2 %collective-permute-start.10 = (bf16[512,256]{1,0:T(8,128)(2,1)S(1)}, bf16[512,256]{1,0:T(8,128)(2,1)S(1)}, u32[]{:S(2)}, u32[]{:S(2)}) collective-permute-start(bf16[512,256]{1,0:T(8,128)(2,1)S(1)} %bitcast.68), channel_id=1, source_target_pairs={{0,3},{1,0},{2,1},{3,2},{4,7},{5,4},{6,5},{7,6},{8,11},{9,8},{10,9... | collective-permute-start | bytes 786440 | tf_op jit(solution)/shard_map/ppermute | solution.py:553
  186.8 10.8 %collective-permute-start.11 = (bf16[512,256]{1,0:T(8,128)(2,1)S(1)}, bf16[512,256]{1,0:T(8,128)(2,1)S(1)}, u32[]{:S(2)}, u32[]{:S(2)}) collective-permute-start(bf16[512,256]{1,0:T(8,128)(2,1)S(1)} %bitcast.69), channel_id=1, source_target_pairs={{0,2},{1,3},{2,0},{3,1},{4,6},{5,7},{6,4},{7,5},{8,10},{9,11},{10,... | collective-permute-start | bytes 786440 | tf_op jit(solution)/shard_map/ppermute | solution.py:553
  188.8 13.4 %collective-permute-start.12 = (bf16[512,256]{1,0:T(8,128)(2,1)S(1)}, bf16[512,256]{1,0:T(8,128)(2,1)S(1)}, u32[]{:S(2)}, u32[]{:S(2)}) collective-permute-start(bf16[512,256]{1,0:T(8,128)(2,1)S(1)} %bitcast.70), channel_id=1, source_target_pairs={{0,1},{1,2},{2,3},{3,0},{4,5},{5,6},{6,7},{7,4},{8,9},{9,10},{10,1... | collective-permute-start | bytes 786440 | tf_op jit(solution)/shard_map/ppermute | solution.py:553
  188.8 0.7 copy-start.13
  197.7 12.4 %copy-start.18 = (bf16[512,256]{1,0:T(8,128)(2,1)}, bf16[512,256]{1,0:T(8,128)(2,1)S(1)}, u32[]{:S(2)}) copy-start(bf16[512,256]{1,0:T(8,128)(2,1)S(1)} %collective-permute-done.10.rest_1_) | copy-start | bytes 786436
  197.7 13.3 %copy-start.19 = (bf16[512,256]{1,0:T(8,128)(2,1)}, bf16[512,256]{1,0:T(8,128)(2,1)S(1)}, u32[]{:S(2)}) copy-start(bf16[512,256]{1,0:T(8,128)(2,1)S(1)} %collective-permute-done.11.rest_2_) | copy-start | bytes 786436
  202.2 0.7 copy-start.20
  202.9 50.7 %all-to-all-start.2 = ((bf16[16,288,256]{2,1,0:T(8,128)(2,1)}), bf16[16,288,256]{2,1,0:T(8,128)(2,1)S(1)}, u32[]{:S(2)}, u32[]{:S(2)}) async-start(bf16[16,288,256]{2,1,0:T(8,128)(2,1)} %proj_parts.1), calls=%async_computation.2 | async-start | bytes 4718592 | tf_op jit(solution)/shard_map/all_to_all | solution.py:558
  210.1 2.0 collective-permute-start.13
  211.0 1.5 collective-permute-start.14
  211.1 2.0 collective-permute-start.15
  212.1 1.0 copy-start.21
  212.5 0.7 copy-start.22
  213.1 0.7 copy-start.23
  220.5 8.5 %collective-permute-start.16 = (bf16[128,1152]{1,0:T(8,128)(2,1)}, bf16[128,1152]{1,0:T(8,128)(2,1)S(1)}, u32[]{:S(2)}, u32[]{:S(2)}) collective-permute-start(bf16[128,1152]{1,0:T(8,128)(2,1)} %get-tuple-element.79), channel_id=1, source_target_pairs={{0,1},{1,2},{2,3},{3,0},{4,5},{5,6},{6,7},{7,4},{8,9},{9,10},{10,1... | collective-permute-start | bytes 884744 | tf_op jit(solution)/shard_map/ppermute | solution.py:563
  221.0 19.3 %collective-permute-start.17 = (bf16[128,1152]{1,0:T(8,128)(2,1)}, bf16[128,1152]{1,0:T(8,128)(2,1)S(1)}, u32[]{:S(2)}, u32[]{:S(2)}) collective-permute-start(bf16[128,1152]{1,0:T(8,128)(2,1)} %get-tuple-element.80), channel_id=1, source_target_pairs={{0,2},{1,3},{2,0},{3,1},{4,6},{5,7},{6,4},{7,5},{8,10},{9,11},{10,... | collective-permute-start | bytes 884744 | tf_op jit(solution)/shard_map/ppermute | solution.py:563
  222.6 18.4 %collective-permute-start.18 = (bf16[128,1152]{1,0:T(8,128)(2,1)}, bf16[128,1152]{1,0:T(8,128)(2,1)S(1)}, u32[]{:S(2)}, u32[]{:S(2)}) collective-permute-start(bf16[128,1152]{1,0:T(8,128)(2,1)} %get-tuple-element.81), channel_id=1, source_target_pairs={{0,3},{1,0},{2,1},{3,2},{4,7},{5,4},{6,5},{7,6},{8,11},{9,8},{10,9... | collective-permute-start | bytes 884744 | tf_op jit(solution)/shard_map/ppermute | solution.py:563
  224.6 16.4 %collective-permute-start.19 = (bf16[128,1152]{1,0:T(8,128)(2,1)}, bf16[128,1152]{1,0:T(8,128)(2,1)S(1)}, u32[]{:S(2)}, u32[]{:S(2)}) collective-permute-start(bf16[128,1152]{1,0:T(8,128)(2,1)} %get-tuple-element.82), channel_id=1, source_target_pairs={{0,4},{1,5},{2,6},{3,7},{4,0},{5,1},{6,2},{7,3},{8,12},{9,13},{10,... | collective-permute-start | bytes 884744 | tf_op jit(solution)/shard_map/ppermute | solution.py:563
  225.8 16.4 %collective-permute-start.20 = (bf16[128,1152]{1,0:T(8,128)(2,1)}, bf16[128,1152]{1,0:T(8,128)(2,1)S(1)}, u32[]{:S(2)}, u32[]{:S(2)}) collective-permute-start(bf16[128,1152]{1,0:T(8,128)(2,1)} %get-tuple-element.83), channel_id=1, source_target_pairs={{0,5},{1,6},{2,7},{3,4},{4,1},{5,2},{6,3},{7,0},{8,13},{9,14},{10,... | collective-permute-start | bytes 884744 | tf_op jit(solution)/shard_map/ppermute | solution.py:563
  229.0 21.4 %copy-start.8 = (bf16[128,1152]{1,0:T(8,128)(2,1)}, bf16[128,1152]{1,0:T(8,128)(2,1)S(1)}, u32[]{:S(2)}) copy-start(bf16[128,1152]{1,0:T(8,128)(2,1)S(1)} %collective-permute-done.16.rest_1_) | copy-start | bytes 884740
  229.0 20.1 %collective-permute-start.21 = (bf16[128,1152]{1,0:T(8,128)(2,1)}, bf16[128,1152]{1,0:T(8,128)(2,1)}, u32[]{:S(2)}, u32[]{:S(2)}) collective-permute-start(bf16[128,1152]{1,0:T(8,128)(2,1)} %get-tuple-element.84), channel_id=1, source_target_pairs={{0,6},{1,7},{2,4},{3,5},{4,2},{5,3},{6,0},{7,1},{8,14},{9,15},{10,... | collective-permute-start | bytes 884744 | tf_op jit(solution)/shard_map/ppermute | solution.py:563
  240.3 10.0 %copy-start.9 = (bf16[128,1152]{1,0:T(8,128)(2,1)}, bf16[128,1152]{1,0:T(8,128)(2,1)S(1)}, u32[]{:S(2)}) copy-start(bf16[128,1152]{1,0:T(8,128)(2,1)S(1)} %collective-permute-done.17.rest_2_) | copy-start | bytes 884740
  240.3 10.0 %collective-permute-start.22 = (bf16[128,1152]{1,0:T(8,128)(2,1)}, bf16[128,1152]{1,0:T(8,128)(2,1)}, u32[]{:S(2)}, u32[]{:S(2)}) collective-permute-start(bf16[128,1152]{1,0:T(8,128)(2,1)} %get-tuple-element.85), channel_id=1, source_target_pairs={{0,7},{1,4},{2,5},{3,6},{4,3},{5,0},{6,1},{7,2},{8,15},{9,12},{10,... | collective-permute-start | bytes 884744 | tf_op jit(solution)/shard_map/ppermute | solution.py:563
  241.0 9.4 %copy-start.10 = (bf16[128,1152]{1,0:T(8,128)(2,1)}, bf16[128,1152]{1,0:T(8,128)(2,1)S(1)}, u32[]{:S(2)}) copy-start(bf16[128,1152]{1,0:T(8,128)(2,1)S(1)} %collective-permute-done.18.rest_3_) | copy-start | bytes 884740
  241.0 9.4 %copy-start.11 = (bf16[128,1152]{1,0:T(8,128)(2,1)}, bf16[128,1152]{1,0:T(8,128)(2,1)S(1)}, u32[]{:S(2)}) copy-start(bf16[128,1152]{1,0:T(8,128)(2,1)S(1)} %collective-permute-done.19.rest_4_) | copy-start | bytes 884740
  242.1 8.3 %copy-start.12 = (bf16[128,1152]{1,0:T(8,128)(2,1)}, bf16[128,1152]{1,0:T(8,128)(2,1)S(1)}, u32[]{:S(2)}) copy-start(bf16[128,1152]{1,0:T(8,128)(2,1)S(1)} %collective-permute-done.20.rest_5_) | copy-start | bytes 884740
Sparse Core Ops, SparseCore 0:
  11.2 58.7 all-gather.3
  72.2 89.9 all-gather.5
